TPU v7x, 32 devices: a whole 2x2x4 slice. The times are simulated.
32 devices in a mesh: row: 8 (over z, y), col: 4 (over x, core).
Axes of the slice: x: 2, y: 2, z: 4, core: 2. Of those that a mesh axis runs over, the one named last changes fastest.
Arguments:
- load_currents: float32 [16, 64, 64, 128], P(None, 'row', 'col'), may hold values from -24 to 24
- block_library: float32 [8, 128, 128], replicated, may hold values from -4.0625 to 24.1, as said below
- strap_conductance: float32 [2, 128], replicated, may hold values from 0.5 to 4
- block_types: int32 [64, 64], P('row', 'col'), may hold values from 0 to 7
- aggregate_map: int32 [64, 64], P('row', 'col'), may hold values from 0 to 63, as said below
Outputs:
- node_voltage: float32 [16, 64, 64, 128], P(None, 'row', 'col')
- residual: float32 [16, 64, 64, 128], P(None, 'row', 'col')
Inputs may be any that keep to these rules, and one draw needn't show every extreme that they name: `aggregate_map`: each aggregate id names an aggregate of one column group of 16 block columns; the same id in another column group is another aggregate. Every aggregate of every column group holds at least one block. `block_library`: each library block is symmetric positive definite, with nonpositive off-diagonal entries and positive row sums.
All inputs are finite; a program needn't handle non-finite values.
Results may differ from a plain program's by a relative error of at most 0.0003.
Values sent between devices are 32-bit elements; how exact they have to be, the bound alone decides.
No kernel may reach another device: no remote copies, remote signals or barrier semaphores. Data moves between devices by JAX's collectives and lax.ppermute only.
A program may use at most 64 MiB of HBM per device.

v0:
```python
import jax
import jax.numpy as jnp
from jax import lax
from jax.sharding import PartitionSpec as P

SWEEPS = 3
ITERS = 2
AGR = 4
AGC = 4


def padded_2(array, sides, width):
    for axis, dim in sides:
        size, length = (lax.axis_size(axis), array.shape[dim])
        up = [(i, (i + 1) % size) for i in range(size - 1)]
        down = [(j, i) for i, j in up]
        last = lax.slice_in_dim(array, length - width, length, axis=dim)
        first = lax.slice_in_dim(array, 0, width, axis=dim)
        before = lax.ppermute(last, axis, up)
        after = lax.ppermute(first, axis, down)
        array = jnp.concatenate([before, array, after], axis=dim)
    return array


def from_behind(array, axis, by):
    length = lax.axis_size(axis)
    pairs = [(i, i + by) for i in range(length) if 0 <= i + by < length]
    return lax.ppermute(array, axis, pairs)


def coarse_terms(group_ids, group_types, block_sums, north_weight, east_weight, count):
    centre = block_sums[group_types] + 2.0 * north_weight + 2.0 * east_weight
    flat = group_ids.reshape(-1)
    upper = group_ids[:-1].reshape(-1)
    lower = group_ids[1:].reshape(-1)
    left = group_ids[:, :-1].reshape(-1)
    right = group_ids[:, 1:].reshape(-1)
    index = jnp.concatenate(
        [
            flat * count + flat,
            upper * count + lower,
            lower * count + upper,
            left * count + right,
            right * count + left,
        ]
    )
    values = jnp.concatenate(
        [
            centre.reshape(-1),
            -north_weight * jnp.ones((2 * upper.shape[0],), jnp.float32),
            -east_weight * jnp.ones((2 * left.shape[0],), jnp.float32),
        ]
    )
    return jax.ops.segment_sum(values, index, num_segments=count * count).reshape(count, count)


def alignment_sum(residual, zeta):
    return lax.psum(jnp.sum(residual * zeta, axis=(1, 2, 3)), ("row", "col"))


def on_device(load_currents, block_library, strap_conductance, block_types, aggregate_map):
    sizings, rows_local, cols_local, nodes = load_currents.shape
    blocks = rows_local * cols_local
    count = rows_local * lax.axis_size("row") // AGR * (cols_local // AGC)
    picked = block_library[block_types.reshape(-1)]
    couple = 2.0 * strap_conductance[0] + 2.0 * strap_conductance[1]
    diag_library = jnp.diagonal(block_library, axis1=1, axis2=2)
    diagonal = diag_library[block_types] + couple
    block_sums = jnp.sum(block_library, axis=(1, 2))
    north_weight = jnp.sum(strap_conductance[0])
    east_weight = jnp.sum(strap_conductance[1])

    def block_products(field):
        flat = field.reshape(sizings, blocks, nodes)
        product = jnp.einsum("bij,sbj->sbi", picked, flat, precision=lax.Precision.HIGHEST)
        return product.reshape(sizings, rows_local, cols_local, nodes)

    local_matrix = coarse_terms(
        aggregate_map, block_types, block_sums, north_weight, east_weight, count
    )
    below_ids = from_behind(aggregate_map[0], "row", -1)
    present = (lax.axis_index("row") < lax.axis_size("row") - 1).astype(jnp.float32)
    bottom_ids = aggregate_map[-1]
    cross_index = jnp.concatenate([bottom_ids * count + below_ids, below_ids * count + bottom_ids])
    cross_values = -north_weight * present * jnp.ones((2 * cols_local,), jnp.float32)
    cross_matrix = jax.ops.segment_sum(
        cross_values, cross_index, num_segments=count * count
    ).reshape(count, count)
    coarse_matrix = lax.psum(local_matrix + cross_matrix, "row")
    factor = jnp.linalg.cholesky(coarse_matrix)
    flat_ids = aggregate_map.reshape(-1)

    def smooth(residual):
        result = residual / diagonal
        for sweep in range(SWEEPS - 1):
            image = block_products(result) + couple * result
            result = result + (residual - image) / diagonal
        return result

    def coarse_part(residual):
        sums = residual.sum(-1).reshape(sizings, blocks).T
        local = jax.ops.segment_sum(sums, flat_ids, num_segments=count)
        gathered = lax.psum(local, "row")
        solved = jax.scipy.linalg.cho_solve((factor, True), gathered)
        return solved[flat_ids].T.reshape(sizings, rows_local, cols_local)[..., None]

    def precondition(residual):
        return smooth(residual) + coarse_part(residual)

    node_voltage = jnp.zeros_like(load_currents)
    residual = load_currents
    zeta = precondition(residual)
    direction = zeta
    aligned = alignment_sum(residual, zeta)
    for iteration in range(ITERS):
        padded = padded_2(direction, (("row", 1), ("col", 2)), 1)
        north = padded[:, :-2, 1:-1]
        south = padded[:, 2:, 1:-1]
        west = padded[:, 1:-1, :-2]
        east = padded[:, 1:-1, 2:]
        lateral = strap_conductance[0] * (2.0 * direction - north - south) + strap_conductance[
            1
        ] * (2.0 * direction - west - east)
        image = block_products(direction) + lateral
        curvature = lax.psum(jnp.sum(direction * image, axis=(1, 2, 3)), ("row", "col"))
        step_size = (aligned / curvature)[:, None, None, None]
        node_voltage = node_voltage + step_size * direction
        residual = residual - step_size * image
        if iteration + 1 < ITERS:
            zeta = precondition(residual)
            fresh = alignment_sum(residual, zeta)
            blend = (fresh / aligned)[:, None, None, None]
            direction = zeta + blend * direction
            aligned = fresh
    return (node_voltage, residual)


def solution(mesh):
    placed = (P(None, "row", "col", None), P(), P(), P("row", "col"), P("row", "col"))
    return jax.shard_map(
        on_device,
        mesh=mesh,
        in_specs=placed,
        out_specs=(P(None, "row", "col", None), P(None, "row", "col", None)),
        check_vma=False,
    )
```

profile of v0, /device:TPU:0, one launch (start us, length us, event | category | flops | bytes accessed | tf_op | source)
XLA Modules:
  0.0 387.7 jit_solution(2048250053962286289)
XLA Ops:
  0.7 0.8 slice_bitcast_fusion
  1.5 1.3 collective-permute-start
  2.7 1.4 slice_reduce_fusion.1
  6.7 0.8 fusion.39
  7.5 0.8 fusion.40
  9.1 0.8 broadcast_in_dim_reshape.2
  12.2 5.9 %copy.47 = f32[8,128,128]{0,2,1:T(8,128)} copy(f32[8,128,128]{2,1,0:T(8,128)} %param.8) | data formatting | bytes 1048576 | tf_op args[1]
  19.1 1.8 gather_fusion
  20.9 1.2 gather_fusion.3
  22.8 1.6 copy_divide_fusion
  24.4 4.3 %gather_fusion.2 = f32[128,128,128]{2,1,0:T(8,128)} fusion(f32[8,128,128]{2,1,0:T(8,128)S(1)} %copy-done.1, s32[1024]{0:T(1024)S(1)} %pad_clamp_fusion.1), kind=kCustom, calls=%fused_computation.2 | custom fusion | bytes 16777728 | tf_op jit(solution)/shard_map/gather | solution.py:65
  28.8 16.6 %fusion.41 = f32[128,16,128]{2,1,0:T(8,128)S(1)} fusion(f32[16,128,128]{2,0,1:T(8,128)} %bitcast.108, f32[128,128,128]{2,1,0:T(8,128)} %gather_fusion.2), kind=kOutput, calls=%fused_computation.117 | convolution fusion | flops 402653184 | bytes 10485760 | tf_op jit(solution)/shard_map/bij,sbj->sbi/dot_general | solution.py:75
  46.1 14.2 %fusion.42 = f32[128,16,128]{2,1,0:T(8,128)} fusion(f32[16,128,128]{2,0,1:T(8,128)S(1)} %bitcast.109, f32[128,128,128]{2,1,0:T(8,128)S(1)} %copy-done), kind=kOutput, calls=%fused_computation.118 | convolution fusion | flops 402653184 | bytes 10485760 | tf_op jit(solution)/shard_map/bij,sbj->sbi/dot_general | solution.py:75
  60.4 1.2 scatter_custom_fusion.1
  62.4 4.8 %scatter_custom_fusion = f32[4096]{0:T(1024)S(1)} fusion(s32[624]{0:T(1024)S(1)} %add_reduce_fusion, f32[624]{0:T(1024)S(1)} %select_maximum_fusion, f32[]{:T(128)} %constant.70.clone.1), kind=kCustom, calls=%fused_computation.82 | custom fusion | flops 624 | bytes 16388 | tf_op jit(solution)/shard_map/add | solution.py:89
  67.4 40.9 %all-reduce.2 = (f32[64,16]{1,0:T(8,128)S(1)}, f32[64,64]{0,1:T(8,128)S(1)}) all-reduce(f32[64,16]{1,0:T(8,128)S(1)} %scatter_custom_fusion.1, f32[64,64]{0,1:T(8,128)S(1)} %copy.52), channel_id=1, replica_groups=mesh['row'=8,'col'=4] {'row'}, use_global_device_ids=true, to_apply=%region_9.10 | all-reduce | flops 5120 | bytes 40960 | tf_op jit(solution)/shard_map/psum | solution.py:103
  108.3 5.8 %cholesky.18 = f32[64,64]{1,0:T(8,128)S(1)} custom-call(f32[64,64]{1,0:T(8,128)S(1)} %fusion.25), custom_call_target="Cholesky" | custom-call | tf_op jit(solution)/shard_map/jit(cholesky)/cholesky | solution.py:90
  115.5 4.9 %custom-call.11 = f32[1,64,64]{1,2,0:T(8,128)S(1)} custom-call(f32[1,64,64]{2,1,0:T(8,128)S(1)} %fusion.16), custom_call_target="InvertDiagBlocksLowerTriangular" | custom-call | tf_op jit(solution)/shard_map/jit(_cho_solve)/triangular_solve | solution.py:104
  121.5 2.0 add_add_fusion.1
  123.5 1.3 collective-permute-start.1
  124.8 1.3 collective-permute-start.2
  126.1 1.2 collective-permute-done.1
  127.3 4.4 %collective-permute-done.2 = f32[16,1,16,128]{3,0,2,1:T(8,128)S(1)} collective-permute-done((f32[16,1,16,128]{3,0,2,1:T(8,128)S(1)}, f32[16,1,16,128]{3,0,2,1:T(8,128)S(1)}, u32[]{:S(2)}, u32[]{:S(2)}) %collective-permute-start.2) | collective-permute-done | bytes 131104 | tf_op jit(solution)/shard_map/ppermute | solution.py:20
  131.7 1.3 collective-permute-start.3
  133.0 1.3 collective-permute-start.4
  134.3 15.4 %fusion.43 = f32[128,16,128]{2,1,0:T(8,128)S(1)} fusion(f32[16,128,128]{2,0,1:T(8,128)S(1)} %bitcast.99, f32[128,128,128]{2,1,0:T(8,128)} %gather_fusion.2), kind=kOutput, calls=%fused_computation.119 | convolution fusion | flops 402653184 | bytes 10485760 | tf_op jit(solution)/shard_map/bij,sbj->sbi/dot_general | solution.py:75
  149.7 1.8 multiply_reduce_fusion.2
  151.5 43.5 %all-reduce.1 = (f32[16]{0:T(128)S(1)}, f32[16]{0:T(128)S(1)}) all-reduce(f32[16]{0:T(128)S(1)} %get-tuple-element.6, f32[16]{0:T(128)S(1)} %get-tuple-element.5), channel_id=1, replica_groups=mesh['row'=8,'col'=4] {'row','col'}, use_global_device_ids=true, to_apply=%region_11.13 | all-reduce | flops 32 | bytes 256 | tf_op jit(solution)/shard_map/psum | solution.py:58
  195.0 2.1 broadcast_divide_fusion
  197.1 16.5 %divide_add_fusion = (f32[16,8,16,128]{3,0,2,1:T(8,128)S(1)}, f32[16,8,16]{0,2,1:T(8,128)S(1)}, f32[128,16,128]{2,1,0:T(8,128)}) fusion(f32[16,8,16,128]{3,0,2,1:T(8,128)S(1)} %get-tuple-element.16, f32[128]{0:T(128)S(1)} %add_multiply_fusion, f32[8,16,128]{2,1,0:T(8,128)S(1)} %broadcast_add_fusion, f32[16,128,128]{2,0,1:T(8,128)S(1)} %bitcast.106, ...), kind=kOutput, calls=%fused_computation.47 | convolution fusion | flops 404486144 | bytes 12657152 | tf_op jit(solution)/shard_map/bij,sbj->sbi/dot_general | solution.py:75
  213.7 14.0 %fusion.44 = f32[128,16,128]{2,1,0:T(8,128)} fusion(f32[16,128,128]{2,0,1:T(8,128)S(1)} %bitcast.107, f32[128,128,128]{2,1,0:T(8,128)S(1)} %bitcast.98), kind=kOutput, calls=%fused_computation.120 | convolution fusion | flops 402653184 | bytes 10485760 | tf_op jit(solution)/shard_map/bij,sbj->sbi/dot_general | solution.py:75
  227.7 1.2 scatter_custom_fusion.2
  228.9 36.9 %psum.53 = f32[64,16]{1,0:T(8,128)S(1)} all-reduce(f32[64,16]{1,0:T(8,128)S(1)} %scatter_custom_fusion.2), channel_id=1, replica_groups=mesh['row'=8,'col'=4] {'row'}, use_global_device_ids=true, to_apply=%region_16.18 | all-reduce | flops 1024 | bytes 8192 | tf_op jit(solution)/shard_map/psum | solution.py:103
  266.8 2.2 multiply_reduce_fusion.1
  269.0 36.9 %psum.54 = f32[16]{0:T(128)S(1)} all-reduce(f32[16]{0:T(128)S(1)} %multiply_reduce_fusion.1), channel_id=1, replica_groups=mesh['row'=8,'col'=4] {'row','col'}, use_global_device_ids=true, to_apply=%region_18.20 | all-reduce | flops 16 | bytes 128 | tf_op jit(solution)/shard_map/psum | solution.py:58
  305.9 2.1 multiply_add_fusion.1
  308.0 4.2 %collective-permute-start.5 = (f32[16,1,16,128]{3,0,2,1:T(8,128)S(1)}, f32[16,1,16,128]{3,0,2,1:T(8,128)S(1)}, u32[]{:S(2)}, u32[]{:S(2)}) collective-permute-start(f32[16,1,16,128]{3,0,2,1:T(8,128)S(1)} %get-tuple-element.22), channel_id=1, source_target_pairs={{0,4},{4,8},{8,12},{12,16},{16,20},{20,24},{24,28},{1,5},{5,9},{9,... | collective-permute-start | bytes 393224 | tf_op jit(solution)/shard_map/ppermute | solution.py:19
  312.2 1.3 collective-permute-start.6
  313.5 1.2 collective-permute-done.5
  314.7 4.4 %collective-permute-done.6 = f32[16,1,16,128]{3,0,2,1:T(8,128)S(1)} collective-permute-done((f32[16,1,16,128]{3,0,2,1:T(8,128)S(1)}, f32[16,1,16,128]{3,0,2,1:T(8,128)S(1)}, u32[]{:S(2)}, u32[]{:S(2)}) %collective-permute-start.6) | collective-permute-done | bytes 131104 | tf_op jit(solution)/shard_map/ppermute | solution.py:20
  319.1 1.5 collective-permute-start.7
  320.6 1.3 collective-permute-start.8
  321.9 15.4 %fusion.45 = f32[128,16,128]{2,1,0:T(8,128)S(1)} fusion(f32[16,128,128]{2,0,1:T(8,128)S(1)} %bitcast.100, f32[128,128,128]{2,1,0:T(8,128)} %gather_fusion.2), kind=kOutput, calls=%fused_computation.121 | convolution fusion | flops 402653184 | bytes 10485760 | tf_op jit(solution)/shard_map/bij,sbj->sbi/dot_general | solution.py:75
  337.3 1.5 multiply_reduce_fusion
  338.8 44.5 %psum.55 = f32[16]{0:T(128)S(1)} all-reduce(f32[16]{0:T(128)S(1)} %get-tuple-element.13), channel_id=1, replica_groups=mesh['row'=8,'col'=4] {'row','col'}, use_global_device_ids=true, to_apply=%region_20.22 | all-reduce | flops 16 | bytes 128 | tf_op jit(solution)/shard_map/psum | solution.py:125
  383.3 1.6 multiply_subtract_fusion
  384.9 1.3 copy.61
  386.2 1.3 copy.62
  (70 shorter events, 10.2 us)
Async XLA Ops:
  0.6 17.4 %copy-start.1 = (f32[8,128,128]{2,1,0:T(8,128)S(1)}, f32[8,128,128]{2,1,0:T(8,128)}, u32[]{:S(2)}) copy-start(f32[8,128,128]{2,1,0:T(8,128)} %param.8) | copy-start | bytes 1572868
  0.6 18.0 %copy-start.2 = (f32[16,8,16,128]{3,2,1,0:T(8,128)S(1)}, f32[16,8,16,128]{3,2,1,0:T(8,128)}, u32[]{:S(2)}) copy-start(f32[16,8,16,128]{3,2,1,0:T(8,128)} %param.7) | copy-start | bytes 3145732
  1.5 60.1 %collective-permute-start = (s32[16]{0:T(128)S(1)}, s32[16]{0:T(128)S(1)}, u32[]{:S(2)}, u32[]{:S(2)}) collective-permute-start(s32[16]{0:T(128)S(1)} %slice_bitcast_fusion), channel_id=1, source_target_pairs={{4,0},{8,4},{12,8},{16,12},{20,16},{24,20},{28,24},{5,1},{9,5},{13... | collective-permute-start | bytes 200 | tf_op jit(solution)/shard_map/ppermute | solution.py:28
  28.8 17.3 %copy-start = (f32[128,128,128]{2,1,0:T(8,128)S(1)}, f32[128,128,128]{2,1,0:T(8,128)}, u32[]{:S(2)}) copy-start(f32[128,128,128]{2,1,0:T(8,128)} %gather_fusion.2) | copy-start | bytes 25165828
  123.5 3.8 collective-permute-start.1
  124.8 6.9 %collective-permute-start.2 = (f32[16,1,16,128]{3,0,2,1:T(8,128)S(1)}, f32[16,1,16,128]{3,0,2,1:T(8,128)S(1)}, u32[]{:S(2)}, u32[]{:S(2)}) collective-permute-start(f32[16,1,16,128]{3,0,2,1:T(8,128)S(1)} %get-tuple-element.27), channel_id=1, source_target_pairs={{4,0},{8,4},{12,8},{16,12},{20,16},{24,20},{28,24},{5,1},{9,5},{13... | collective-permute-start | bytes 393224 | tf_op jit(solution)/shard_map/ppermute | solution.py:20
  131.7 18.0 %collective-permute-start.3 = (f32[16,10,1,128]{3,0,2,1:T(8,128)S(1)}, f32[16,10,1,128]{3,0,2,1:T(8,128)S(1)}, u32[]{:S(2)}, u32[]{:S(2)}) collective-permute-start(f32[16,10,1,128]{3,0,2,1:T(8,128)S(1)} %get-tuple-element.20), channel_id=1, source_target_pairs={{0,1},{1,2},{2,3},{4,5},{5,6},{6,7},{8,9},{9,10},{10,11},{12,13},{... | collective-permute-start | bytes 245768 | tf_op jit(solution)/shard_map/ppermute | solution.py:19
  133.0 16.7 %collective-permute-start.4 = (f32[16,10,1,128]{3,0,2,1:T(8,128)S(1)}, f32[16,10,1,128]{3,0,2,1:T(8,128)S(1)}, u32[]{:S(2)}, u32[]{:S(2)}) collective-permute-start(f32[16,10,1,128]{3,0,2,1:T(8,128)S(1)} %get-tuple-element.21), channel_id=1, source_target_pairs={{1,0},{2,1},{3,2},{5,4},{6,5},{7,6},{9,8},{10,9},{11,10},{13,12},{... | collective-permute-start | bytes 245768 | tf_op jit(solution)/shard_map/ppermute | solution.py:20
  195.0 18.6 %slice-start = ((s8[8388608]{0:T(1024)(128)(4,1)}), s8[4194304]{0:T(1024)(128)(4,1)S(1)}, s32[]{:S(2)}) async-start(s8[8388608]{0:T(1024)(128)(4,1)} %bitcast.97), calls=%async_computation | async-start | bytes 8388608
  197.1 16.5 %slice-start.1 = ((s8[8388608]{0:T(1024)(128)(4,1)}), s8[4194304]{0:T(1024)(128)(4,1)S(1)}, s32[]{:S(2)}) async-start(s8[8388608]{0:T(1024)(128)(4,1)} %bitcast.97), calls=%async_computation.1 | async-start | bytes 8388608
  308.0 6.7 %collective-permute-start.5 = (f32[16,1,16,128]{3,0,2,1:T(8,128)S(1)}, f32[16,1,16,128]{3,0,2,1:T(8,128)S(1)}, u32[]{:S(2)}, u32[]{:S(2)}) collective-permute-start(f32[16,1,16,128]{3,0,2,1:T(8,128)S(1)} %get-tuple-element.22), channel_id=1, source_target_pairs={{0,4},{4,8},{8,12},{12,16},{16,20},{20,24},{24,28},{1,5},{5,9},{9,... | collective-permute-start | bytes 393224 | tf_op jit(solution)/shard_map/ppermute | solution.py:19
  312.2 6.9 %collective-permute-start.6 = (f32[16,1,16,128]{3,0,2,1:T(8,128)S(1)}, f32[16,1,16,128]{3,0,2,1:T(8,128)S(1)}, u32[]{:S(2)}, u32[]{:S(2)}) collective-permute-start(f32[16,1,16,128]{3,0,2,1:T(8,128)S(1)} %get-tuple-element.23), channel_id=1, source_target_pairs={{4,0},{8,4},{12,8},{16,12},{20,16},{24,20},{28,24},{5,1},{9,5},{13... | collective-permute-start | bytes 393224 | tf_op jit(solution)/shard_map/ppermute | solution.py:20
  319.1 18.2 %collective-permute-start.7 = (f32[16,10,1,128]{3,0,2,1:T(8,128)S(1)}, f32[16,10,1,128]{3,0,2,1:T(8,128)S(1)}, u32[]{:S(2)}, u32[]{:S(2)}) collective-permute-start(f32[16,10,1,128]{3,0,2,1:T(8,128)S(1)} %get-tuple-element.18), channel_id=1, source_target_pairs={{0,1},{1,2},{2,3},{4,5},{5,6},{6,7},{8,9},{9,10},{10,11},{12,13},{... | collective-permute-start | bytes 245768 | tf_op jit(solution)/shard_map/ppermute | solution.py:19
  320.6 16.7 %collective-permute-start.8 = (f32[16,10,1,128]{3,0,2,1:T(8,128)S(1)}, f32[16,10,1,128]{3,0,2,1:T(8,128)S(1)}, u32[]{:S(2)}, u32[]{:S(2)}) collective-permute-start(f32[16,10,1,128]{3,0,2,1:T(8,128)S(1)} %get-tuple-element.19), channel_id=1, source_target_pairs={{1,0},{2,1},{3,2},{5,4},{6,5},{7,6},{9,8},{10,9},{11,10},{13,12},{... | collective-permute-start | bytes 245768 | tf_op jit(solution)/shard_map/ppermute | solution.py:20
where the time goes:
time: 395 us; the launch traced here: 388 us
  blocking collectives  203 us (51%)
  matrix products  92.9 us (24%)
  other arithmetic  39.1 us (10%)
  local copies, waits for them, and re-layouts  23.3 us (6%)
  starting transfers between devices  14.7 us (4%)
  waiting for transfers between devices  11.2 us (3%)
    dot_general x6, matrix products, block_products(): jnp.einsum('bij,sbj->sbi', picked, flat, precision=lax.Precision.HIGHEST)  92.1 us
    psum x2, blocking collectives, alignment_sum(): return lax.psum(jnp.sum(residual * zeta, axis=(1, 2, 3)), ('row', 'col'))  80.4 us
    psum x2, blocking collectives, coarse_part(): gathered = lax.psum(local, 'row')  77.7 us
    psum x1, blocking collectives, on_device(): lax.psum(jnp.sum(direction * image, axis=(1, 2, 3)), ('row', 'col'))  44.5 us
    ppermute x4, waiting for transfers between devices, padded_2(): after = lax.ppermute(first, axis, down)  8.8 us
    unnamed x13, local copies, waits for them, and re-layouts  8.47 us
    ppermute x4, starting transfers between devices, padded_2(): before = lax.ppermute(last, axis, up)  8.28 us
  transfers between devices with their start and end apart: 9, of which 4 were waited for; matrix products, arithmetic and copies ran while one was open for 22% of the time, Pallas kernels for 0%

commit v1 on v0

v1 whole, which is shorter than its diff:
```python
import functools

import jax
import jax.numpy as jnp
from jax import lax
from jax.experimental import pallas as pl
from jax.experimental.pallas import tpu as pltpu
from jax.sharding import PartitionSpec as P

AGR = 4
AGC = 4
TILE = 8
GROUP = 2
F32 = jnp.float32
BF16 = jnp.bfloat16
HIGHEST = lax.Precision.HIGHEST
VMEM = pl.BlockSpec(memory_space=pltpu.VMEM)
SMEM = pl.BlockSpec(memory_space=pltpu.SMEM)
PARAMS = pltpu.CompilerParams(vmem_limit_bytes=56 * 1024 * 1024)


def iota(shape, dim):
    return lax.broadcasted_iota(jnp.int32, shape, dim)


def pack(values, count):
    if count < 128:
        fold = 128 // count
        height = values.shape[0] // fold
        return jnp.concatenate(
            [values[p * height : (p + 1) * height, :count] for p in range(fold)], axis=1
        )
    return jnp.concatenate([values[:, j : j + 128] for j in range(0, count, 128)], axis=0)


def unpack(rows, count, sizings):
    if count < 128:
        return jnp.concatenate(
            [rows[:, j : j + count] for j in range(0, 128, count)], axis=0
        )
    return jnp.concatenate(
        [rows[j : j + sizings] for j in range(0, rows.shape[0], sizings)], axis=1
    )


def split3(values):
    first = values.astype(BF16)
    rest = values - first.astype(F32)
    second = rest.astype(BF16)
    third = (rest - second.astype(F32)).astype(BF16)
    return first, second, third


def sums_kernel(dims, ids, ids_row, types_row, load, blocks, top, bottom, pay):
    sizings, rows, cols, nodes, count = dims
    many = rows * cols
    lanes = iota((sizings, max(count, 128)), 1)

    def step(r, sums):
        for c in range(cols):
            b = r * cols + c
            block = load[pl.ds(b, sizings, stride=many), :]
            blocks[pl.ds(pl.multiple_of(b * sizings, sizings), sizings), :] = block
            total = jnp.sum(block, axis=1, keepdims=True)
            sums = sums + jnp.where(lanes == ids[b], total, 0.0)
        return sums

    sums = lax.fori_loop(0, rows, step, jnp.zeros(lanes.shape, F32))
    edge = 2 * cols * sizings
    top[...] = blocks[0:edge, :]
    bottom[...] = blocks[many * sizings - edge : many * sizings, :]
    height = sizings * count // 128
    packed = pack(sums, count)
    spare = jnp.zeros((pay.shape[1] - height - 2, 128), F32)
    whole = jnp.concatenate([packed, ids_row[...], types_row[...], spare], axis=0)

    def copy(d, carry):
        pay[d] = whole
        return carry

    lax.fori_loop(0, pay.shape[0], copy, 0)


def weights_kernel(library, strap, stacked, low, row_sums):
    kinds, nodes, _ = library.shape
    eye = iota((nodes, nodes), 0) == iota((nodes, nodes), 1)
    couple_row = 2.0 * strap[0:1, :] + 2.0 * strap[1:2, :]
    couple_col = jnp.sum(jnp.where(eye, couple_row, 0.0), axis=1, keepdims=True)

    def step(t, carry):
        block = library[t]
        on = jnp.where(eye, block, 0.0)
        inv_row = 1.0 / (jnp.sum(on, axis=0, keepdims=True) + couple_row)
        inv_col = 1.0 / (jnp.sum(on, axis=1, keepdims=True) + couple_col)
        off = jnp.where(eye, 0.0, -block)
        once = inv_col * off * inv_row
        twice = jnp.dot(once, off, precision=HIGHEST, preferred_element_type=F32) * inv_row
        smoother = jnp.where(eye, inv_row, 0.0) + once + twice
        product = jnp.dot(smoother, block, precision=HIGHEST, preferred_element_type=F32)
        both = jnp.concatenate([smoother, product], axis=1)
        high = both.astype(BF16)
        stacked[t] = jnp.concatenate([high, high], axis=0)
        low[t] = (both - high.astype(F32)).astype(BF16)
        row_sums[pl.ds(t, 1), :] = jnp.sum(block, axis=0, keepdims=True)
        return carry

    lax.fori_loop(0, kinds, step, 0)


def sides_kernel(dims, blocks, above, below, west, east):
    sizings, rows, cols, nodes, count = dims
    for out, first in ((west, 0), (east, cols - 2)):
        for side in range(2):
            c = first + side
            for k in range(rows + 2):
                if k == 0:
                    src, at = above, cols + c
                elif k == rows + 1:
                    src, at = below, c
                else:
                    src, at = blocks, (k - 1) * cols + c
                to = (k * 2 + side) * sizings
                out[to : to + sizings, :] = src[at * sizings : (at + 1) * sizings, :]


def sorted_products(order, kinds, pairs, source, stacked, low, sizings, store):
    def step(it, carry):
        for one in range(GROUP):
            tile = it * GROUP + one
            kind = kinds[tile]
            places = [
                pl.ds(pl.multiple_of(order[tile * TILE + j] * sizings, sizings), sizings)
                for j in range(TILE)
            ]
            field = jnp.concatenate([source[place, :] for place in places], axis=0)
            high = field.astype(BF16)
            rest = (field - high.astype(F32)).astype(BF16)
            out = jnp.dot(
                jnp.concatenate([high, rest], axis=1), stacked[kind], preferred_element_type=F32
            ) + jnp.dot(high, low[kind], preferred_element_type=F32)
            store(kind, places, out)
        return carry

    lax.fori_loop(0, pairs, step, 0)


def neighbour_ids(ids, cols):
    height, many = ids.shape
    lane, row = iota(ids.shape, 1), iota(ids.shape, 0)
    down = pltpu.roll(ids, many - cols, 1)
    south = jnp.where(lane < many - cols, down, pltpu.roll(down, height - 1, 0))
    south = jnp.where((lane >= many - cols) & (row == height - 1), -1.0, south)
    up = pltpu.roll(ids, cols, 1)
    north = jnp.where(lane >= cols, up, pltpu.roll(up, 1, 0))
    north = jnp.where((lane < cols) & (row == 0), -1.0, north)
    east = jnp.where(lane % cols == cols - 1, -1.0, pltpu.roll(ids, many - 1, 1))
    west = jnp.where(lane % cols == 0, -1.0, pltpu.roll(ids, 1, 1))
    return south, north, east, west


def invert_unrolled(matrix, count):
    width = matrix.shape[1]
    lane = iota((1, width), 1) % count
    row = iota((count, 1), 0)
    tile_lane = iota((count, 128), 1)
    for k in range(count):
        parts = []
        for base in range(0, width, 128):
            part = jnp.broadcast_to(matrix[:, base + k : base + k + 1], (count, 128))
            for j in range(1, 128 // count):
                at = base + j * count + k
                part = jnp.where(tile_lane >= j * count, matrix[:, at : at + 1], part)
            parts.append(part)
        column = jnp.concatenate(parts, axis=1)
        inverse = 1.0 / column[k : k + 1, :]
        scaled = jnp.where(lane == k, 1.0, matrix[k : k + 1, :]) * inverse
        column = jnp.where(row == k, -1.0, column)
        matrix = jnp.where((lane == k) | (row == k), 0.0, matrix) - column * scaled
    return matrix


def invert_looped(ref, count):
    def step(k, carry):
        for base in range(0, ref.shape[1], count):
            here = slice(base, base + count)
            lane = iota((1, count), 1)
            row = iota((count, 1), 0)
            pivot_row = ref[pl.ds(k, 1), here]
            part = ref[:, here]
            column = jnp.sum(jnp.where(lane == k, part, 0.0), axis=1, keepdims=True)
            inverse = 1.0 / jnp.sum(jnp.where(lane == k, pivot_row, 0.0), axis=1, keepdims=True)
            scaled = jnp.where(lane == k, 1.0, pivot_row) * inverse
            column = jnp.where(row == k, -1.0, column)
            ref[:, here] = jnp.where((lane == k) | (row == k), 0.0, part) - column * scaled
        return carry

    lax.fori_loop(0, count, step, 0)


def coarse_matrices(dims, mesh_dims, gathered, row_sums, strap, inverses, cross, nearby):
    sizings, rows, cols, nodes, count = dims
    n_row, n_col = mesh_dims
    many = rows * cols
    height = sizings * count // 128
    kinds = row_sums.shape[0]
    north_weight = jnp.sum(strap[0:1, :], axis=1, keepdims=True)
    east_weight = jnp.sum(strap[1:2, :], axis=1, keepdims=True)
    block_sums = jnp.sum(row_sums[...], axis=1, keepdims=True)
    names = iota((count, many), 0).astype(F32)
    lane = iota((n_row, many), 1)

    def rows_of(g, at):
        return jnp.concatenate(
            [gathered[i * n_col + g, at : at + 1, :] for i in range(n_row)], axis=0
        )

    all_ids = [rows_of(g, height) for g in range(n_col)]
    eye = iota((count, count), 0) == iota((count, count), 1)
    contract = (((1,), (1,)), ((), ()))
    for g in range(n_col):
        ids = all_ids[g]
        types = rows_of(g, height + 1)
        centre = jnp.zeros(ids.shape, F32) + 2.0 * north_weight + 2.0 * east_weight
        for t in range(kinds):
            centre = centre + jnp.where(types == float(t), block_sums[t : t + 1, :], 0.0)
        beyond = all_ids[min(g + 1, n_col - 1)]
        beyond = jnp.where(lane % cols == cols - 1, pltpu.roll(beyond, cols - 1, 1), -1.0)
        for slot, value in enumerate((ids, *neighbour_ids(ids, cols), beyond, centre)):
            nearby[slot] = value

        def step(i, carry):
            pairs, crossed, diagonal = carry
            hot = [names == nearby[slot, pl.ds(i, 1), :] for slot in range(6)]
            soft = [h.astype(F32).astype(BF16) for h in hot]
            around = jnp.concatenate([soft[1] + soft[2], soft[3] + soft[4], soft[5]], axis=0)
            pairs = pairs + lax.dot_general(
                soft[0], around, contract, preferred_element_type=F32
            )
            diagonal = diagonal + jnp.where(hot[0], nearby[6, pl.ds(i, 1), :], 0.0)
            return pairs, crossed, diagonal

        start = (
            jnp.zeros((count, 3 * count), F32),
            0,
            jnp.zeros((count, many), F32),
        )
        pairs, _, diagonal = lax.fori_loop(0, n_row, step, start, unroll=n_row <= 8)
        diagonal = jnp.sum(diagonal, axis=1, keepdims=True)
        matrix = jnp.where(eye, diagonal, 0.0) - (
            north_weight * pairs[:, :count] + east_weight * pairs[:, count : 2 * count]
        )
        inverses[:, g * count : (g + 1) * count] = matrix
        cross[g] = pairs[:, 2 * count :]


def coarse_solve(gathered, first, height, mesh_dims, count, sizings, inverses, g):
    n_row, n_col = mesh_dims
    total = gathered[g, first : first + height, :]
    for i in range(1, n_row):
        total = total + gathered[i * n_col + g, first : first + height, :]
    sums = unpack(total, count, sizings)
    solved = jnp.dot(
        sums, inverses[:, g * count : (g + 1) * count], precision=HIGHEST,
        preferred_element_type=F32,
    )
    return sums, solved


def spread(solved, col, keys, out, count, sizings, nodes, many):
    three = jnp.concatenate([solved[col], solved[col + 1], solved[col + 2]], axis=1)
    hot = (iota((3 * count, keys.shape[1]), 0) == keys[...]).astype(F32).astype(BF16)
    parts = jnp.concatenate(split3(three), axis=0)
    values = jnp.dot(parts, hot, preferred_element_type=F32)
    values = (
        values[2 * sizings : 3 * sizings] + values[sizings : 2 * sizings] + values[:sizings]
    )
    for e in range(many):
        out[e * sizings : (e + 1) * sizings, :] = jnp.broadcast_to(
            values[:, e : e + 1], (sizings, nodes)
        )


def middle_kernel(
    dims, mesh_dims,
    order_1, kinds_1, order_2, kinds_2, info, ids,
    gathered, keys, blocks, above, below, west, east, stacked, low, row_sums, strap,
    z_out, q_out, u_out, au_out, inverses, cross, pay,
    field, level, z, bz, q, u, bu, solved, nearby,
):
    sizings, rows, cols, nodes, count = dims
    n_row, n_col = mesh_dims
    wide = cols + 4
    many = (rows + 4) * wide
    height = sizings * count // 128

    def at(er, ec):
        return pl.ds(pl.multiple_of((er * wide + ec) * sizings, sizings), sizings)

    span = cols * sizings
    for r in range(rows):
        to = ((r + 2) * wide + 2) * sizings
        field[to : to + span, :] = blocks[r * span : (r + 1) * span, :]
    for r in range(2):
        to = (r * wide + 2) * sizings
        field[to : to + span, :] = above[r * span : (r + 1) * span, :]
        to = ((rows + 2 + r) * wide + 2) * sizings
        field[to : to + span, :] = below[r * span : (r + 1) * span, :]
    for k in range(rows + 2):
        pair = 2 * sizings
        to = (k + 1) * wide * sizings
        field[to : to + pair, :] = west[k * pair : (k + 1) * pair, :]
        to = to + (cols + 2) * sizings
        field[to : to + pair, :] = east[k * pair : (k + 1) * pair, :]
    field[many * sizings :, :] = jnp.zeros((sizings, nodes), F32)
    level[many * sizings :, :] = jnp.zeros((sizings, nodes), F32)
    q[many * sizings :, :] = jnp.zeros((sizings, nodes), F32)

    coarse_matrices(dims, mesh_dims, gathered, row_sums, strap, inverses, cross, nearby)
    if count <= 64:
        inverses[...] = invert_unrolled(inverses[...], count)
    else:
        invert_looped(inverses, count)
    solved[0] = jnp.zeros((sizings, count), F32)
    solved[n_col + 1] = jnp.zeros((sizings, count), F32)
    for g in range(n_col):
        _, solved[g + 1] = coarse_solve(
            gathered, 0, height, mesh_dims, count, sizings, inverses, g
        )
    spread(solved, info[2], keys, level, count, sizings, nodes, many)

    def store_z(kind, places, out):
        sums = row_sums[pl.ds(kind, 1), :]
        for j, place in enumerate(places):
            here = level[place, :]
            z[place, :] = out[j * sizings : (j + 1) * sizings, :nodes] + here
            bz[place, :] = out[j * sizings : (j + 1) * sizings, nodes:] + sums * here

    sorted_products(order_1, kinds_1, info[0], field, stacked, low, sizings, store_z)

    north, east_strap = strap[0:1, :], strap[1:2, :]
    couple = 2.0 * north + 2.0 * east_strap

    def operator(v, bv, er, ec):
        here = v[at(er, ec), :]
        image = (
            bv[at(er, ec), :]
            + couple * here
            - north * (v[at(er - 1, ec), :] + v[at(er + 1, ec), :])
            - east_strap * (v[at(er, ec - 1), :] + v[at(er, ec + 1), :])
        )
        return here, image

    for er, flag in ((1, info[3]), (rows + 2, info[4])):
        inside = flag.astype(F32)

        def across(ec, carry):
            q[at(er, ec), :] = operator(z, bz, er, ec)[1] * inside
            return carry

        lax.fori_loop(2, cols + 2, across, 0)
    for ec, flag in ((1, info[5]), (cols + 2, info[6])):
        inside = flag.astype(F32)

        def along(er, carry):
            q[at(er, ec), :] = operator(z, bz, er, ec)[1] * inside
            return carry

        lax.fori_loop(2, rows + 2, along, 0)

    lanes = iota((sizings, max(count, 128)), 1)
    blank = jnp.zeros((sizings, nodes), F32)
    zero_sums = jnp.zeros(lanes.shape, F32)

    def first_row(r, carry):
        rz, zq, sums = carry
        for c in range(cols):
            here, image = operator(z, bz, r + 2, c + 2)
            q[at(r + 2, c + 2), :] = image
            b = r * cols + c
            own = pl.ds(pl.multiple_of(b * sizings, sizings), sizings)
            z_out[own, :] = here
            q_out[own, :] = image
            rz = rz + blocks[own, :] * here
            zq = zq + here * image
            total = jnp.sum(image, axis=1, keepdims=True)
            sums = sums + jnp.where(lanes == ids[b], total, 0.0)
        return rz, zq, sums

    rz, zq, sums_q = lax.fori_loop(0, rows, first_row, (blank, blank, zero_sums))

    def store_u(kind, places, out):
        for j, place in enumerate(places):
            u[place, :] = out[j * sizings : (j + 1) * sizings, :nodes]
            bu[place, :] = out[j * sizings : (j + 1) * sizings, nodes:]

    sorted_products(order_2, kinds_2, info[1], q, stacked, low, sizings, store_u)

    def second_row(r, carry):
        qu, uau, sums = carry
        for c in range(cols):
            here, image = operator(u, bu, r + 2, c + 2)
            b = r * cols + c
            own = pl.ds(pl.multiple_of(b * sizings, sizings), sizings)
            u_out[own, :] = here
            au_out[own, :] = image
            qu = qu + q[at(r + 2, c + 2), :] * here
            uau = uau + here * image
            total = jnp.sum(image, axis=1, keepdims=True)
            sums = sums + jnp.where(lanes == ids[b], total, 0.0)
        return qu, uau, sums

    qu, uau, sums_u = lax.fori_loop(0, rows, second_row, (blank, blank, zero_sums))

    lane = iota((sizings, 128), 1)
    dots = jnp.zeros((sizings, 128), F32)
    for j, one in enumerate((rz, zq, qu, uau)):
        dots = jnp.where(lane % 4 == j, jnp.sum(one, axis=1, keepdims=True), dots)
    dots = jnp.where(lane // 4 == iota((sizings, 128), 0), dots, 0.0)
    dots = jnp.sum(dots, axis=0, keepdims=True)
    whole = jnp.concatenate([pack(sums_q, count), pack(sums_u, count), dots], axis=0)

    def copy(d, carry):
        pay[d] = whole
        return carry

    lax.fori_loop(0, pay.shape[0], copy, 0)


def last_kernel(
    dims, mesh_dims,
    types, info,
    gathered, keys, inverses, cross, z, q, u, au, blocks, row_sums, strap,
    voltage, residual,
    level, solved,
):
    sizings, rows, cols, nodes, count = dims
    n_row, n_col = mesh_dims
    wide = cols + 4
    many = (rows + 4) * wide
    height = sizings * count // 128
    mesh_args = (mesh_dims, count, sizings)

    solved[0] = jnp.zeros((sizings, count), F32)
    solved[n_col + 1] = jnp.zeros((sizings, count), F32)
    with_q = jnp.zeros((sizings, count), F32)
    with_u = jnp.zeros((sizings, count), F32)
    crossed = jnp.zeros((sizings, count), F32)
    before = None
    for g in range(n_col):
        sums, one = coarse_solve(gathered, 0, height, *mesh_args, inverses, g)
        solved[g + 1] = one
        image = gathered[g, height : 2 * height, :]
        for i in range(1, n_row):
            image = image + gathered[i * n_col + g, height : 2 * height, :]
        with_q = with_q + sums * one
        with_u = with_u + unpack(image, count, sizings) * one
        if before is not None:
            crossed = crossed + one * jnp.dot(
                before, cross[g - 1], precision=HIGHEST, preferred_element_type=F32
            )
        before = one
    spread(solved, info[2], keys, level, count, sizings, nodes, many)

    dots = gathered[0, 2 * height : 2 * height + 1, :]
    for d in range(1, n_row * n_col):
        dots = dots + gathered[d, 2 * height : 2 * height + 1, :]
    lane = iota((sizings, 128), 1)
    dots = jnp.where(lane // 4 == iota((sizings, 128), 0), dots, 0.0)
    rz, zq, qu, uau = [
        jnp.sum(jnp.where(lane % 4 == j, dots, 0.0), axis=1, keepdims=True) for j in range(4)
    ]
    east_weight = jnp.sum(strap[1:2, :], axis=1, keepdims=True)
    total = functools.partial(jnp.sum, axis=1, keepdims=True)
    qw = qu + total(with_q)
    wp = uau + 2.0 * total(with_u) + total(with_q) - 2.0 * east_weight * total(crossed)
    step_1 = rz / zq
    fresh = step_1 * step_1 * qw - rz
    grown = 1.0 + fresh / rz
    step_2 = fresh / (grown * grown * zq - 2.0 * grown * step_1 * qw + step_1 * step_1 * wp)
    alpha = jnp.broadcast_to(step_1 + step_2 * grown, (sizings, nodes))
    gamma = jnp.broadcast_to(-step_2 * step_1, (sizings, nodes))

    north, east_strap = strap[0:1, :], strap[1:2, :]
    couple = 2.0 * north + 2.0 * east_strap

    def step(r, carry):
        for c in range(cols):
            b = r * cols + c
            own = pl.ds(pl.multiple_of(b * sizings, sizings), sizings)

            def value(dr, dc):
                e = (r + 2 + dr) * wide + c + 2 + dc
                return level[pl.ds(pl.multiple_of(e * sizings, sizings), sizings), :]

            here = value(0, 0)
            lift = (
                (row_sums[pl.ds(types[b], 1), :] + couple) * here
                - north * (value(-1, 0) + value(1, 0))
                - east_strap * (value(0, -1) + value(0, 1))
            )
            voltage[pl.ds(b, sizings, stride=rows * cols), :] = alpha * z[own, :] + gamma * (
                u[own, :] + here
            )
            residual[pl.ds(b, sizings, stride=rows * cols), :] = (
                blocks[own, :] - alpha * q[own, :] - gamma * (au[own, :] + lift)
            )
        return carry

    lax.fori_loop(0, rows, step, 0)


def tile_plan(types, needed, kinds, many):
    n = sum(needed)
    most = (n + (TILE - 1) * kinds) // TILE
    most = -(-most // GROUP) * GROUP
    flat = jnp.where(jnp.array(needed), types.reshape(-1), kinds)
    hot = (flat[None, :] == jnp.arange(kinds)[:, None]).astype(jnp.int32)
    index = jnp.arange(many)
    rank = jnp.dot(
        hot.astype(BF16), (index[:, None] < index[None, :]).astype(BF16),
        preferred_element_type=F32,
    ).astype(jnp.int32)
    tiles = (jnp.sum(hot, axis=1) + TILE - 1) // TILE
    below = jnp.arange(kinds)[:, None] >= jnp.arange(kinds)[None, :]
    ends = jnp.sum(jnp.where(below, tiles[None, :], 0), axis=1)
    starts = ends - tiles
    place = jnp.sum(hot * (starts[:, None] * TILE + rank + 1), axis=0) - 1
    slots = jnp.arange(most * TILE)
    order = many + jnp.sum(
        jnp.where(place[None, :] == slots[:, None], index[None, :] - many, 0), axis=1
    )
    tile_kinds = jnp.sum(jnp.arange(most)[:, None] >= ends[None, :], axis=1)
    tile_kinds = jnp.minimum(tile_kinds, kinds - 1)
    groups = (ends[-1] + GROUP - 1) // GROUP
    return order.astype(jnp.int32), tile_kinds.astype(jnp.int32), groups.astype(jnp.int32)


def call(kernel, in_specs, out_shape, scratch, cost):
    return pl.pallas_call(
        kernel,
        in_specs=in_specs,
        out_specs=jax.tree.map(lambda _: VMEM, out_shape),
        out_shape=out_shape,
        scratch_shapes=scratch,
        compiler_params=PARAMS,
        cost_estimate=pl.CostEstimate(flops=cost, bytes_accessed=4_000_000, transcendentals=0),
    )


def on_device(load_currents, block_library, strap_conductance, block_types, aggregate_map):
    sizings, rows, cols, nodes = load_currents.shape
    kinds = block_library.shape[0]
    n_row, n_col = lax.axis_size("row"), lax.axis_size("col")
    n_dev = n_row * n_col
    row, col = lax.axis_index("row"), lax.axis_index("col")
    count = rows * n_row // AGR * (cols // AGC)
    dims, mesh_dims = (sizings, rows, cols, nodes, count), (n_row, n_col)
    block_rows = rows * cols * sizings
    wide, tall = cols + 4, rows + 4
    many = wide * tall
    height = sizings * count // 128
    shape = jax.ShapeDtypeStruct

    edge = shape((2 * cols * sizings, nodes), F32)
    own = shape((block_rows, nodes), F32)
    ids = aggregate_map.reshape(-1)
    types = block_types.reshape(-1)
    pay_rows = -(-(height + 2) // 8) * 8
    blocks, top, bottom, pay = call(
        functools.partial(sums_kernel, dims),
        [SMEM] + [VMEM] * 3,
        [own, edge, edge, shape((n_dev, pay_rows, 128), F32)],
        [],
        1_000_000,
    )(
        ids,
        ids.reshape(1, -1).astype(F32),
        types.reshape(1, -1).astype(F32),
        load_currents.reshape(-1, nodes),
    )
    forth = [(i, i + 1) for i in range(n_row - 1)]
    above = lax.ppermute(bottom, "row", forth)
    below = lax.ppermute(top, "row", [(j, i) for i, j in forth])
    gathered = lax.all_to_all(pay, ("row", "col"), 0, 0)
    stacked, low, row_sums = call(
        weights_kernel,
        [VMEM, VMEM],
        [
            shape((kinds, 2 * nodes, 2 * nodes), BF16),
            shape((kinds, nodes, 2 * nodes), BF16),
            shape((kinds, nodes), F32),
        ],
        [],
        1_000_000_000,
    )(block_library, strap_conductance)
    side = shape(((rows + 2) * 2 * sizings, nodes), F32)
    to_west, to_east = call(
        functools.partial(sides_kernel, dims), [VMEM] * 3, [side, side], [], 1_000_000
    )(blocks, above, below)
    forth = [(i, i + 1) for i in range(n_col - 1)]
    west = lax.ppermute(to_east, "col", forth)
    east = lax.ppermute(to_west, "col", [(j, i) for i, j in forth])

    def die(at):
        whole = gathered[:, at, :].astype(jnp.int32).reshape(n_row, n_col, rows, cols)
        whole = whole.transpose(0, 2, 1, 3).reshape(n_row * rows, n_col * cols)
        whole = jnp.pad(whole, 2, constant_values=-1)
        return lax.dynamic_slice(whole, (row * rows, col * cols), (tall, wide))

    place = jnp.arange(wide)
    relative = (place >= 2).astype(jnp.int32) + (place >= cols + 2).astype(jnp.int32)
    near_ids, near_types = die(height), jnp.maximum(die(height + 1), 0)
    keys = jnp.where(near_ids >= 0, near_ids + relative[None, :] * count, -1).reshape(1, -1)
    keys = jnp.pad(keys, ((0, 0), (0, -many % 128)), constant_values=-1)

    def ring(er, ec):
        down = max(2 - er, er - (rows + 1), 0)
        over = max(2 - ec, ec - (cols + 1), 0)
        return down, over

    rings = [ring(er, ec) for er in range(tall) for ec in range(wide)]
    needed_1 = [down + over <= 2 for down, over in rings]
    needed_2 = [down + over <= 1 for down, over in rings]
    order_1, kinds_1, groups_1 = tile_plan(near_types, needed_1, kinds, many)
    order_2, kinds_2, groups_2 = tile_plan(near_types, needed_2, kinds, many)
    info = jnp.stack(
        [
            groups_1,
            groups_2,
            col,
            (row > 0).astype(jnp.int32),
            (row < n_row - 1).astype(jnp.int32),
            (col > 0).astype(jnp.int32),
            (col < n_col - 1).astype(jnp.int32),
        ]
    )
    big = pltpu.VMEM(((many + 1) * sizings, nodes), F32)
    coarse = pltpu.VMEM((n_col + 2, sizings, count), F32)
    z, q, u, au, inverses, cross, pay = call(
        functools.partial(middle_kernel, dims, mesh_dims),
        [SMEM] * 6 + [VMEM] * 11,
        [own] * 4
        + [
            shape((count, n_col * count), F32),
            shape((n_col, count, count), F32),
            shape((n_dev, 2 * height + 1, 128), F32),
        ],
        [big] * 7 + [coarse, pltpu.VMEM((7, n_row, rows * cols), F32)],
        1_000_000_000,
    )(
        order_1, kinds_1, order_2, kinds_2, info, ids,
        gathered, keys, blocks, above, below, west, east, stacked, low, row_sums,
        strap_conductance,
    )
    gathered = lax.all_to_all(pay, ("row", "col"), 0, 0)
    out = shape((sizings * rows * cols, nodes), F32)
    voltage, residual = call(
        functools.partial(last_kernel, dims, mesh_dims),
        [SMEM] * 2 + [VMEM] * 11,
        [out, out],
        [big, coarse],
        1_000_000_000,
    )(
        types, info,
        gathered, keys, inverses, cross, z, q, u, au, blocks, row_sums, strap_conductance,
    )
    return voltage.reshape(load_currents.shape), residual.reshape(load_currents.shape)


def solution(mesh):
    placed = (P(None, "row", "col", None), P(), P(), P("row", "col"), P("row", "col"))
    return jax.shard_map(
        on_device,
        mesh=mesh,
        in_specs=placed,
        out_specs=(P(None, "row", "col", None), P(None, "row", "col", None)),
        check_vma=False,
    )
```

time: 395 us -> 103 us (0.26); the launches traced: 388 us -> 103 us
  blocking collectives: 203 us -> 0 us
  matrix products: 92.9 us -> 0.32 us
  Pallas kernels: 0 us -> 45.2 us
  other arithmetic: 39.1 us -> 3.51 us
  local copies, waits for them, and re-layouts: 23.3 us -> 9.55 us
  starting transfers between devices: 14.7 us -> 24.5 us
  waiting for transfers between devices: 11.2 us -> 17.6 us
    psum x5 -> x0, blocking collectives: 203 us -> none  [the longest x2 80.4 us: alignment_sum(): return lax.psum(jnp.sum(residual * zeta, axis=(1, 2, 3)), ('row', 'col'))]
    dot_general x6 -> x2, matrix products: 92.1 us -> 0.32 us  [tile_plan(): jnp.dot(hot.astype(BF16), (index[:, None] < index[None, :]).astype(BF16),...]
    pallas_call x0 -> x5, Pallas kernels: none -> 45.2 us  [the longest x1 25.4 us: on_device(): call(functools.partial(middle_kernel, dims, mesh_dims), [SMEM] * 6 + [VME...]
    all_to_all x0 -> x2, starting transfers between devices: none -> 16.7 us  [on_device(): gathered = lax.all_to_all(pay, ('row', 'col'), 0, 0)]
    all_to_all x0 -> x2, waiting for transfers between devices: none -> 12.6 us  [on_device(): gathered = lax.all_to_all(pay, ('row', 'col'), 0, 0)]
    another operation x6 -> x0, other arithmetic: 12.2 us -> none  [the longest x3 6.52 us: on_device(): factor = jnp.linalg.cholesky(coarse_matrix)]
    add x11 -> x2, other arithmetic: 11.1 us -> 1.19 us  [tile_plan(): many + jnp.sum(jnp.where(place[None, :] == slots[:, None], index[None, :]...]
    gather x7 -> x0, local copies, waits for them, and re-layouts: 9.32 us -> none  [the longest x1 4.31 us: on_device(): picked = block_library[block_types.reshape(-1)]]
  transfers between devices with their start and end apart: 9 -> 6, of which waited for: 4 -> 2; matrix products, arithmetic and copies ran while one was open for 22% -> 7% of each run, Pallas kernels for 0% -> 8%
where the time goes in v1:
time: 103 us
  Pallas kernels  45.2 us (44%)
  starting transfers between devices  24.5 us (24%)
  waiting for transfers between devices  17.6 us (17%)
  local copies, waits for them, and re-layouts  9.55 us (9%)
  other arithmetic  3.51 us (3%)
  between operations  2.1 us (2%)
    pallas_call x1, Pallas kernels, on_device(): call(functools.partial(middle_kernel, dims, mesh_dims), [SMEM] * 6 + [VME...  25.4 us
    all_to_all x2, starting transfers between devices, on_device(): gathered = lax.all_to_all(pay, ('row', 'col'), 0, 0)  16.7 us
    all_to_all x2, waiting for transfers between devices, on_device(): gathered = lax.all_to_all(pay, ('row', 'col'), 0, 0)  12.6 us
    pallas_call x1, Pallas kernels, on_device(): call(functools.partial(last_kernel, dims, mesh_dims), [SMEM] * 2 + [VMEM]...  7.37 us
    pallas_call x1, Pallas kernels, on_device(): call(weights_kernel, [VMEM, VMEM], [shape((kinds, 2 * nodes, 2 * nodes),...  6.42 us
    ppermute x1, waiting for transfers between devices, on_device(): above = lax.ppermute(bottom, 'row', forth)  4.99 us
    pallas_call x1, Pallas kernels, on_device(): call(functools.partial(sums_kernel, dims), [SMEM] + [VMEM] * 3, [own, edg...  3.91 us
    ppermute x1, starting transfers between devices, on_device(): above = lax.ppermute(bottom, 'row', forth)  3.69 us
  transfers between devices with their start and end apart: 6, of which 2 were waited for; matrix products, arithmetic and copies ran while one was open for 7% of the time, Pallas kernels for 8%

profile of v1, /device:TPU:0, one launch (start us, length us, event | category | flops | bytes accessed | tf_op | source)
XLA Modules:
  0.0 102.7 jit_solution(7878351161227340068)
XLA Ops:
  0.6 1.3 %reshape.177.ids = s32[128]{0:T(128)} reshape(s32[8,16]{1,0:T(8,128)} %param.11) | data formatting | bytes 1024 | tf_op jit(solution)/shard_map/reshape | solution.py:566
  2.0 0.6 convert_element_type.69.ids_row
  2.6 0.6 convert_element_type.71.types_row
  3.3 3.9 %shard_map.86 = (f32[2048,128]{1,0:T(8,128)}, f32[512,128]{1,0:T(8,128)}, f32[512,128]{1,0:T(8,128)}, f32[32,16,128]{2,1,0:T(8,128)}) custom-call(s32[128]{0:T(128)} %reshape.177.ids, f32[1,128]{1,0:T(1,128)} %convert_element_type.69.ids_row, f32[1,128]{1,0:T(1,128)} %convert_element_type.71.types_row, f32[2048,128]{1,0:T(8,128)} %bitcast.14), custom_call_target="tpu_custom_call" | custom-call | flops 1000000 | bytes 4000000 | tf_op jit(solution)/shard_map/pallas_call | solution.py:569
  7.2 7.3 %all-to-all-start = ((f32[32,16,128]{2,1,0:T(8,128)}), f32[32,16,128]{2,1,0:T(8,128)S(1)}, u32[]{:S(2)}, u32[]{:S(2)}) async-start(f32[32,16,128]{2,1,0:T(8,128)} %get-tuple-element.20), calls=%async_computation | async-start | bytes 524288 | tf_op jit(solution)/shard_map/all_to_all | solution.py:584
  14.5 3.7 %collective-permute-start = (f32[512,128]{1,0:T(8,128)S(1)}, f32[512,128]{1,0:T(8,128)S(1)}, u32[]{:S(2)}, u32[]{:S(2)}) collective-permute-start(f32[512,128]{1,0:T(8,128)S(1)} %copy-done.11), channel_id=1, source_target_pairs={{0,4},{4,8},{8,12},{12,16},{16,20},{20,24},{24,28},{1,5},{5,9},{9,... | collective-permute-start | bytes 786440 | tf_op jit(solution)/shard_map/ppermute | solution.py:582
  18.2 1.3 %collective-permute-start.1 = (f32[512,128]{1,0:T(8,128)S(1)}, f32[512,128]{1,0:T(8,128)S(1)}, u32[]{:S(2)}, u32[]{:S(2)}) collective-permute-start(f32[512,128]{1,0:T(8,128)S(1)} %copy-done.10), channel_id=1, source_target_pairs={{4,0},{8,4},{12,8},{16,12},{20,16},{24,20},{28,24},{5,1},{9,5},{13... | collective-permute-start | bytes 786440 | tf_op jit(solution)/shard_map/ppermute | solution.py:583
  19.5 6.4 %shard_map.88 = (bf16[8,256,256]{2,1,0:T(8,128)(2,1)}, bf16[8,128,256]{2,1,0:T(8,128)(2,1)}, f32[8,128]{1,0:T(8,128)}) custom-call(f32[8,128,128]{2,1,0:T(8,128)} %library.1, f32[2,128]{1,0:T(2,128)} %strap.5), custom_call_target="tpu_custom_call" | custom-call | flops 1000000000 | bytes 4000000 | tf_op jit(solution)/shard_map/pallas_call | solution.py:585
  25.9 5.0 %collective-permute-done.above = f32[512,128]{1,0:T(8,128)S(1)} collective-permute-done((f32[512,128]{1,0:T(8,128)S(1)}, f32[512,128]{1,0:T(8,128)S(1)}, u32[]{:S(2)}, u32[]{:S(2)}) %collective-permute-start) | collective-permute-done | bytes 262176 | tf_op jit(solution)/shard_map/ppermute | solution.py:582
  30.9 0.7 copy-done.2
  31.6 0.1 copy-done.3
  31.7 2.1 %shard_map.87 = (f32[320,128]{1,0:T(8,128)}, f32[320,128]{1,0:T(8,128)}) custom-call(f32[2048,128]{1,0:T(8,128)} %get-tuple-element.21.blocks, f32[512,128]{1,0:T(8,128)} %copy-done.2, f32[512,128]{1,0:T(8,128)} %copy-done.3), custom_call_target="tpu_custom_call" | custom-call | flops 1000000 | bytes 4000000 | tf_op jit(solution)/shard_map/pallas_call | solution.py:597
  33.8 1.5 %collective-permute-start.2 = (f32[320,128]{1,0:T(8,128)}, f32[320,128]{1,0:T(8,128)S(1)}, u32[]{:S(2)}, u32[]{:S(2)}) collective-permute-start(f32[320,128]{1,0:T(8,128)} %get-tuple-element.24), channel_id=1, source_target_pairs={{0,1},{1,2},{2,3},{4,5},{5,6},{6,7},{8,9},{9,10},{10,11},{12,13},{... | collective-permute-start | bytes 491528 | tf_op jit(solution)/shard_map/ppermute | solution.py:601
  35.3 1.3 %collective-permute-start.3 = (f32[320,128]{1,0:T(8,128)}, f32[320,128]{1,0:T(8,128)S(1)}, u32[]{:S(2)}, u32[]{:S(2)}) collective-permute-start(f32[320,128]{1,0:T(8,128)} %get-tuple-element.25), channel_id=1, source_target_pairs={{1,0},{2,1},{3,2},{5,4},{6,5},{7,6},{9,8},{10,9},{11,10},{13,12},{... | collective-permute-start | bytes 491528 | tf_op jit(solution)/shard_map/ppermute | solution.py:602
  36.7 0.1 fusion.8
  36.8 0.1 convert_element_type.73
  36.9 0.1 reshape.179
  37.0 0.3 copy-done.1
  37.3 0.1 convert_element_type.83
  37.5 0.1 reshape.181
  37.6 0.5 copy-done.8
  38.2 0.1 fusion.12
  38.3 0.1 reshape.190
  38.4 0.1 convert_reduce_fusion
  38.5 0.1 select_reduce_fusion.2
  38.6 0.6 slice.14
  39.9 0.1 convert_reduce_fusion.1
  40.1 0.1 select_reduce_fusion.3
  40.2 0.6 slice.13
  41.5 0.1 convert_reduce_fusion.2
  41.6 0.1 convert_reduce_fusion.3
  41.6 0.2 fusion.7
  41.8 0.1 select_reduce_fusion.1
  41.9 0.6 broadcast_add_fusion.1.order_2
  42.5 0.2 fusion.6
  42.7 0.1 select_reduce_fusion
  42.8 0.6 broadcast_add_fusion.order_1
  43.4 0.6 broadcast_minimum_fusion.kinds_2
  44.1 0.6 pad.13.keys
  44.7 0.6 stack.47.info
  45.3 0.6 broadcast_minimum_fusion.1.kinds_1
  45.9 0.7 copy-done.4
  46.6 25.4 %shard_map.89 = (f32[2048,128]{1,0:T(8,128)}, f32[2048,128]{1,0:T(8,128)}, f32[2048,128]{1,0:T(8,128)}, f32[2048,128]{1,0:T(8,128)}, f32[64,256]{1,0:T(8,128)}, ...) custom-call(s32[288]{0:T(512)} %broadcast_add_fusion.order_1, s32[36]{0:T(128)} %broadcast_minimum_fusion.1.kinds_1, ...), custom_call_target="tpu_custom_call" | custom-call | flops 1000000000 | bytes 4000000 | tf_op jit(solution)/shard_map/pallas_call | solution.py:639
  72.0 9.4 %all-to-all-start.1 = ((f32[32,17,128]{2,1,0:T(8,128)}), f32[32,17,128]{2,1,0:T(8,128)S(1)}, u32[]{:S(2)}, u32[]{:S(2)}) async-start(f32[32,17,128]{2,1,0:T(8,128)} %get-tuple-element.29), calls=%async_computation.1 | async-start | bytes 786432 | tf_op jit(solution)/shard_map/all_to_all | solution.py:655
  81.4 0.6 reshape.176.types
  82.0 12.6 %all-to-all-done.1.gathered = f32[32,17,128]{2,1,0:T(8,128)S(1)} async-done(((f32[32,17,128]{2,1,0:T(8,128)}), f32[32,17,128]{2,1,0:T(8,128)S(1)}, u32[]{:S(2)}, u32[]{:S(2)}) %all-to-all-start.1) | async-done | bytes 278560 | tf_op jit(solution)/shard_map/all_to_all | solution.py:655
  94.6 0.7 copy-done
  95.3 7.4 %shard_map.90 = (f32[2048,128]{1,0:T(8,128)}, f32[2048,128]{1,0:T(8,128)}) custom-call(s32[128]{0:T(128)} %reshape.176.types, s32[7]{0:T(128)} %stack.47.info, f32[32,17,128]{2,1,0:T(8,128)} %copy-done, s32[1,256]{1,0:T(1,128)} %pad.13.keys, f32[64,256]{1,0:T(8,128)} %get-tuple-element.30.inverses, f32[4,64,64]{2,1,0:T(8,128)} %get-tuple-element.31.cross, ...), custom_call_target="tpu_custom_call" | custom-call | flops 1000000000 | bytes 4000000 | tf_op jit(solution)/shard_map/pallas_call | solution.py:657
  (36 shorter events, 0.5 us)
Async XLA Ops:
  0.6 1.3 %copy-start.6 = (s32[8,16]{1,0:T(8,128)S(1)}, s32[8,16]{1,0:T(8,128)}, u32[]{:S(2)}) copy-start(s32[8,16]{1,0:T(8,128)} %param.11) | copy-start | bytes 1540
  2.0 0.7 copy-start.7
  7.2 7.3 %copy-start.11 = (f32[512,128]{1,0:T(8,128)S(1)}, f32[512,128]{1,0:T(8,128)}, u32[]{:S(2)}) copy-start(f32[512,128]{1,0:T(8,128)} %get-tuple-element.22) | copy-start | bytes 786436
  7.2 11.0 %copy-start.10 = (f32[512,128]{1,0:T(8,128)S(1)}, f32[512,128]{1,0:T(8,128)}, u32[]{:S(2)}) copy-start(f32[512,128]{1,0:T(8,128)} %get-tuple-element.23) | copy-start | bytes 786436
  7.2 29.5 %all-to-all-start = ((f32[32,16,128]{2,1,0:T(8,128)}), f32[32,16,128]{2,1,0:T(8,128)S(1)}, u32[]{:S(2)}, u32[]{:S(2)}) async-start(f32[32,16,128]{2,1,0:T(8,128)} %get-tuple-element.20), calls=%async_computation | async-start | bytes 524288 | tf_op jit(solution)/shard_map/all_to_all | solution.py:584
  14.5 16.4 %collective-permute-start = (f32[512,128]{1,0:T(8,128)S(1)}, f32[512,128]{1,0:T(8,128)S(1)}, u32[]{:S(2)}, u32[]{:S(2)}) collective-permute-start(f32[512,128]{1,0:T(8,128)S(1)} %copy-done.11), channel_id=1, source_target_pairs={{0,4},{4,8},{8,12},{12,16},{16,20},{20,24},{24,28},{1,5},{5,9},{9,... | collective-permute-start | bytes 786440 | tf_op jit(solution)/shard_map/ppermute | solution.py:582
  18.2 12.7 %collective-permute-start.1 = (f32[512,128]{1,0:T(8,128)S(1)}, f32[512,128]{1,0:T(8,128)S(1)}, u32[]{:S(2)}, u32[]{:S(2)}) collective-permute-start(f32[512,128]{1,0:T(8,128)S(1)} %copy-done.10), channel_id=1, source_target_pairs={{4,0},{8,4},{12,8},{16,12},{20,16},{24,20},{28,24},{5,1},{9,5},{13... | collective-permute-start | bytes 786440 | tf_op jit(solution)/shard_map/ppermute | solution.py:583
  30.9 0.7 copy-start.2
  30.9 0.8 copy-start.3
  33.8 12.1 %collective-permute-start.2 = (f32[320,128]{1,0:T(8,128)}, f32[320,128]{1,0:T(8,128)S(1)}, u32[]{:S(2)}, u32[]{:S(2)}) collective-permute-start(f32[320,128]{1,0:T(8,128)} %get-tuple-element.24), channel_id=1, source_target_pairs={{0,1},{1,2},{2,3},{4,5},{5,6},{6,7},{8,9},{9,10},{10,11},{12,13},{... | collective-permute-start | bytes 491528 | tf_op jit(solution)/shard_map/ppermute | solution.py:601
  35.3 10.6 %collective-permute-start.3 = (f32[320,128]{1,0:T(8,128)}, f32[320,128]{1,0:T(8,128)S(1)}, u32[]{:S(2)}, u32[]{:S(2)}) collective-permute-start(f32[320,128]{1,0:T(8,128)} %get-tuple-element.25), channel_id=1, source_target_pairs={{1,0},{2,1},{3,2},{5,4},{6,5},{7,6},{9,8},{10,9},{11,10},{13,12},{... | collective-permute-start | bytes 491528 | tf_op jit(solution)/shard_map/ppermute | solution.py:602
  36.6 0.7 copy-start.1
  37.5 0.7 copy-start.8
  37.5 0.7 copy-start.9
  45.9 0.7 copy-start.4
  45.9 0.7 copy-start.5
  72.0 22.6 %all-to-all-start.1 = ((f32[32,17,128]{2,1,0:T(8,128)}), f32[32,17,128]{2,1,0:T(8,128)S(1)}, u32[]{:S(2)}, u32[]{:S(2)}) async-start(f32[32,17,128]{2,1,0:T(8,128)} %get-tuple-element.29), calls=%async_computation.1 | async-start | bytes 786432 | tf_op jit(solution)/shard_map/all_to_all | solution.py:655
  94.6 0.7 copy-start

commit v2 on v1

--- a/solution.py
+++ b/solution.py
@@ -6,17 +6,18 @@
 from jax.experimental import pallas as pl
 from jax.experimental.pallas import tpu as pltpu
 from jax.sharding import PartitionSpec as P
+import numpy as np
 
 AGR = 4
 AGC = 4
 TILE = 8
 GROUP = 2
+PANEL = 8
 F32 = jnp.float32
 BF16 = jnp.bfloat16
 HIGHEST = lax.Precision.HIGHEST
 VMEM = pl.BlockSpec(memory_space=pltpu.VMEM)
 SMEM = pl.BlockSpec(memory_space=pltpu.SMEM)
-PARAMS = pltpu.CompilerParams(vmem_limit_bytes=56 * 1024 * 1024)
 
 
 def iota(shape, dim):
@@ -51,7 +52,41 @@
     return first, second, third
 
 
-def sums_kernel(dims, ids, ids_row, types_row, load, blocks, top, bottom, pay):
+def flat_row(table, many):
+    rows, cols = table.shape
+    repeat = (iota((cols, many), 1) % cols == iota((cols, many), 0)).astype(F32).astype(BF16)
+    wide = jnp.dot(table.astype(F32).astype(BF16), repeat, preferred_element_type=F32)
+    own = iota((rows, many), 1) // cols == iota((rows, many), 0)
+    return jnp.sum(jnp.where(own, wide, 0.0), axis=0, keepdims=True)
+
+
+def meta_rows(types, ids, many, height):
+    rows = [flat_row(types[...], many), flat_row(ids[...], many) + 1.0]
+    return jnp.concatenate(rows + [jnp.zeros((height - 2, many), F32)], axis=0)
+
+
+def edges_kernel(dims, load, types, ids, top, bottom, sems):
+    sizings, rows, cols, nodes, count = dims
+    many = rows * cols
+    copies = [
+        pltpu.make_async_copy(
+            load.at[:, pl.ds(first, 2)], out.at[pl.ds(0, sizings)], sems.at[i]
+        )
+        for i, (out, first) in enumerate(((top, 0), (bottom, rows - 2)))
+    ]
+    for copy in copies:
+        copy.start()
+    meta = meta_rows(types, ids, many, cols)
+    blank = jnp.zeros((cols, nodes), F32)
+    top[sizings, 0] = meta
+    top[sizings, 1] = blank
+    bottom[sizings, 0] = pltpu.roll(meta, 2 * cols, 1)
+    bottom[sizings, 1] = blank
+    for copy in copies:
+        copy.wait()
+
+
+def sums_kernel(dims, ids_smem, types, ids, load, blocks, pay):
     sizings, rows, cols, nodes, count = dims
     many = rows * cols
     lanes = iota((sizings, max(count, 128)), 1)
@@ -62,17 +97,13 @@
             block = load[pl.ds(b, sizings, stride=many), :]
             blocks[pl.ds(pl.multiple_of(b * sizings, sizings), sizings), :] = block
             total = jnp.sum(block, axis=1, keepdims=True)
-            sums = sums + jnp.where(lanes == ids[b], total, 0.0)
+            sums = sums + jnp.where(lanes == ids_smem[r, c], total, 0.0)
         return sums
 
     sums = lax.fori_loop(0, rows, step, jnp.zeros(lanes.shape, F32))
-    edge = 2 * cols * sizings
-    top[...] = blocks[0:edge, :]
-    bottom[...] = blocks[many * sizings - edge : many * sizings, :]
     height = sizings * count // 128
-    packed = pack(sums, count)
-    spare = jnp.zeros((pay.shape[1] - height - 2, 128), F32)
-    whole = jnp.concatenate([packed, ids_row[...], types_row[...], spare], axis=0)
+    meta = meta_rows(types, ids, many, pay.shape[1] - height)
+    whole = jnp.concatenate([pack(sums, count), meta], axis=0)
 
     def copy(d, carry):
         pay[d] = whole
@@ -104,32 +135,93 @@
         row_sums[pl.ds(t, 1), :] = jnp.sum(block, axis=0, keepdims=True)
         return carry
 
-    lax.fori_loop(0, kinds, step, 0)
-
-
-def sides_kernel(dims, blocks, above, below, west, east):
+    lax.fori_loop(0, kinds, step, 0, unroll=True)
+
+
+def sides_kernel(dims, types, ids, blocks, above, below, west, east):
     sizings, rows, cols, nodes, count = dims
+    last = sizings * 2 * cols
+    own = meta_rows(types, ids, rows * cols, 8)
+    metas = [own, above[last : last + 8, :], below[last : last + 8, :]]
+    metas = jnp.concatenate(metas, axis=1).astype(BF16)
+    shape = (metas.shape[1], 128)
+    slot, lane = iota(shape, 0), iota(shape, 1)
     for out, first in ((west, 0), (east, cols - 2)):
         for side in range(2):
             c = first + side
             for k in range(rows + 2):
+                to = (k * 2 + side) * sizings
                 if k == 0:
-                    src, at = above, cols + c
+                    block = above[pl.ds(cols + c, sizings, stride=2 * cols), :]
                 elif k == rows + 1:
-                    src, at = below, c
+                    block = below[pl.ds(c, sizings, stride=2 * cols), :]
                 else:
-                    src, at = blocks, (k - 1) * cols + c
-                to = (k * 2 + side) * sizings
-                out[to : to + sizings, :] = src[at * sizings : (at + 1) * sizings, :]
-
-
-def sorted_products(order, kinds, pairs, source, stacked, low, sizings, store):
+                    at = ((k - 1) * cols + c) * sizings
+                    block = blocks[at : at + sizings, :]
+                out[to : to + sizings, :] = block
+        k = lane // 2
+        place = (k - 1) * cols
+        place = jnp.where(k == 0, rows * cols + cols, place)
+        place = jnp.where(k == rows + 1, 2 * rows * cols, place) + first + lane % 2
+        pick = (slot == place) & (k < rows + 2)
+        picked = jnp.dot(metas, pick.astype(F32).astype(BF16), preferred_element_type=F32)
+        out[(rows + 2) * 2 * sizings :, :] = picked
+
+
+def order_kernel(dims, kinds, lengths, maps, types, ids, above, below, west, east, plan, keys):
+    sizings, rows, cols, nodes, count = dims
+    many = rows * cols
+    own = meta_rows(types, ids, many, 8)
+    metas = jnp.concatenate([own, above[...], below[...], west[...], east[...]], axis=1)
+    shape = (metas.shape[1], maps.shape[1])
+    pick = (iota(shape, 0) == maps[0:1, :]).astype(F32).astype(BF16)
+    near = jnp.dot(metas.astype(BF16), pick, preferred_element_type=F32)
+    near_types, near_ids = near[0:1, :], near[1:2, :]
+    keys[...] = jnp.where(
+        near_ids > 0.0, near_ids - 1.0 + maps[3:4, :].astype(F32), -1.0
+    ).astype(jnp.int32)
+
+    length = maps.shape[1]
+    total = (rows + 4) * (cols + 4)
+    before = (iota((length, length), 0) < iota((length, length), 1)).astype(F32).astype(BF16)
+    upto = (iota((kinds, kinds), 0) >= iota((kinds, kinds), 1)).astype(F32).astype(BF16)
+    slot = iota((plan.shape[1], length), 0).astype(F32)
+    slot_row = iota((kinds, plan.shape[1]), 1).astype(F32)
+    side = iota((8, length), 0)
+    index = jnp.where(side == 0, iota((8, length), 1), jnp.where(side == 1, 1, 0))
+    index = index.astype(F32).astype(BF16)
+    orders, tile_kinds, groups = [], [], []
+    for which in (1, 2):
+        needed = maps[which : which + 1, :] > 0
+        hot = (iota((kinds, length), 0).astype(F32) == near_types) & needed
+        hot = hot.astype(F32)
+        rank = jnp.dot(hot.astype(BF16), before, preferred_element_type=F32)
+        tiles = jnp.floor((jnp.sum(hot, axis=1, keepdims=True) + (TILE - 1)) * (1.0 / TILE))
+        tiles = jnp.broadcast_to(tiles, (kinds, 128))
+        ends = jnp.dot(upto, tiles.astype(BF16), preferred_element_type=F32)
+        starts = (ends - tiles)[:, :1]
+        place = jnp.sum(hot * (starts * TILE + rank + 1.0), axis=0, keepdims=True) - 1.0
+        hit = (slot == place).astype(F32).astype(BF16)
+        found = lax.dot_general(
+            index, hit, (((1,), (1,)), ((), ())), preferred_element_type=F32
+        )
+        orders.append(found[0:1, :] + float(total) * (1.0 - found[1:2, :]))
+        kind = jnp.sum(jnp.where(slot_row >= ends[:, :1], 1.0, 0.0), axis=0, keepdims=True)
+        tile_kinds.append(jnp.minimum(kind, kinds - 1.0))
+        last = jnp.floor((ends[kinds - 1 : kinds, :1] + (GROUP - 1)) * (1.0 / GROUP))
+        groups.append(jnp.broadcast_to(last, (1, plan.shape[1])))
+    rest = jnp.zeros((2, plan.shape[1]), F32)
+    whole = jnp.concatenate(orders + tile_kinds + groups + [rest], axis=0)
+    plan[...] = whole.astype(jnp.int32)
+
+
+def sorted_products(plan, which, source, stacked, low, sizings, store):
     def step(it, carry):
         for one in range(GROUP):
             tile = it * GROUP + one
-            kind = kinds[tile]
+            kind = plan[2 + which, tile]
             places = [
-                pl.ds(pl.multiple_of(order[tile * TILE + j] * sizings, sizings), sizings)
+                pl.ds(pl.multiple_of(plan[which, tile * TILE + j] * sizings, sizings), sizings)
                 for j in range(TILE)
             ]
             field = jnp.concatenate([source[place, :] for place in places], axis=0)
@@ -141,7 +233,7 @@
             store(kind, places, out)
         return carry
 
-    lax.fori_loop(0, pairs, step, 0)
+    lax.fori_loop(0, plan[4 + which, 0], step, 0)
 
 
 def neighbour_ids(ids, cols):
@@ -158,25 +250,47 @@
     return south, north, east, west
 
 
-def invert_unrolled(matrix, count):
-    width = matrix.shape[1]
-    lane = iota((1, width), 1) % count
-    row = iota((count, 1), 0)
-    tile_lane = iota((count, 128), 1)
-    for k in range(count):
+def invert_unrolled(ref, count):
+    width = ref.shape[1]
+    fold = 128 // count
+    lane = iota((8, width), 1) % count
+    row = iota((8, width), 0)
+    tile_lane = iota((8, 128), 1)
+    many = count // 8
+    tiles = [ref[i * 8 : (i + 1) * 8, :] for i in range(many)]
+
+    def column(tile, k):
         parts = []
         for base in range(0, width, 128):
-            part = jnp.broadcast_to(matrix[:, base + k : base + k + 1], (count, 128))
-            for j in range(1, 128 // count):
+            part = jnp.broadcast_to(tile[:, base + k : base + k + 1], (8, 128))
+            for j in range(1, fold):
                 at = base + j * count + k
-                part = jnp.where(tile_lane >= j * count, matrix[:, at : at + 1], part)
+                part = jnp.where(tile_lane >= j * count, tile[:, at : at + 1], part)
             parts.append(part)
-        column = jnp.concatenate(parts, axis=1)
-        inverse = 1.0 / column[k : k + 1, :]
-        scaled = jnp.where(lane == k, 1.0, matrix[k : k + 1, :]) * inverse
-        column = jnp.where(row == k, -1.0, column)
-        matrix = jnp.where((lane == k) | (row == k), 0.0, matrix) - column * scaled
-    return matrix
+        return jnp.concatenate(parts, axis=1)
+
+    for first in range(0, count, PANEL):
+        columns = [[column(t, first + j) for t in tiles] for j in range(PANEL)]
+        for j in range(PANEL):
+            k = first + j
+            at, within = k // 8, k % 8
+            here = columns[j]
+            inverse = 1.0 / here[at][within : within + 1, :]
+            scaled = jnp.where(
+                lane[:1] == k, inverse, tiles[at][within : within + 1, :] * inverse
+            )
+            pivot = row == within
+            for i in range(many):
+                new = jnp.where(lane == k, 0.0, tiles[i]) - here[i] * scaled
+                tiles[i] = jnp.where(pivot, scaled, new) if i == at else new
+            for later in range(j + 1, PANEL):
+                other = columns[later]
+                factor = other[at][within : within + 1, :] * inverse
+                for i in range(many):
+                    new = other[i] - here[i] * factor
+                    other[i] = jnp.where(pivot, factor, new) if i == at else new
+    for i in range(many):
+        ref[i * 8 : (i + 1) * 8, :] = tiles[i]
 
 
 def invert_looped(ref, count):
@@ -197,7 +311,7 @@
     lax.fori_loop(0, count, step, 0)
 
 
-def coarse_matrices(dims, mesh_dims, gathered, row_sums, strap, inverses, cross, nearby):
+def coarse_matrices(dims, mesh_dims, gathered, row_sums, strap, inverses, cross):
     sizings, rows, cols, nodes, count = dims
     n_row, n_col = mesh_dims
     many = rows * cols
@@ -205,52 +319,51 @@
     kinds = row_sums.shape[0]
     north_weight = jnp.sum(strap[0:1, :], axis=1, keepdims=True)
     east_weight = jnp.sum(strap[1:2, :], axis=1, keepdims=True)
-    block_sums = jnp.sum(row_sums[...], axis=1, keepdims=True)
-    names = iota((count, many), 0).astype(F32)
+    names = iota((count, many), 0).astype(F32).astype(BF16)
+    kind_names = iota((16, many), 0).astype(F32).astype(BF16)
     lane = iota((n_row, many), 1)
+    eye = iota((count, count), 0) == iota((count, count), 1)
+    contract = (((1,), (1,)), ((), ()))
+    spot = iota((kinds, 16), 0) == iota((kinds, 16), 1)
+    centre = jnp.sum(row_sums[...], axis=1, keepdims=True) + 2.0 * north_weight
+    centre = centre + 2.0 * east_weight
+    centre = jnp.sum(jnp.where(spot, centre, 0.0), axis=0, keepdims=True)
 
     def rows_of(g, at):
         return jnp.concatenate(
             [gathered[i * n_col + g, at : at + 1, :] for i in range(n_row)], axis=0
         )
 
-    all_ids = [rows_of(g, height) for g in range(n_col)]
-    eye = iota((count, count), 0) == iota((count, count), 1)
-    contract = (((1,), (1,)), ((), ()))
+    def hot(values, labels):
+        rows_bf = values.astype(BF16)
+        one, zero = jnp.ones(labels.shape, BF16), jnp.zeros(labels.shape, BF16)
+        return [
+            jnp.where(labels == rows_bf[i : i + 1, :], one, zero) for i in range(n_row)
+        ]
+
+    all_ids = [rows_of(g, height + 1) - 1.0 for g in range(n_col)]
     for g in range(n_col):
         ids = all_ids[g]
-        types = rows_of(g, height + 1)
-        centre = jnp.zeros(ids.shape, F32) + 2.0 * north_weight + 2.0 * east_weight
-        for t in range(kinds):
-            centre = centre + jnp.where(types == float(t), block_sums[t : t + 1, :], 0.0)
         beyond = all_ids[min(g + 1, n_col - 1)]
         beyond = jnp.where(lane % cols == cols - 1, pltpu.roll(beyond, cols - 1, 1), -1.0)
-        for slot, value in enumerate((ids, *neighbour_ids(ids, cols), beyond, centre)):
-            nearby[slot] = value
-
-        def step(i, carry):
-            pairs, crossed, diagonal = carry
-            hot = [names == nearby[slot, pl.ds(i, 1), :] for slot in range(6)]
-            soft = [h.astype(F32).astype(BF16) for h in hot]
-            around = jnp.concatenate([soft[1] + soft[2], soft[3] + soft[4], soft[5]], axis=0)
-            pairs = pairs + lax.dot_general(
-                soft[0], around, contract, preferred_element_type=F32
-            )
-            diagonal = diagonal + jnp.where(hot[0], nearby[6, pl.ds(i, 1), :], 0.0)
-            return pairs, crossed, diagonal
-
-        start = (
-            jnp.zeros((count, 3 * count), F32),
-            0,
-            jnp.zeros((count, many), F32),
-        )
-        pairs, _, diagonal = lax.fori_loop(0, n_row, step, start, unroll=n_row <= 8)
-        diagonal = jnp.sum(diagonal, axis=1, keepdims=True)
-        matrix = jnp.where(eye, diagonal, 0.0) - (
+        south, north, east, west = [hot(v, names) for v in neighbour_ids(ids, cols)]
+        own, over = hot(ids, names), hot(beyond, names)
+        types = hot(rows_of(g, height), kind_names)
+        right = jnp.concatenate(
+            [
+                jnp.concatenate([south[i] + north[i], east[i] + west[i], over[i], types[i]], axis=0)
+                for i in range(n_row)
+            ],
+            axis=1,
+        )
+        pairs = lax.dot_general(
+            jnp.concatenate(own, axis=1), right, contract, preferred_element_type=F32
+        )
+        diagonal = jnp.sum(pairs[:, 3 * count :] * centre, axis=1, keepdims=True)
+        inverses[:, g * count : (g + 1) * count] = jnp.where(eye, diagonal, 0.0) - (
             north_weight * pairs[:, :count] + east_weight * pairs[:, count : 2 * count]
         )
-        inverses[:, g * count : (g + 1) * count] = matrix
-        cross[g] = pairs[:, 2 * count :]
+        cross[g] = pairs[:, 2 * count : 3 * count]
 
 
 def coarse_solve(gathered, first, height, mesh_dims, count, sizings, inverses, g):
@@ -282,10 +395,10 @@
 
 def middle_kernel(
     dims, mesh_dims,
-    order_1, kinds_1, order_2, kinds_2, info, ids,
+    plan, info, ids,
     gathered, keys, blocks, above, below, west, east, stacked, low, row_sums, strap,
     z_out, q_out, u_out, au_out, inverses, cross, pay,
-    field, level, z, bz, q, u, bu, solved, nearby,
+    field, level, z, bz, q, u, bu, solved,
 ):
     sizings, rows, cols, nodes, count = dims
     n_row, n_col = mesh_dims
@@ -301,10 +414,12 @@
         to = ((r + 2) * wide + 2) * sizings
         field[to : to + span, :] = blocks[r * span : (r + 1) * span, :]
     for r in range(2):
-        to = (r * wide + 2) * sizings
-        field[to : to + span, :] = above[r * span : (r + 1) * span, :]
-        to = ((rows + 2 + r) * wide + 2) * sizings
-        field[to : to + span, :] = below[r * span : (r + 1) * span, :]
+        for c in range(cols):
+            from_edge = pl.ds(r * cols + c, sizings, stride=2 * cols)
+            to = (r * wide + 2 + c) * sizings
+            field[to : to + sizings, :] = above[from_edge, :]
+            to = ((rows + 2 + r) * wide + 2 + c) * sizings
+            field[to : to + sizings, :] = below[from_edge, :]
     for k in range(rows + 2):
         pair = 2 * sizings
         to = (k + 1) * wide * sizings
@@ -315,9 +430,9 @@
     level[many * sizings :, :] = jnp.zeros((sizings, nodes), F32)
     q[many * sizings :, :] = jnp.zeros((sizings, nodes), F32)
 
-    coarse_matrices(dims, mesh_dims, gathered, row_sums, strap, inverses, cross, nearby)
+    coarse_matrices(dims, mesh_dims, gathered, row_sums, strap, inverses, cross)
     if count <= 64:
-        inverses[...] = invert_unrolled(inverses[...], count)
+        invert_unrolled(inverses, count)
     else:
         invert_looped(inverses, count)
     solved[0] = jnp.zeros((sizings, count), F32)
@@ -326,7 +441,7 @@
         _, solved[g + 1] = coarse_solve(
             gathered, 0, height, mesh_dims, count, sizings, inverses, g
         )
-    spread(solved, info[2], keys, level, count, sizings, nodes, many)
+    spread(solved, info[0], keys, level, count, sizings, nodes, many)
 
     def store_z(kind, places, out):
         sums = row_sums[pl.ds(kind, 1), :]
@@ -335,7 +450,7 @@
             z[place, :] = out[j * sizings : (j + 1) * sizings, :nodes] + here
             bz[place, :] = out[j * sizings : (j + 1) * sizings, nodes:] + sums * here
 
-    sorted_products(order_1, kinds_1, info[0], field, stacked, low, sizings, store_z)
+    sorted_products(plan, 0, field, stacked, low, sizings, store_z)
 
     north, east_strap = strap[0:1, :], strap[1:2, :]
     couple = 2.0 * north + 2.0 * east_strap
@@ -350,7 +465,7 @@
         )
         return here, image
 
-    for er, flag in ((1, info[3]), (rows + 2, info[4])):
+    for er, flag in ((1, info[1]), (rows + 2, info[2])):
         inside = flag.astype(F32)
 
         def across(ec, carry):
@@ -358,7 +473,7 @@
             return carry
 
         lax.fori_loop(2, cols + 2, across, 0)
-    for ec, flag in ((1, info[5]), (cols + 2, info[6])):
+    for ec, flag in ((1, info[3]), (cols + 2, info[4])):
         inside = flag.astype(F32)
 
         def along(er, carry):
@@ -383,7 +498,7 @@
             rz = rz + blocks[own, :] * here
             zq = zq + here * image
             total = jnp.sum(image, axis=1, keepdims=True)
-            sums = sums + jnp.where(lanes == ids[b], total, 0.0)
+            sums = sums + jnp.where(lanes == ids[r, c], total, 0.0)
         return rz, zq, sums
 
     rz, zq, sums_q = lax.fori_loop(0, rows, first_row, (blank, blank, zero_sums))
@@ -393,7 +508,7 @@
             u[place, :] = out[j * sizings : (j + 1) * sizings, :nodes]
             bu[place, :] = out[j * sizings : (j + 1) * sizings, nodes:]
 
-    sorted_products(order_2, kinds_2, info[1], q, stacked, low, sizings, store_u)
+    sorted_products(plan, 1, q, stacked, low, sizings, store_u)
 
     def second_row(r, carry):
         qu, uau, sums = carry
@@ -406,7 +521,7 @@
             qu = qu + q[at(r + 2, c + 2), :] * here
             uau = uau + here * image
             total = jnp.sum(image, axis=1, keepdims=True)
-            sums = sums + jnp.where(lanes == ids[b], total, 0.0)
+            sums = sums + jnp.where(lanes == ids[r, c], total, 0.0)
         return qu, uau, sums
 
     qu, uau, sums_u = lax.fori_loop(0, rows, second_row, (blank, blank, zero_sums))
@@ -459,7 +574,7 @@
                 before, cross[g - 1], precision=HIGHEST, preferred_element_type=F32
             )
         before = one
-    spread(solved, info[2], keys, level, count, sizings, nodes, many)
+    spread(solved, info[0], keys, level, count, sizings, nodes, many)
 
     dots = gathered[0, 2 * height : 2 * height + 1, :]
     for d in range(1, n_row * n_col):
@@ -494,7 +609,7 @@
 
             here = value(0, 0)
             lift = (
-                (row_sums[pl.ds(types[b], 1), :] + couple) * here
+                (row_sums[pl.ds(types[r, c], 1), :] + couple) * here
                 - north * (value(-1, 0) + value(1, 0))
                 - east_strap * (value(0, -1) + value(0, 1))
             )
@@ -509,41 +624,41 @@
     lax.fori_loop(0, rows, step, 0)
 
 
-def tile_plan(types, needed, kinds, many):
-    n = sum(needed)
-    most = (n + (TILE - 1) * kinds) // TILE
-    most = -(-most // GROUP) * GROUP
-    flat = jnp.where(jnp.array(needed), types.reshape(-1), kinds)
-    hot = (flat[None, :] == jnp.arange(kinds)[:, None]).astype(jnp.int32)
-    index = jnp.arange(many)
-    rank = jnp.dot(
-        hot.astype(BF16), (index[:, None] < index[None, :]).astype(BF16),
-        preferred_element_type=F32,
-    ).astype(jnp.int32)
-    tiles = (jnp.sum(hot, axis=1) + TILE - 1) // TILE
-    below = jnp.arange(kinds)[:, None] >= jnp.arange(kinds)[None, :]
-    ends = jnp.sum(jnp.where(below, tiles[None, :], 0), axis=1)
-    starts = ends - tiles
-    place = jnp.sum(hot * (starts[:, None] * TILE + rank + 1), axis=0) - 1
-    slots = jnp.arange(most * TILE)
-    order = many + jnp.sum(
-        jnp.where(place[None, :] == slots[:, None], index[None, :] - many, 0), axis=1
-    )
-    tile_kinds = jnp.sum(jnp.arange(most)[:, None] >= ends[None, :], axis=1)
-    tile_kinds = jnp.minimum(tile_kinds, kinds - 1)
-    groups = (ends[-1] + GROUP - 1) // GROUP
-    return order.astype(jnp.int32), tile_kinds.astype(jnp.int32), groups.astype(jnp.int32)
-
-
-def call(kernel, in_specs, out_shape, scratch, cost):
+def ring_maps(rows, cols, count):
+    tall, wide = rows + 4, cols + 4
+    many = rows * cols
+    length = -(-tall * wide // 128) * 128
+    maps = np.zeros((8, length), np.int32)
+    maps[0] = -1
+    for er in range(tall):
+        for ec in range(wide):
+            e = er * wide + ec
+            down = max(2 - er, er - (rows + 1), 0)
+            over = max(2 - ec, ec - (cols + 1), 0)
+            maps[1, e] = down + over <= 2
+            maps[2, e] = down + over <= 1
+            maps[3, e] = count * ((ec >= 2) + (ec >= cols + 2))
+            if not down and not over:
+                maps[0, e] = (er - 2) * cols + ec - 2
+            elif not over:
+                south = er > 1
+                maps[0, e] = (1 + south) * many + (er - (rows + 2 if south else 0)) * cols + ec - 2
+            elif down <= 1:
+                right = ec > 1
+                maps[0, e] = (3 + right) * many + (er - 1) * 2 + ec - (cols + 2 if right else 0)
+    return maps
+
+
+def call(kernel, in_specs, out_shape, scratch, cost, megabytes, **more):
     return pl.pallas_call(
         kernel,
         in_specs=in_specs,
         out_specs=jax.tree.map(lambda _: VMEM, out_shape),
         out_shape=out_shape,
         scratch_shapes=scratch,
-        compiler_params=PARAMS,
+        compiler_params=pltpu.CompilerParams(vmem_limit_bytes=megabytes * 1024 * 1024),
         cost_estimate=pl.CostEstimate(flops=cost, bytes_accessed=4_000_000, transcendentals=0),
+        **more,
     )
 
 
@@ -556,31 +671,34 @@
     count = rows * n_row // AGR * (cols // AGC)
     dims, mesh_dims = (sizings, rows, cols, nodes, count), (n_row, n_col)
     block_rows = rows * cols * sizings
-    wide, tall = cols + 4, rows + 4
-    many = wide * tall
+    many = (rows + 4) * (cols + 4)
     height = sizings * count // 128
     shape = jax.ShapeDtypeStruct
-
-    edge = shape((2 * cols * sizings, nodes), F32)
     own = shape((block_rows, nodes), F32)
-    ids = aggregate_map.reshape(-1)
-    types = block_types.reshape(-1)
+
+    edge = shape((sizings + 1, 2, cols, nodes), F32)
+    top, bottom = call(
+        functools.partial(edges_kernel, dims),
+        [pl.BlockSpec(memory_space=pl.ANY), VMEM, VMEM],
+        [edge, edge],
+        [pltpu.SemaphoreType.DMA((2,))],
+        1_000_000,
+        8,
+    )(load_currents, block_types, aggregate_map)
+    forth = [(i, i + 1) for i in range(n_row - 1)]
+    edge_rows = (sizings + 1) * 2 * cols
+    above = lax.ppermute(bottom.reshape(edge_rows, nodes), "row", forth)
+    below = lax.ppermute(top.reshape(edge_rows, nodes), "row", [(j, i) for i, j in forth])
+
     pay_rows = -(-(height + 2) // 8) * 8
-    blocks, top, bottom, pay = call(
+    blocks, pay = call(
         functools.partial(sums_kernel, dims),
         [SMEM] + [VMEM] * 3,
-        [own, edge, edge, shape((n_dev, pay_rows, 128), F32)],
+        [own, shape((n_dev, pay_rows, 128), F32)],
         [],
         1_000_000,
-    )(
-        ids,
-        ids.reshape(1, -1).astype(F32),
-        types.reshape(1, -1).astype(F32),
-        load_currents.reshape(-1, nodes),
-    )
-    forth = [(i, i + 1) for i in range(n_row - 1)]
-    above = lax.ppermute(bottom, "row", forth)
-    below = lax.ppermute(top, "row", [(j, i) for i, j in forth])
+        16,
+    )(aggregate_map, block_types, aggregate_map, load_currents.reshape(-1, nodes))
     gathered = lax.all_to_all(pay, ("row", "col"), 0, 0)
     stacked, low, row_sums = call(
         weights_kernel,
@@ -592,41 +710,33 @@
         ],
         [],
         1_000_000_000,
+        16,
     )(block_library, strap_conductance)
-    side = shape(((rows + 2) * 2 * sizings, nodes), F32)
+    side_rows = (rows + 2) * 2 * sizings
+    side = shape((side_rows + 8, nodes), F32)
     to_west, to_east = call(
-        functools.partial(sides_kernel, dims), [VMEM] * 3, [side, side], [], 1_000_000
-    )(blocks, above, below)
+        functools.partial(sides_kernel, dims), [VMEM] * 5, [side, side], [], 1_000_000, 16
+    )(block_types, aggregate_map, blocks, above, below)
     forth = [(i, i + 1) for i in range(n_col - 1)]
     west = lax.ppermute(to_east, "col", forth)
     east = lax.ppermute(to_west, "col", [(j, i) for i, j in forth])
 
-    def die(at):
-        whole = gathered[:, at, :].astype(jnp.int32).reshape(n_row, n_col, rows, cols)
-        whole = whole.transpose(0, 2, 1, 3).reshape(n_row * rows, n_col * cols)
-        whole = jnp.pad(whole, 2, constant_values=-1)
-        return lax.dynamic_slice(whole, (row * rows, col * cols), (tall, wide))
-
-    place = jnp.arange(wide)
-    relative = (place >= 2).astype(jnp.int32) + (place >= cols + 2).astype(jnp.int32)
-    near_ids, near_types = die(height), jnp.maximum(die(height + 1), 0)
-    keys = jnp.where(near_ids >= 0, near_ids + relative[None, :] * count, -1).reshape(1, -1)
-    keys = jnp.pad(keys, ((0, 0), (0, -many % 128)), constant_values=-1)
-
-    def ring(er, ec):
-        down = max(2 - er, er - (rows + 1), 0)
-        over = max(2 - ec, ec - (cols + 1), 0)
-        return down, over
-
-    rings = [ring(er, ec) for er in range(tall) for ec in range(wide)]
-    needed_1 = [down + over <= 2 for down, over in rings]
-    needed_2 = [down + over <= 1 for down, over in rings]
-    order_1, kinds_1, groups_1 = tile_plan(near_types, needed_1, kinds, many)
-    order_2, kinds_2, groups_2 = tile_plan(near_types, needed_2, kinds, many)
+    maps = ring_maps(rows, cols, count)
+    longest = int(max(maps[1].sum(), maps[2].sum())) + (TILE - 1) * kinds + GROUP * TILE
+    longest = -(-longest // 128) * 128
+    edge_meta = pl.BlockSpec((8, 128), lambda i: (sizings * 2 * cols // 8, 0))
+    side_meta = pl.BlockSpec((8, 128), lambda i: (side_rows // 8, 0))
+    plan, keys = call(
+        functools.partial(order_kernel, dims, kinds, longest),
+        [VMEM] * 3 + [edge_meta, edge_meta, side_meta, side_meta],
+        [shape((8, longest), jnp.int32), shape((1, maps.shape[1]), jnp.int32)],
+        [],
+        1_000_000,
+        16,
+        grid=(1,),
+    )(jnp.asarray(maps), block_types, aggregate_map, above, below, west, east)
     info = jnp.stack(
         [
-            groups_1,
-            groups_2,
             col,
             (row > 0).astype(jnp.int32),
             (row < n_row - 1).astype(jnp.int32),
@@ -638,17 +748,18 @@
     coarse = pltpu.VMEM((n_col + 2, sizings, count), F32)
     z, q, u, au, inverses, cross, pay = call(
         functools.partial(middle_kernel, dims, mesh_dims),
-        [SMEM] * 6 + [VMEM] * 11,
+        [SMEM] * 3 + [VMEM] * 11,
         [own] * 4
         + [
             shape((count, n_col * count), F32),
             shape((n_col, count, count), F32),
             shape((n_dev, 2 * height + 1, 128), F32),
         ],
-        [big] * 7 + [coarse, pltpu.VMEM((7, n_row, rows * cols), F32)],
+        [big] * 7 + [coarse],
         1_000_000_000,
+        32 if count <= 64 else 56,
     )(
-        order_1, kinds_1, order_2, kinds_2, info, ids,
+        plan, info, aggregate_map,
         gathered, keys, blocks, above, below, west, east, stacked, low, row_sums,
         strap_conductance,
     )
@@ -660,8 +771,9 @@
         [out, out],
         [big, coarse],
         1_000_000_000,
+        16 if count <= 64 else 32,
     )(
-        types, info,
+        block_types, info,
         gathered, keys, inverses, cross, z, q, u, au, blocks, row_sums, strap_conductance,
     )
     return voltage.reshape(load_currents.shape), residual.reshape(load_currents.shape)

time: 103 us -> 85.3 us (0.83)
  blocking collectives: 0 us -> 21 us
  Pallas kernels: 45.2 us -> 28.8 us
  starting transfers between devices: 24.5 us -> 16.1 us
  waiting for transfers between devices: 17.6 us -> 11.9 us
  other arithmetic: 3.51 us -> 0 us
  local copies, waits for them, and re-layouts: 9.55 us -> 6.14 us
  between operations: 2.1 us -> 0.79 us
    all_to_all x0 -> x1, blocking collectives: none -> 21 us  [on_device(): gathered = lax.all_to_all(pay, ('row', 'col'), 0, 0)]
    all_to_all x2 -> x1, waiting for transfers between devices: 12.6 us -> 0.01 us  [on_device(): gathered = lax.all_to_all(pay, ('row', 'col'), 0, 0)]
    all_to_all x2 -> x1, starting transfers between devices: 16.7 us -> 7.3 us  [on_device(): gathered = lax.all_to_all(pay, ('row', 'col'), 0, 0)]
    pallas_call x3 -> x5, Pallas kernels: 31.4 us -> 22 us  [the longest x1 17 us: on_device(): call(functools.partial(middle_kernel, dims, mesh_dims), [SMEM] * 3 + [VME...]
    ppermute x2, waiting for transfers between devices: 4.99 us -> 11.9 us  [the longest x1 6.55 us: on_device(): lax.ppermute(top.reshape(edge_rows, nodes), 'row', [(j, i) for i, j in fo...]
    pallas_call x1, Pallas kernels: 6.42 us -> 1.4 us  [on_device(): call(weights_kernel, [VMEM, VMEM], [shape((kinds, 2 * nodes, 2 * nodes),...]
    unnamed x24 -> x22, local copies, waits for them, and re-layouts: 3.19 us -> 6.06 us
    reshape x5 -> x0, local copies, waits for them, and re-layouts: 2.24 us -> none  [the longest x1 1.31 us: on_device(): ids = aggregate_map.reshape(-1)]
  transfers between devices with their start and end apart: 6 -> 5, of which waited for: 2 -> 2; matrix products, arithmetic and copies ran while one was open for 7% -> 0% of each run, Pallas kernels for 8% -> 4%
where the time goes in v2:
time: 85.3 us; the launch traced here: 84.8 us
  Pallas kernels  28.8 us (34%)
  blocking collectives  21 us (25%)
  starting transfers between devices  16.1 us (19%)
  waiting for transfers between devices  11.9 us (14%)
  local copies, waits for them, and re-layouts  6.14 us (7%)
    all_to_all x1, blocking collectives, on_device(): gathered = lax.all_to_all(pay, ('row', 'col'), 0, 0)  21 us
    pallas_call x1, Pallas kernels, on_device(): call(functools.partial(middle_kernel, dims, mesh_dims), [SMEM] * 3 + [VME...  17 us
    all_to_all x1, starting transfers between devices, on_device(): gathered = lax.all_to_all(pay, ('row', 'col'), 0, 0)  7.3 us
    ppermute x1, waiting for transfers between devices, on_device(): lax.ppermute(top.reshape(edge_rows, nodes), 'row', [(j, i) for i, j in fo...  6.55 us
    unnamed x22, local copies, waits for them, and re-layouts  6.06 us
    ppermute x1, waiting for transfers between devices, on_device(): above = lax.ppermute(bottom.reshape(edge_rows, nodes), 'row', forth)  5.38 us
    pallas_call x1, Pallas kernels, on_device(): call(functools.partial(last_kernel, dims, mesh_dims), [SMEM] * 2 + [VMEM]...  5.35 us
    ppermute x1, starting transfers between devices, on_device(): above = lax.ppermute(bottom.reshape(edge_rows, nodes), 'row', forth)  4.56 us
  transfers between devices with their start and end apart: 5, of which 2 were waited for; matrix products, arithmetic and copies ran while one was open for 0% of the time, Pallas kernels for 4%

profile of v2, /device:TPU:0, one launch (start us, length us, event | category | flops | bytes accessed | tf_op | source)
XLA Modules:
  0.0 84.8 jit_solution(8763728298381185669)
XLA Ops:
  0.6 0.0 copy-start
  0.6 1.2 %copy-done = f32[16,8,16,128]{3,2,1,0:T(8,128)S(1)} copy-done((f32[16,8,16,128]{3,2,1,0:T(8,128)S(1)}, f32[16,8,16,128]{3,2,1,0:T(8,128)}, u32[]{:S(2)}) %copy-start) | copy-done | bytes 1048600
  1.9 0.0 copy-start.4
  1.9 0.7 copy-done.4
  2.5 0.0 copy-start.6
  2.5 0.7 copy-done.6
  3.2 0.0 copy-start.1
  3.2 2.8 %shard_map.78 = (f32[2048,128]{1,0:T(8,128)S(1)}, f32[32,16,128]{2,1,0:T(8,128)}) custom-call(s32[8,16]{1,0:T(8,128)S(1)} %copy-done.4, s32[8,16]{1,0:T(8,128)S(1)} %copy-done.6, s32[8,16]{1,0:T(8,128)S(1)} %copy-done.4, f32[2048,128]{1,0:T(8,128)S(1)} %bitcast.10), custom_call_target="tpu_custom_call" | custom-call | flops 1000000 | bytes 4000000 | tf_op jit(solution)/shard_map/pallas_call | solution.py:694
  6.0 0.0 copy-start.5
  6.0 0.0 copy-start.7
  6.0 7.3 %all-to-all-start = ((f32[32,16,128]{2,1,0:T(8,128)}), f32[32,16,128]{2,1,0:T(8,128)S(1)}, u32[]{:S(2)}, u32[]{:S(2)}) async-start(f32[32,16,128]{2,1,0:T(8,128)} %get-tuple-element.28), calls=%async_computation | async-start | bytes 524288 | tf_op jit(solution)/shard_map/all_to_all | solution.py:702
  13.3 0.0 copy-done.1
  13.3 0.0 copy-done.5
  13.4 0.0 copy-done.7
  13.4 0.3 shard_map.77
  13.6 1.3 %collective-permute-start.1 = (f32[544,128]{1,0:T(8,128)S(1)}, f32[544,128]{1,0:T(8,128)S(1)}, u32[]{:S(2)}, u32[]{:S(2)}) collective-permute-start(f32[544,128]{1,0:T(8,128)S(1)} %bitcast.12), channel_id=1, source_target_pairs={{4,0},{8,4},{12,8},{16,12},{20,16},{24,20},{28,24},{5,1},{9,5},{13... | collective-permute-start | bytes 835592 | tf_op jit(solution)/shard_map/ppermute | solution.py:691
  14.9 4.6 %collective-permute-start = (f32[544,128]{1,0:T(8,128)S(1)}, f32[544,128]{1,0:T(8,128)S(1)}, u32[]{:S(2)}, u32[]{:S(2)}) collective-permute-start(f32[544,128]{1,0:T(8,128)S(1)} %bitcast.11), channel_id=1, source_target_pairs={{0,4},{4,8},{8,12},{12,16},{16,20},{20,24},{24,28},{1,5},{5,9},{9,... | collective-permute-start | bytes 835592 | tf_op jit(solution)/shard_map/ppermute | solution.py:690
  19.5 6.6 %collective-permute-done.1.below = f32[544,128]{1,0:T(8,128)S(1)} collective-permute-done((f32[544,128]{1,0:T(8,128)S(1)}, f32[544,128]{1,0:T(8,128)S(1)}, u32[]{:S(2)}, u32[]{:S(2)}) %collective-permute-start.1) | collective-permute-done | bytes 278560 | tf_op jit(solution)/shard_map/ppermute | solution.py:691
  26.1 5.4 %collective-permute-done.above = f32[544,128]{1,0:T(8,128)S(1)} collective-permute-done((f32[544,128]{1,0:T(8,128)S(1)}, f32[544,128]{1,0:T(8,128)S(1)}, u32[]{:S(2)}, u32[]{:S(2)}) %collective-permute-start) | collective-permute-done | bytes 278560 | tf_op jit(solution)/shard_map/ppermute | solution.py:690
  31.4 0.9 %shard_map.79 = (f32[328,128]{1,0:T(8,128)S(1)}, f32[328,128]{1,0:T(8,128)}) custom-call(s32[8,16]{1,0:T(8,128)S(1)} %copy-done.7, s32[8,16]{1,0:T(8,128)S(1)} %copy-done.5, f32[2048,128]{1,0:T(8,128)S(1)} %get-tuple-element.24.blocks, f32[544,128]{1,0:T(8,128)S(1)} %collective-permute-done.above, f32[544,128]{1,0:T(8,128)S(1)} %collective-permute-done.1.below), custom_call_target="tpu_custom_call" | custom-call | flops 1000000 | bytes 4000000 | tf_op jit(solution)/shard_map/pallas_call | solution.py:717
  32.4 1.7 %collective-permute-start.2 = (f32[328,128]{1,0:T(8,128)}, f32[328,128]{1,0:T(8,128)S(1)}, u32[]{:S(2)}, u32[]{:S(2)}) collective-permute-start(f32[328,128]{1,0:T(8,128)} %get-tuple-element.25), channel_id=1, source_target_pairs={{0,1},{1,2},{2,3},{4,5},{5,6},{6,7},{8,9},{9,10},{10,11},{12,13},{... | collective-permute-start | bytes 503816 | tf_op jit(solution)/shard_map/ppermute | solution.py:721
  34.1 1.3 %collective-permute-start.3 = (f32[328,128]{1,0:T(8,128)S(1)}, f32[328,128]{1,0:T(8,128)S(1)}, u32[]{:S(2)}, u32[]{:S(2)}) collective-permute-start(f32[328,128]{1,0:T(8,128)S(1)} %get-tuple-element.26), channel_id=1, source_target_pairs={{1,0},{2,1},{3,2},{5,4},{6,5},{7,6},{9,8},{10,9},{11,10},{13,12},{... | collective-permute-start | bytes 503816 | tf_op jit(solution)/shard_map/ppermute | solution.py:722
  35.4 0.0 copy-start.9
  35.4 0.1 stack.39.info
  35.5 0.6 copy-done.9
  36.1 0.0 copy-start.10
  36.1 1.0 %copy-done.10 = f32[8,128,128]{2,1,0:T(8,128)S(1)} copy-done((f32[8,128,128]{2,1,0:T(8,128)S(1)}, f32[8,128,128]{2,1,0:T(8,128)}, u32[]{:S(2)}) %copy-start.10) | copy-done | bytes 524312
  37.1 0.0 copy-start.8
  37.1 1.4 %shard_map.81 = (bf16[8,256,256]{2,1,0:T(8,128)(2,1)S(1)}, bf16[8,128,256]{2,1,0:T(8,128)(2,1)S(1)}, f32[8,128]{1,0:T(8,128)S(1)}) custom-call(f32[8,128,128]{2,1,0:T(8,128)S(1)} %copy-done.10, f32[2,128]{1,0:T(2,128)S(1)} %copy-done.9), custom_call_target="tpu_custom_call" | custom-call | flops 1000000000 | bytes 4000000 | tf_op jit(solution)/shard_map/pallas_call | solution.py:703
  38.5 0.0 copy-start.2
  38.5 0.8 copy-done.2
  39.3 0.0 collective-permute-done.2.west
  39.3 0.0 collective-permute-done.3.east
  39.3 0.0 copy-done.8
  39.3 1.1 %shard_map.80 = (s32[8,384]{1,0:T(8,128)S(1)}, s32[1,256]{1,0:T(1,128)S(1)}) custom-call(s32[8,256]{1,0:T(8,128)S(1)} %copy-done.8, s32[8,16]{1,0:T(8,128)S(1)} %copy-done.7, s32[8,16]{1,0:T(8,128)S(1)} %copy-done.5, f32[544,128]{1,0:T(8,128)S(1)} %collective-permute-done.above, f32[544,128]{1,0:T(8,128)S(1)} %collective-permute-done.1.below, ...), custom_call_target="tpu_custom_call" | custom-call | flops 1000000 | bytes 4000000 | tf_op jit(solution)/shard_map/pallas_call | solution.py:729
  40.4 0.0 all-to-all-done.gathered
  40.4 0.0 copy-start.3
  40.4 1.0 %copy-done.3 = bf16[8,128,256]{2,1,0:T(8,128)(2,1)S(1)} copy-done((bf16[8,128,256]{2,1,0:T(8,128)(2,1)S(1)}, bf16[8,128,256]{2,1,0:T(8,128)(2,1)}, u32[]{:S(2)}) %copy-start.3) | copy-done | bytes 524312
  41.5 17.0 %shard_map.82 = (f32[2048,128]{1,0:T(8,128)S(1)}, f32[2048,128]{1,0:T(8,128)S(1)}, f32[2048,128]{1,0:T(8,128)S(1)}, f32[2048,128]{1,0:T(8,128)S(1)}, f32[64,256]...) custom-call(s32[8,384]{1,0:T(8,128)S(1)} %get-tuple-element.27.plan, s32[5]{0:T(128)S(1)} %stack.39.info, ...), custom_call_target="tpu_custom_call" | custom-call | flops 1000000000 | bytes 4000000 | tf_op jit(solution)/shard_map/pallas_call | solution.py:749
  58.4 21.0 %all_to_all.10.gathered = f32[32,17,128]{2,1,0:T(8,128)S(1)} all-to-all(f32[32,17,128]{2,1,0:T(8,128)S(1)} %get-tuple-element.33), channel_id=1, replica_groups=mesh['row'=8,'col'=4] {'row','col'}, dimensions={0} | all-to-all | bytes 557056 | tf_op jit(solution)/shard_map/all_to_all | solution.py:766
  79.4 5.3 %shard_map.83 = (f32[2048,128]{1,0:T(8,128)}, f32[2048,128]{1,0:T(8,128)}) custom-call(s32[8,16]{1,0:T(8,128)S(1)} %copy-done.7, s32[5]{0:T(128)S(1)} %stack.39.info, f32[32,17,128]{2,1,0:T(8,128)S(1)} %all_to_all.10.gathered, s32[1,256]{1,0:T(1,128)S(1)} %get-tuple-element.29.keys, f32[64,256]{1,0:T(8,128)S(1)} %get-tuple-element.34.inverses, ...), custom_call_target="tpu_custom_call" | custom-call | flops 1000000000 | bytes 4000000 | tf_op jit(solution)/shard_map/pallas_call | solution.py:768
Async XLA Ops:
  0.6 1.2 %copy-start = (f32[16,8,16,128]{3,2,1,0:T(8,128)S(1)}, f32[16,8,16,128]{3,2,1,0:T(8,128)}, u32[]{:S(2)}) copy-start(f32[16,8,16,128]{3,2,1,0:T(8,128)} %load.1) | copy-start | bytes 3145732
  1.9 0.7 copy-start.4
  2.5 0.7 copy-start.6
  3.2 10.1 %copy-start.1 = (f32[16,8,16,128]{3,2,1,0:T(8,128)S(1)}, f32[16,8,16,128]{3,2,1,0:T(8,128)}, u32[]{:S(2)}) copy-start(f32[16,8,16,128]{3,2,1,0:T(8,128)} %load.1) | copy-start | bytes 3145732
  6.0 7.3 %copy-start.5 = (s32[8,16]{1,0:T(8,128)S(1)}, s32[8,16]{1,0:T(8,128)}, u32[]{:S(2)}) copy-start(s32[8,16]{1,0:T(8,128)} %ids.9) | copy-start | bytes 1540
  6.0 7.3 %copy-start.7 = (s32[8,16]{1,0:T(8,128)S(1)}, s32[8,16]{1,0:T(8,128)}, u32[]{:S(2)}) copy-start(s32[8,16]{1,0:T(8,128)} %types.9) | copy-start | bytes 1540
  6.0 34.4 %all-to-all-start = ((f32[32,16,128]{2,1,0:T(8,128)}), f32[32,16,128]{2,1,0:T(8,128)S(1)}, u32[]{:S(2)}, u32[]{:S(2)}) async-start(f32[32,16,128]{2,1,0:T(8,128)} %get-tuple-element.28), calls=%async_computation | async-start | bytes 524288 | tf_op jit(solution)/shard_map/all_to_all | solution.py:702
  13.6 12.4 %collective-permute-start.1 = (f32[544,128]{1,0:T(8,128)S(1)}, f32[544,128]{1,0:T(8,128)S(1)}, u32[]{:S(2)}, u32[]{:S(2)}) collective-permute-start(f32[544,128]{1,0:T(8,128)S(1)} %bitcast.12), channel_id=1, source_target_pairs={{4,0},{8,4},{12,8},{16,12},{20,16},{24,20},{28,24},{5,1},{9,5},{13... | collective-permute-start | bytes 835592 | tf_op jit(solution)/shard_map/ppermute | solution.py:691
  14.9 16.5 %collective-permute-start = (f32[544,128]{1,0:T(8,128)S(1)}, f32[544,128]{1,0:T(8,128)S(1)}, u32[]{:S(2)}, u32[]{:S(2)}) collective-permute-start(f32[544,128]{1,0:T(8,128)S(1)} %bitcast.11), channel_id=1, source_target_pairs={{0,4},{4,8},{8,12},{12,16},{16,20},{20,24},{24,28},{1,5},{5,9},{9,... | collective-permute-start | bytes 835592 | tf_op jit(solution)/shard_map/ppermute | solution.py:690
  32.4 7.0 %collective-permute-start.2 = (f32[328,128]{1,0:T(8,128)}, f32[328,128]{1,0:T(8,128)S(1)}, u32[]{:S(2)}, u32[]{:S(2)}) collective-permute-start(f32[328,128]{1,0:T(8,128)} %get-tuple-element.25), channel_id=1, source_target_pairs={{0,1},{1,2},{2,3},{4,5},{5,6},{6,7},{8,9},{9,10},{10,11},{12,13},{... | collective-permute-start | bytes 503816 | tf_op jit(solution)/shard_map/ppermute | solution.py:721
  34.1 5.3 %collective-permute-start.3 = (f32[328,128]{1,0:T(8,128)S(1)}, f32[328,128]{1,0:T(8,128)S(1)}, u32[]{:S(2)}, u32[]{:S(2)}) collective-permute-start(f32[328,128]{1,0:T(8,128)S(1)} %get-tuple-element.26), channel_id=1, source_target_pairs={{1,0},{2,1},{3,2},{5,4},{6,5},{7,6},{9,8},{10,9},{11,10},{13,12},{... | collective-permute-start | bytes 503816 | tf_op jit(solution)/shard_map/ppermute | solution.py:722
  35.4 0.7 copy-start.9
  36.1 1.0 %copy-start.10 = (f32[8,128,128]{2,1,0:T(8,128)S(1)}, f32[8,128,128]{2,1,0:T(8,128)}, u32[]{:S(2)}) copy-start(f32[8,128,128]{2,1,0:T(8,128)} %library.1) | copy-start | bytes 1572868
  37.1 2.2 %copy-start.8 = (s32[8,256]{1,0:T(8,128)S(1)}, s32[8,256]{1,0:T(8,128)}, u32[]{:S(2)}) copy-start(s32[8,256]{1,0:T(8,128)} %constant.17.clone.maps) | copy-start | bytes 24580
  38.5 0.8 copy-start.2
  40.4 1.0 %copy-start.3 = (bf16[8,128,256]{2,1,0:T(8,128)(2,1)S(1)}, bf16[8,128,256]{2,1,0:T(8,128)(2,1)}, u32[]{:S(2)}) copy-start(bf16[8,128,256]{2,1,0:T(8,128)(2,1)} %copy-done.2) | copy-start | bytes 1572868

commit v3 on v2

--- a/solution.py
+++ b/solution.py
@@ -709,7 +709,7 @@
             shape((kinds, nodes), F32),
         ],
         [],
-        1_000_000_000,
+        40_000_000_000,
         16,
     )(block_library, strap_conductance)
     side_rows = (rows + 2) * 2 * sizings

time: 85.3 us -> 76.4 us (0.90)
  waiting for transfers between devices: 11.9 us -> 3.36 us
  local copies, waits for them, and re-layouts: 6.14 us -> 4.53 us
    ppermute x1, waiting for transfers between devices: 6.55 us -> 0.01 us  [on_device(): lax.ppermute(top.reshape(edge_rows, nodes), 'row', [(j, i) for i, j in fo...]
    ppermute x1, waiting for transfers between devices: 5.38 us -> 1.85 us  [on_device(): above = lax.ppermute(bottom.reshape(edge_rows, nodes), 'row', forth)]
    unnamed x22, local copies, waits for them, and re-layouts: 6.06 us -> 4.44 us
    ppermute x1, waiting for transfers between devices: 0.01 us -> 1.5 us  [on_device(): east = lax.ppermute(to_west, 'col', [(j, i) for i, j in forth])]
    all_to_all x1, starting transfers between devices: 7.3 us -> 6.22 us  [on_device(): gathered = lax.all_to_all(pay, ('row', 'col'), 0, 0)]
    ppermute x1, starting transfers between devices: 4.56 us -> 5.52 us  [on_device(): above = lax.ppermute(bottom.reshape(edge_rows, nodes), 'row', forth)]
    all_to_all x1, blocking collectives: 21 us -> 21.8 us  [on_device(): gathered = lax.all_to_all(pay, ('row', 'col'), 0, 0)]
  transfers between devices with their start and end apart: 5 -> 5, of which waited for: 2 -> 2; matrix products, arithmetic and copies ran while one was open for 0% -> 0% of each run, Pallas kernels for 4% -> 8%
where the time goes in v3:
time: 76.4 us; the launch traced here: 75.9 us
  Pallas kernels  29 us (38%)
  blocking collectives  21.8 us (29%)
  starting transfers between devices  16.4 us (21%)
  local copies, waits for them, and re-layouts  4.53 us (6%)
  waiting for transfers between devices  3.36 us (4%)
  between operations  0.8 us (1%)
    all_to_all x1, blocking collectives, on_device(): gathered = lax.all_to_all(pay, ('row', 'col'), 0, 0)  21.8 us
    pallas_call x1, Pallas kernels, on_device(): call(functools.partial(middle_kernel, dims, mesh_dims), [SMEM] * 3 + [VME...  17.2 us
    all_to_all x1, starting transfers between devices, on_device(): gathered = lax.all_to_all(pay, ('row', 'col'), 0, 0)  6.22 us
    ppermute x1, starting transfers between devices, on_device(): above = lax.ppermute(bottom.reshape(edge_rows, nodes), 'row', forth)  5.52 us
    pallas_call x1, Pallas kernels, on_device(): call(functools.partial(last_kernel, dims, mesh_dims), [SMEM] * 2 + [VMEM]...  5.35 us
    unnamed x22, local copies, waits for them, and re-layouts  4.44 us
    pallas_call x1, Pallas kernels, on_device(): call(functools.partial(sums_kernel, dims), [SMEM] + [VMEM] * 3, [own, sha...  2.79 us
    ppermute x1, starting transfers between devices, on_device(): west = lax.ppermute(to_east, 'col', forth)  1.96 us
  transfers between devices with their start and end apart: 5, of which 2 were waited for; matrix products, arithmetic and copies ran while one was open for 0% of the time, Pallas kernels for 8%

profile of v3, /device:TPU:0, one launch (start us, length us, event | category | flops | bytes accessed | tf_op | source)
XLA Modules:
  0.0 75.9 jit_solution(15369700525969318770)
XLA Ops:
  0.6 0.0 copy-start
  0.6 1.2 %copy-done = f32[16,8,16,128]{3,2,1,0:T(8,128)S(1)} copy-done((f32[16,8,16,128]{3,2,1,0:T(8,128)S(1)}, f32[16,8,16,128]{3,2,1,0:T(8,128)}, u32[]{:S(2)}) %copy-start) | copy-done | bytes 1048600
  1.9 0.0 copy-start.4
  1.9 0.7 copy-done.4
  2.5 0.0 copy-start.6
  2.5 0.7 copy-done.6
  3.2 0.0 copy-start.1
  3.2 0.3 shard_map.77
  3.5 0.0 copy-start.7
  3.5 0.0 copy-start.5
  3.5 1.4 %collective-permute-start.1 = (f32[544,128]{1,0:T(8,128)S(1)}, f32[544,128]{1,0:T(8,128)S(1)}, u32[]{:S(2)}, u32[]{:S(2)}) collective-permute-start(f32[544,128]{1,0:T(8,128)S(1)} %bitcast.12), channel_id=1, source_target_pairs={{4,0},{8,4},{12,8},{16,12},{20,16},{24,20},{28,24},{5,1},{9,5},{13... | collective-permute-start | bytes 835592 | tf_op jit(solution)/shard_map/ppermute | solution.py:691
  4.9 5.5 %collective-permute-start = (f32[544,128]{1,0:T(8,128)S(1)}, f32[544,128]{1,0:T(8,128)S(1)}, u32[]{:S(2)}, u32[]{:S(2)}) collective-permute-start(f32[544,128]{1,0:T(8,128)S(1)} %bitcast.11), channel_id=1, source_target_pairs={{0,4},{4,8},{8,12},{12,16},{16,20},{20,24},{24,28},{1,5},{5,9},{9,... | collective-permute-start | bytes 835592 | tf_op jit(solution)/shard_map/ppermute | solution.py:690
  10.5 0.0 copy-done.1
  10.5 0.0 copy-done.7
  10.5 0.0 copy-done.5
  10.5 2.8 %shard_map.78 = (f32[2048,128]{1,0:T(8,128)S(1)}, f32[32,16,128]{2,1,0:T(8,128)}) custom-call(s32[8,16]{1,0:T(8,128)S(1)} %copy-done.5, s32[8,16]{1,0:T(8,128)S(1)} %copy-done.7, s32[8,16]{1,0:T(8,128)S(1)} %copy-done.5, f32[2048,128]{1,0:T(8,128)S(1)} %bitcast.10), custom_call_target="tpu_custom_call" | custom-call | flops 1000000 | bytes 4000000 | tf_op jit(solution)/shard_map/pallas_call | solution.py:694
  13.3 6.2 %all-to-all-start = ((f32[32,16,128]{2,1,0:T(8,128)}), f32[32,16,128]{2,1,0:T(8,128)S(1)}, u32[]{:S(2)}, u32[]{:S(2)}) async-start(f32[32,16,128]{2,1,0:T(8,128)} %get-tuple-element.28), calls=%async_computation | async-start | bytes 524288 | tf_op jit(solution)/shard_map/all_to_all | solution.py:702
  19.5 0.0 collective-permute-done.1.below
  19.5 1.9 %collective-permute-done.above = f32[544,128]{1,0:T(8,128)S(1)} collective-permute-done((f32[544,128]{1,0:T(8,128)S(1)}, f32[544,128]{1,0:T(8,128)S(1)}, u32[]{:S(2)}, u32[]{:S(2)}) %collective-permute-start) | collective-permute-done | bytes 278560 | tf_op jit(solution)/shard_map/ppermute | solution.py:690
  21.4 0.0 copy-start.10
  21.4 0.9 %shard_map.79 = (f32[328,128]{1,0:T(8,128)S(1)}, f32[328,128]{1,0:T(8,128)}) custom-call(s32[8,16]{1,0:T(8,128)S(1)} %copy-done.7, s32[8,16]{1,0:T(8,128)S(1)} %copy-done.5, f32[2048,128]{1,0:T(8,128)S(1)} %get-tuple-element.24.blocks, f32[544,128]{1,0:T(8,128)S(1)} %collective-permute-done.above, f32[544,128]{1,0:T(8,128)S(1)} %collective-permute-done.1.below), custom_call_target="tpu_custom_call" | custom-call | flops 1000000 | bytes 4000000 | tf_op jit(solution)/shard_map/pallas_call | solution.py:717
  22.3 0.0 copy-start.9
  22.3 2.0 %collective-permute-start.2 = (f32[328,128]{1,0:T(8,128)}, f32[328,128]{1,0:T(8,128)S(1)}, u32[]{:S(2)}, u32[]{:S(2)}) collective-permute-start(f32[328,128]{1,0:T(8,128)} %get-tuple-element.25), channel_id=1, source_target_pairs={{0,1},{1,2},{2,3},{4,5},{5,6},{6,7},{8,9},{9,10},{10,11},{12,13},{... | collective-permute-start | bytes 503816 | tf_op jit(solution)/shard_map/ppermute | solution.py:721
  24.3 1.3 %collective-permute-start.3 = (f32[328,128]{1,0:T(8,128)S(1)}, f32[328,128]{1,0:T(8,128)S(1)}, u32[]{:S(2)}, u32[]{:S(2)}) collective-permute-start(f32[328,128]{1,0:T(8,128)S(1)} %get-tuple-element.26), channel_id=1, source_target_pairs={{1,0},{2,1},{3,2},{5,4},{6,5},{7,6},{9,8},{10,9},{11,10},{13,12},{... | collective-permute-start | bytes 503816 | tf_op jit(solution)/shard_map/ppermute | solution.py:722
  25.6 0.0 copy-done.10
  25.6 0.0 copy-done.9
  25.6 1.4 %shard_map.81 = (bf16[8,256,256]{2,1,0:T(8,128)(2,1)S(1)}, bf16[8,128,256]{2,1,0:T(8,128)(2,1)S(1)}, f32[8,128]{1,0:T(8,128)S(1)}) custom-call(f32[8,128,128]{2,1,0:T(8,128)S(1)} %copy-done.10, f32[2,128]{1,0:T(2,128)S(1)} %copy-done.9), custom_call_target="tpu_custom_call" | custom-call | flops 40000000000 | bytes 4000000 | tf_op jit(solution)/shard_map/pallas_call | solution.py:703
  27.0 0.0 copy-start.2
  27.0 0.8 %copy-done.2 = bf16[8,128,256]{2,1,0:T(8,128)(2,1)} copy-done((bf16[8,128,256]{2,1,0:T(8,128)(2,1)}, bf16[8,128,256]{2,1,0:T(8,128)(2,1)S(1)}, u32[]{:S(2)}) %copy-start.2) | copy-done | bytes 524312
  27.8 0.0 copy-start.8
  27.8 0.1 stack.39.info
  27.9 0.0 collective-permute-done.2.west
  27.9 1.5 %collective-permute-done.3.east = f32[328,128]{1,0:T(8,128)S(1)} collective-permute-done((f32[328,128]{1,0:T(8,128)S(1)}, f32[328,128]{1,0:T(8,128)S(1)}, u32[]{:S(2)}, u32[]{:S(2)}) %collective-permute-start.3) | collective-permute-done | bytes 167968 | tf_op jit(solution)/shard_map/ppermute | solution.py:722
  29.4 0.0 copy-done.8
  29.4 1.1 %shard_map.80 = (s32[8,384]{1,0:T(8,128)S(1)}, s32[1,256]{1,0:T(1,128)S(1)}) custom-call(s32[8,256]{1,0:T(8,128)S(1)} %copy-done.8, s32[8,16]{1,0:T(8,128)S(1)} %copy-done.7, s32[8,16]{1,0:T(8,128)S(1)} %copy-done.5, f32[544,128]{1,0:T(8,128)S(1)} %collective-permute-done.above, f32[544,128]{1,0:T(8,128)S(1)} %collective-permute-done.1.below, ...), custom_call_target="tpu_custom_call" | custom-call | flops 1000000 | bytes 4000000 | tf_op jit(solution)/shard_map/pallas_call | solution.py:729
  30.5 0.0 all-to-all-done.gathered
  30.5 0.0 copy-start.3
  30.5 1.0 %copy-done.3 = bf16[8,128,256]{2,1,0:T(8,128)(2,1)S(1)} copy-done((bf16[8,128,256]{2,1,0:T(8,128)(2,1)S(1)}, bf16[8,128,256]{2,1,0:T(8,128)(2,1)}, u32[]{:S(2)}) %copy-start.3) | copy-done | bytes 524312
  31.5 17.2 %shard_map.82 = (f32[2048,128]{1,0:T(8,128)S(1)}, f32[2048,128]{1,0:T(8,128)S(1)}, f32[2048,128]{1,0:T(8,128)S(1)}, f32[2048,128]{1,0:T(8,128)S(1)}, f32[64,256]...) custom-call(s32[8,384]{1,0:T(8,128)S(1)} %get-tuple-element.27.plan, s32[5]{0:T(128)S(1)} %stack.39.info, ...), custom_call_target="tpu_custom_call" | custom-call | flops 1000000000 | bytes 4000000 | tf_op jit(solution)/shard_map/pallas_call | solution.py:749
  48.7 21.8 %all_to_all.10.gathered = f32[32,17,128]{2,1,0:T(8,128)S(1)} all-to-all(f32[32,17,128]{2,1,0:T(8,128)S(1)} %get-tuple-element.33), channel_id=1, replica_groups=mesh['row'=8,'col'=4] {'row','col'}, dimensions={0} | all-to-all | bytes 557056 | tf_op jit(solution)/shard_map/all_to_all | solution.py:766
  70.6 5.3 %shard_map.83 = (f32[2048,128]{1,0:T(8,128)}, f32[2048,128]{1,0:T(8,128)}) custom-call(s32[8,16]{1,0:T(8,128)S(1)} %copy-done.7, s32[5]{0:T(128)S(1)} %stack.39.info, f32[32,17,128]{2,1,0:T(8,128)S(1)} %all_to_all.10.gathered, s32[1,256]{1,0:T(1,128)S(1)} %get-tuple-element.29.keys, f32[64,256]{1,0:T(8,128)S(1)} %get-tuple-element.34.inverses, ...), custom_call_target="tpu_custom_call" | custom-call | flops 1000000000 | bytes 4000000 | tf_op jit(solution)/shard_map/pallas_call | solution.py:768
Async XLA Ops:
  0.6 1.2 %copy-start = (f32[16,8,16,128]{3,2,1,0:T(8,128)S(1)}, f32[16,8,16,128]{3,2,1,0:T(8,128)}, u32[]{:S(2)}) copy-start(f32[16,8,16,128]{3,2,1,0:T(8,128)} %load.1) | copy-start | bytes 3145732
  1.9 0.7 copy-start.4
  2.5 0.7 copy-start.6
  3.2 7.2 %copy-start.1 = (f32[16,8,16,128]{3,2,1,0:T(8,128)S(1)}, f32[16,8,16,128]{3,2,1,0:T(8,128)}, u32[]{:S(2)}) copy-start(f32[16,8,16,128]{3,2,1,0:T(8,128)} %load.1) | copy-start | bytes 3145732
  3.5 7.0 %copy-start.7 = (s32[8,16]{1,0:T(8,128)S(1)}, s32[8,16]{1,0:T(8,128)}, u32[]{:S(2)}) copy-start(s32[8,16]{1,0:T(8,128)} %types.9) | copy-start | bytes 1540
  3.5 7.0 %copy-start.5 = (s32[8,16]{1,0:T(8,128)S(1)}, s32[8,16]{1,0:T(8,128)}, u32[]{:S(2)}) copy-start(s32[8,16]{1,0:T(8,128)} %ids.9) | copy-start | bytes 1540
  3.5 16.0 %collective-permute-start.1 = (f32[544,128]{1,0:T(8,128)S(1)}, f32[544,128]{1,0:T(8,128)S(1)}, u32[]{:S(2)}, u32[]{:S(2)}) collective-permute-start(f32[544,128]{1,0:T(8,128)S(1)} %bitcast.12), channel_id=1, source_target_pairs={{4,0},{8,4},{12,8},{16,12},{20,16},{24,20},{28,24},{5,1},{9,5},{13... | collective-permute-start | bytes 835592 | tf_op jit(solution)/shard_map/ppermute | solution.py:691
  4.9 16.4 %collective-permute-start = (f32[544,128]{1,0:T(8,128)S(1)}, f32[544,128]{1,0:T(8,128)S(1)}, u32[]{:S(2)}, u32[]{:S(2)}) collective-permute-start(f32[544,128]{1,0:T(8,128)S(1)} %bitcast.11), channel_id=1, source_target_pairs={{0,4},{4,8},{8,12},{12,16},{16,20},{20,24},{24,28},{1,5},{5,9},{9,... | collective-permute-start | bytes 835592 | tf_op jit(solution)/shard_map/ppermute | solution.py:690
  13.3 17.2 %all-to-all-start = ((f32[32,16,128]{2,1,0:T(8,128)}), f32[32,16,128]{2,1,0:T(8,128)S(1)}, u32[]{:S(2)}, u32[]{:S(2)}) async-start(f32[32,16,128]{2,1,0:T(8,128)} %get-tuple-element.28), calls=%async_computation | async-start | bytes 524288 | tf_op jit(solution)/shard_map/all_to_all | solution.py:702
  21.4 4.2 %copy-start.10 = (f32[8,128,128]{2,1,0:T(8,128)S(1)}, f32[8,128,128]{2,1,0:T(8,128)}, u32[]{:S(2)}) copy-start(f32[8,128,128]{2,1,0:T(8,128)} %library.1) | copy-start | bytes 1572868
  22.3 3.3 %copy-start.9 = (f32[2,128]{1,0:T(2,128)S(1)}, f32[2,128]{1,0:T(2,128)}, u32[]{:S(2)}) copy-start(f32[2,128]{1,0:T(2,128)} %strap.5) | copy-start | bytes 3076
  22.3 5.6 %collective-permute-start.2 = (f32[328,128]{1,0:T(8,128)}, f32[328,128]{1,0:T(8,128)S(1)}, u32[]{:S(2)}, u32[]{:S(2)}) collective-permute-start(f32[328,128]{1,0:T(8,128)} %get-tuple-element.25), channel_id=1, source_target_pairs={{0,1},{1,2},{2,3},{4,5},{5,6},{6,7},{8,9},{9,10},{10,11},{12,13},{... | collective-permute-start | bytes 503816 | tf_op jit(solution)/shard_map/ppermute | solution.py:721
  24.3 5.1 %collective-permute-start.3 = (f32[328,128]{1,0:T(8,128)S(1)}, f32[328,128]{1,0:T(8,128)S(1)}, u32[]{:S(2)}, u32[]{:S(2)}) collective-permute-start(f32[328,128]{1,0:T(8,128)S(1)} %get-tuple-element.26), channel_id=1, source_target_pairs={{1,0},{2,1},{3,2},{5,4},{6,5},{7,6},{9,8},{10,9},{11,10},{13,12},{... | collective-permute-start | bytes 503816 | tf_op jit(solution)/shard_map/ppermute | solution.py:722
  27.0 0.8 %copy-start.2 = (bf16[8,128,256]{2,1,0:T(8,128)(2,1)}, bf16[8,128,256]{2,1,0:T(8,128)(2,1)S(1)}, u32[]{:S(2)}) copy-start(bf16[8,128,256]{2,1,0:T(8,128)(2,1)S(1)} %get-tuple-element.31.low) | copy-start | bytes 1572868
  27.8 1.6 %copy-start.8 = (s32[8,256]{1,0:T(8,128)S(1)}, s32[8,256]{1,0:T(8,128)}, u32[]{:S(2)}) copy-start(s32[8,256]{1,0:T(8,128)} %constant.17.clone.maps) | copy-start | bytes 24580
  30.5 1.0 %copy-start.3 = (bf16[8,128,256]{2,1,0:T(8,128)(2,1)S(1)}, bf16[8,128,256]{2,1,0:T(8,128)(2,1)}, u32[]{:S(2)}) copy-start(bf16[8,128,256]{2,1,0:T(8,128)(2,1)} %copy-done.2) | copy-start | bytes 1572868

commit v4 on v3

--- a/solution.py
+++ b/solution.py
@@ -11,13 +11,14 @@
 AGR = 4
 AGC = 4
 TILE = 8
-GROUP = 2
+GROUP = 4
 PANEL = 8
 F32 = jnp.float32
 BF16 = jnp.bfloat16
 HIGHEST = lax.Precision.HIGHEST
 VMEM = pl.BlockSpec(memory_space=pltpu.VMEM)
 SMEM = pl.BlockSpec(memory_space=pltpu.SMEM)
+HBM = pl.BlockSpec(memory_space=pltpu.HBM)
 
 
 def iota(shape, dim):
@@ -62,54 +63,93 @@
 
 def meta_rows(types, ids, many, height):
     rows = [flat_row(types[...], many), flat_row(ids[...], many) + 1.0]
-    return jnp.concatenate(rows + [jnp.zeros((height - 2, many), F32)], axis=0)
-
-
-def edges_kernel(dims, load, types, ids, top, bottom, sems):
+    spare = [jnp.zeros((height - 2, many), F32)] if height > 2 else []
+    return jnp.concatenate(rows + spare, axis=0)
+
+
+def either(odd, if_even, if_odd):
+    return jnp.where(odd == 1, if_odd, if_even)
+
+
+def edges_kernel(
+    dims, info, load, types_hbm, ids_hbm, first, second, types, ids, sems
+):
     sizings, rows, cols, nodes, count = dims
     many = rows * cols
+    odd = info[5]
     copies = [
+        pltpu.make_async_copy(types_hbm, types, sems.at[0]),
+        pltpu.make_async_copy(ids_hbm, ids, sems.at[1]),
         pltpu.make_async_copy(
-            load.at[:, pl.ds(first, 2)], out.at[pl.ds(0, sizings)], sems.at[i]
-        )
-        for i, (out, first) in enumerate(((top, 0), (bottom, rows - 2)))
+            load.at[:, pl.ds(either(odd, rows - 2, 0), 2)],
+            first.at[pl.ds(0, sizings)],
+            sems.at[2],
+        ),
+        pltpu.make_async_copy(
+            load.at[:, pl.ds(either(odd, 0, rows - 2), 2)],
+            second.at[pl.ds(0, sizings)],
+            sems.at[3],
+        ),
     ]
     for copy in copies:
         copy.start()
+    copies[0].wait()
+    copies[1].wait()
     meta = meta_rows(types, ids, many, cols)
     blank = jnp.zeros((cols, nodes), F32)
-    top[sizings, 0] = meta
-    top[sizings, 1] = blank
-    bottom[sizings, 0] = pltpu.roll(meta, 2 * cols, 1)
-    bottom[sizings, 1] = blank
-    for copy in copies:
-        copy.wait()
-
-
-def sums_kernel(dims, ids_smem, types, ids, load, blocks, pay):
+    top, bottom = meta, pltpu.roll(meta, 2 * cols, 1)
+    first[sizings, 0] = either(odd, bottom, top)
+    first[sizings, 1] = blank
+    second[sizings, 0] = either(odd, top, bottom)
+    second[sizings, 1] = blank
+    copies[2].wait()
+    copies[3].wait()
+
+
+def sums_kernel(dims, ids_smem, types, ids, load, pay):
     sizings, rows, cols, nodes, count = dims
     many = rows * cols
-    lanes = iota((sizings, max(count, 128)), 1)
-
-    def step(r, sums):
+    width = max(count, 128)
+    lane, side = iota((cols, width), 1), iota((cols, width), 0)
+    hots = []
+    for r in range(rows):
+        names = jnp.zeros((cols, width), jnp.int32)
+        for c in range(cols):
+            names = jnp.where(side == c, ids_smem[r, c], names)
+        hots.append((names == lane).astype(F32))
+    sums = []
+    for s in range(sizings):
+        total = jnp.zeros((cols, width), F32)
+        for r in range(rows):
+            at = s * many + r * cols
+            total = total + hots[r] * jnp.sum(load[at : at + cols, :], axis=1, keepdims=True)
+        sums.append(jnp.sum(total, axis=0, keepdims=True))
+    height = sizings * count // 128
+    meta = meta_rows(types, ids, many, pay.shape[1] - height)
+    whole = jnp.concatenate([pack(jnp.concatenate(sums, axis=0), count), meta], axis=0)
+    send_all(pay, whole)
+
+
+def send_all(pay, whole):
+    def copy(d, carry):
+        pay[d] = whole.reshape(pay.shape[1:])
+        return carry
+
+    lax.fori_loop(0, pay.shape[0], copy, 0)
+
+
+def blocks_kernel(dims, load, blocks):
+    sizings, rows, cols, nodes, count = dims
+    many = rows * cols
+
+    def step(r, carry):
         for c in range(cols):
             b = r * cols + c
-            block = load[pl.ds(b, sizings, stride=many), :]
-            blocks[pl.ds(pl.multiple_of(b * sizings, sizings), sizings), :] = block
-            total = jnp.sum(block, axis=1, keepdims=True)
-            sums = sums + jnp.where(lanes == ids_smem[r, c], total, 0.0)
-        return sums
-
-    sums = lax.fori_loop(0, rows, step, jnp.zeros(lanes.shape, F32))
-    height = sizings * count // 128
-    meta = meta_rows(types, ids, many, pay.shape[1] - height)
-    whole = jnp.concatenate([pack(sums, count), meta], axis=0)
-
-    def copy(d, carry):
-        pay[d] = whole
+            at = pl.ds(pl.multiple_of(b * sizings, sizings), sizings)
+            blocks[at, :] = load[pl.ds(b, sizings, stride=many), :]
         return carry
 
-    lax.fori_loop(0, pay.shape[0], copy, 0)
+    lax.fori_loop(0, rows, step, 0)
 
 
 def weights_kernel(library, strap, stacked, low, row_sums):
@@ -138,41 +178,50 @@
     lax.fori_loop(0, kinds, step, 0, unroll=True)
 
 
-def sides_kernel(dims, types, ids, blocks, above, below, west, east):
+def sides_kernel(
+    dims, info, types, ids, blocks, row_first, row_second, row_sums, first, second
+):
     sizings, rows, cols, nodes, count = dims
     last = sizings * 2 * cols
+    row_odd, odd = info[5], info[6]
     own = meta_rows(types, ids, rows * cols, 8)
-    metas = [own, above[last : last + 8, :], below[last : last + 8, :]]
+    one, two = row_first[last : last + 8, :], row_second[last : last + 8, :]
+    metas = [own, either(row_odd, two, one), either(row_odd, one, two)]
     metas = jnp.concatenate(metas, axis=1).astype(BF16)
     shape = (metas.shape[1], 128)
     slot, lane = iota(shape, 0), iota(shape, 1)
-    for out, first in ((west, 0), (east, cols - 2)):
+    for out, begin in ((first, either(odd, cols - 2, 0)), (second, either(odd, 0, cols - 2))):
         for side in range(2):
-            c = first + side
-            for k in range(rows + 2):
-                to = (k * 2 + side) * sizings
-                if k == 0:
-                    block = above[pl.ds(cols + c, sizings, stride=2 * cols), :]
-                elif k == rows + 1:
-                    block = below[pl.ds(c, sizings, stride=2 * cols), :]
-                else:
-                    at = ((k - 1) * cols + c) * sizings
-                    block = blocks[at : at + sizings, :]
-                out[to : to + sizings, :] = block
+            c = begin + side
+            above = pl.ds(cols + c, sizings, stride=2 * cols)
+            below = pl.ds(c, sizings, stride=2 * cols)
+            to = side * sizings
+            out[to : to + sizings, :] = either(row_odd, row_second[above, :], row_first[above, :])
+            to = ((rows + 1) * 2 + side) * sizings
+            out[to : to + sizings, :] = either(row_odd, row_first[below, :], row_second[below, :])
+            for r in range(rows):
+                at = pl.multiple_of((r * cols + c) * sizings, sizings)
+                to = ((r + 1) * 2 + side) * sizings
+                out[to : to + sizings, :] = blocks[pl.ds(at, sizings), :]
         k = lane // 2
         place = (k - 1) * cols
         place = jnp.where(k == 0, rows * cols + cols, place)
-        place = jnp.where(k == rows + 1, 2 * rows * cols, place) + first + lane % 2
+        place = jnp.where(k == rows + 1, 2 * rows * cols, place) + begin + lane % 2
         pick = (slot == place) & (k < rows + 2)
         picked = jnp.dot(metas, pick.astype(F32).astype(BF16), preferred_element_type=F32)
         out[(rows + 2) * 2 * sizings :, :] = picked
 
 
-def order_kernel(dims, kinds, lengths, maps, types, ids, above, below, west, east, plan, keys):
+def order_kernel(
+    dims, kinds, info, maps, types, ids, row_first, row_second, col_first, col_second, solved, plan, keys
+):
     sizings, rows, cols, nodes, count = dims
     many = rows * cols
     own = meta_rows(types, ids, many, 8)
-    metas = jnp.concatenate([own, above[...], below[...], west[...], east[...]], axis=1)
+    metas = [own]
+    for odd, one, two in ((info[5], row_first, row_second), (info[6], col_first, col_second)):
+        metas += [either(odd, two[...], one[...]), either(odd, one[...], two[...])]
+    metas = jnp.concatenate(metas, axis=1)
     shape = (metas.shape[1], maps.shape[1])
     pick = (iota(shape, 0) == maps[0:1, :]).astype(F32).astype(BF16)
     near = jnp.dot(metas.astype(BF16), pick, preferred_element_type=F32)
@@ -331,7 +380,7 @@
 
     def rows_of(g, at):
         return jnp.concatenate(
-            [gathered[i * n_col + g, at : at + 1, :] for i in range(n_row)], axis=0
+            [gathered[i * n_col + g, at : at + 1, 0, :] for i in range(n_row)], axis=0
         )
 
     def hot(values, labels):
@@ -366,12 +415,16 @@
         cross[g] = pairs[:, 2 * count : 3 * count]
 
 
+def total_of(gathered, first, height, mesh_dims, g):
+    n_row, n_col = mesh_dims
+    total = gathered[g, first : first + height]
+    for i in range(1, n_row):
+        total = total + gathered[i * n_col + g, first : first + height]
+    return total.reshape(height, 128)
+
+
 def coarse_solve(gathered, first, height, mesh_dims, count, sizings, inverses, g):
-    n_row, n_col = mesh_dims
-    total = gathered[g, first : first + height, :]
-    for i in range(1, n_row):
-        total = total + gathered[i * n_col + g, first : first + height, :]
-    sums = unpack(total, count, sizings)
+    sums = unpack(total_of(gathered, first, height, mesh_dims, g), count, sizings)
     solved = jnp.dot(
         sums, inverses[:, g * count : (g + 1) * count], precision=HIGHEST,
         preferred_element_type=F32,
@@ -393,43 +446,10 @@
         )
 
 
-def middle_kernel(
-    dims, mesh_dims,
-    plan, info, ids,
-    gathered, keys, blocks, above, below, west, east, stacked, low, row_sums, strap,
-    z_out, q_out, u_out, au_out, inverses, cross, pay,
-    field, level, z, bz, q, u, bu, solved,
-):
+def coarse_kernel(dims, mesh_dims, gathered, row_sums, strap, inverses, cross, solved):
     sizings, rows, cols, nodes, count = dims
-    n_row, n_col = mesh_dims
-    wide = cols + 4
-    many = (rows + 4) * wide
+    n_col = mesh_dims[1]
     height = sizings * count // 128
-
-    def at(er, ec):
-        return pl.ds(pl.multiple_of((er * wide + ec) * sizings, sizings), sizings)
-
-    span = cols * sizings
-    for r in range(rows):
-        to = ((r + 2) * wide + 2) * sizings
-        field[to : to + span, :] = blocks[r * span : (r + 1) * span, :]
-    for r in range(2):
-        for c in range(cols):
-            from_edge = pl.ds(r * cols + c, sizings, stride=2 * cols)
-            to = (r * wide + 2 + c) * sizings
-            field[to : to + sizings, :] = above[from_edge, :]
-            to = ((rows + 2 + r) * wide + 2 + c) * sizings
-            field[to : to + sizings, :] = below[from_edge, :]
-    for k in range(rows + 2):
-        pair = 2 * sizings
-        to = (k + 1) * wide * sizings
-        field[to : to + pair, :] = west[k * pair : (k + 1) * pair, :]
-        to = to + (cols + 2) * sizings
-        field[to : to + pair, :] = east[k * pair : (k + 1) * pair, :]
-    field[many * sizings :, :] = jnp.zeros((sizings, nodes), F32)
-    level[many * sizings :, :] = jnp.zeros((sizings, nodes), F32)
-    q[many * sizings :, :] = jnp.zeros((sizings, nodes), F32)
-
     coarse_matrices(dims, mesh_dims, gathered, row_sums, strap, inverses, cross)
     if count <= 64:
         invert_unrolled(inverses, count)
@@ -441,6 +461,46 @@
         _, solved[g + 1] = coarse_solve(
             gathered, 0, height, mesh_dims, count, sizings, inverses, g
         )
+
+
+def middle_kernel(
+    dims,
+    plan, info, ids,
+    solved, keys, blocks, row_first, row_second, col_first, col_second,
+    stacked, low, row_sums, strap,
+    z_out, q_out, u_out, au_out, pay,
+    field, level, z, bz, q, u, bu,
+):
+    sizings, rows, cols, nodes, count = dims
+    wide = cols + 4
+    many = (rows + 4) * wide
+
+    def at(er, ec):
+        return pl.ds(pl.multiple_of((er * wide + ec) * sizings, sizings), sizings)
+
+    row_odd, col_odd = info[5], info[6]
+    span = cols * sizings
+    for r in range(rows):
+        to = ((r + 2) * wide + 2) * sizings
+        field[to : to + span, :] = blocks[r * span : (r + 1) * span, :]
+    for r in range(2):
+        for c in range(cols):
+            edge = pl.ds(r * cols + c, sizings, stride=2 * cols)
+            one, two = row_first[edge, :], row_second[edge, :]
+            to = (r * wide + 2 + c) * sizings
+            field[to : to + sizings, :] = either(row_odd, two, one)
+            to = ((rows + 2 + r) * wide + 2 + c) * sizings
+            field[to : to + sizings, :] = either(row_odd, one, two)
+    for k in range(rows + 2):
+        pair = 2 * sizings
+        one, two = [ref[k * pair : (k + 1) * pair, :] for ref in (col_first, col_second)]
+        to = (k + 1) * wide * sizings
+        field[to : to + pair, :] = either(col_odd, two, one)
+        to = to + (cols + 2) * sizings
+        field[to : to + pair, :] = either(col_odd, one, two)
+    field[many * sizings :, :] = jnp.zeros((sizings, nodes), F32)
+    level[many * sizings :, :] = jnp.zeros((sizings, nodes), F32)
+    q[many * sizings :, :] = jnp.zeros((sizings, nodes), F32)
     spread(solved, info[0], keys, level, count, sizings, nodes, many)
 
     def store_z(kind, places, out):
@@ -455,15 +515,15 @@
     north, east_strap = strap[0:1, :], strap[1:2, :]
     couple = 2.0 * north + 2.0 * east_strap
 
-    def operator(v, bv, er, ec):
-        here = v[at(er, ec), :]
+    def operator(v, bv, er, ec, row=None):
+        row = row or [v[at(er, ec + j), :] for j in (-1, 0, 1)]
         image = (
             bv[at(er, ec), :]
-            + couple * here
+            + couple * row[1]
             - north * (v[at(er - 1, ec), :] + v[at(er + 1, ec), :])
-            - east_strap * (v[at(er, ec - 1), :] + v[at(er, ec + 1), :])
-        )
-        return here, image
+            - east_strap * (row[0] + row[2])
+        )
+        return row[1], image
 
     for er, flag in ((1, info[1]), (rows + 2, info[2])):
         inside = flag.astype(F32)
@@ -488,8 +548,10 @@
 
     def first_row(r, carry):
         rz, zq, sums = carry
+        line = [z[at(r + 2, 1), :], z[at(r + 2, 2), :]]
         for c in range(cols):
-            here, image = operator(z, bz, r + 2, c + 2)
+            line.append(z[at(r + 2, c + 3), :])
+            here, image = operator(z, bz, r + 2, c + 2, line[c : c + 3])
             q[at(r + 2, c + 2), :] = image
             b = r * cols + c
             own = pl.ds(pl.multiple_of(b * sizings, sizings), sizings)
@@ -512,8 +574,10 @@
 
     def second_row(r, carry):
         qu, uau, sums = carry
+        line = [u[at(r + 2, 1), :], u[at(r + 2, 2), :]]
         for c in range(cols):
-            here, image = operator(u, bu, r + 2, c + 2)
+            line.append(u[at(r + 2, c + 3), :])
+            here, image = operator(u, bu, r + 2, c + 2, line[c : c + 3])
             b = r * cols + c
             own = pl.ds(pl.multiple_of(b * sizings, sizings), sizings)
             u_out[own, :] = here
@@ -534,11 +598,7 @@
     dots = jnp.sum(dots, axis=0, keepdims=True)
     whole = jnp.concatenate([pack(sums_q, count), pack(sums_u, count), dots], axis=0)
 
-    def copy(d, carry):
-        pay[d] = whole
-        return carry
-
-    lax.fori_loop(0, pay.shape[0], copy, 0)
+    send_all(pay, whole)
 
 
 def last_kernel(
@@ -564,9 +624,7 @@
     for g in range(n_col):
         sums, one = coarse_solve(gathered, 0, height, *mesh_args, inverses, g)
         solved[g + 1] = one
-        image = gathered[g, height : 2 * height, :]
-        for i in range(1, n_row):
-            image = image + gathered[i * n_col + g, height : 2 * height, :]
+        image = total_of(gathered, height, height, mesh_dims, g)
         with_q = with_q + sums * one
         with_u = with_u + unpack(image, count, sizings) * one
         if before is not None:
@@ -576,9 +634,9 @@
         before = one
     spread(solved, info[0], keys, level, count, sizings, nodes, many)
 
-    dots = gathered[0, 2 * height : 2 * height + 1, :]
+    dots = gathered[0, 2 * height]
     for d in range(1, n_row * n_col):
-        dots = dots + gathered[d, 2 * height : 2 * height + 1, :]
+        dots = dots + gathered[d, 2 * height]
     lane = iota((sizings, 128), 1)
     dots = jnp.where(lane // 4 == iota((sizings, 128), 0), dots, 0.0)
     rz, zq, qu, uau = [
@@ -662,6 +720,11 @@
     )
 
 
+def swap(payload, axis, begin):
+    pairs = [(i, i + 1) for i in range(begin, lax.axis_size(axis) - 1, 2)]
+    return lax.ppermute(payload, axis, pairs + [(j, i) for i, j in pairs])
+
+
 def on_device(load_currents, block_library, strap_conductance, block_types, aggregate_map):
     sizings, rows, cols, nodes = load_currents.shape
     kinds = block_library.shape[0]
@@ -676,29 +739,40 @@
     shape = jax.ShapeDtypeStruct
     own = shape((block_rows, nodes), F32)
 
+    info = jnp.stack(
+        [
+            col,
+            (row > 0).astype(jnp.int32),
+            (row < n_row - 1).astype(jnp.int32),
+            (col > 0).astype(jnp.int32),
+            (col < n_col - 1).astype(jnp.int32),
+            row % 2,
+            col % 2,
+        ]
+    )
     edge = shape((sizings + 1, 2, cols, nodes), F32)
-    top, bottom = call(
+    first, second = call(
         functools.partial(edges_kernel, dims),
-        [pl.BlockSpec(memory_space=pl.ANY), VMEM, VMEM],
+        [SMEM] + [HBM] * 3,
         [edge, edge],
-        [pltpu.SemaphoreType.DMA((2,))],
+        [pltpu.VMEM((rows, cols), jnp.int32)] * 2 + [pltpu.SemaphoreType.DMA((4,))],
         1_000_000,
-        8,
-    )(load_currents, block_types, aggregate_map)
-    forth = [(i, i + 1) for i in range(n_row - 1)]
+        4,
+    )(info, load_currents, block_types, aggregate_map)
     edge_rows = (sizings + 1) * 2 * cols
-    above = lax.ppermute(bottom.reshape(edge_rows, nodes), "row", forth)
-    below = lax.ppermute(top.reshape(edge_rows, nodes), "row", [(j, i) for i, j in forth])
-
-    pay_rows = -(-(height + 2) // 8) * 8
-    blocks, pay = call(
+    row_first = swap(first.reshape(edge_rows, nodes), "row", 0)
+    row_second = swap(second.reshape(edge_rows, nodes), "row", 1)
+
+    pay_rows = height + 2
+    flat_load = load_currents.reshape(-1, nodes)
+    (pay,) = call(
         functools.partial(sums_kernel, dims),
         [SMEM] + [VMEM] * 3,
-        [own, shape((n_dev, pay_rows, 128), F32)],
+        [shape((n_dev, pay_rows, 1, 128), F32)],
         [],
-        1_000_000,
-        16,
-    )(aggregate_map, block_types, aggregate_map, load_currents.reshape(-1, nodes))
+        20_000_000_000,
+        4 if count <= 64 else 16,
+    )(aggregate_map, block_types, aggregate_map, flat_load)
     gathered = lax.all_to_all(pay, ("row", "col"), 0, 0)
     stacked, low, row_sums = call(
         weights_kernel,
@@ -709,59 +783,66 @@
             shape((kinds, nodes), F32),
         ],
         [],
-        40_000_000_000,
-        16,
+        1_000_000,
+        8,
     )(block_library, strap_conductance)
+    (blocks,) = call(
+        functools.partial(blocks_kernel, dims), [VMEM], [own], [], 1_000_000, 4
+    )(flat_load)
     side_rows = (rows + 2) * 2 * sizings
     side = shape((side_rows + 8, nodes), F32)
-    to_west, to_east = call(
-        functools.partial(sides_kernel, dims), [VMEM] * 5, [side, side], [], 1_000_000, 16
-    )(block_types, aggregate_map, blocks, above, below)
-    forth = [(i, i + 1) for i in range(n_col - 1)]
-    west = lax.ppermute(to_east, "col", forth)
-    east = lax.ppermute(to_west, "col", [(j, i) for i, j in forth])
-
+    first, second = call(
+        functools.partial(sides_kernel, dims),
+        [SMEM] + [VMEM] * 6,
+        [side, side],
+        [],
+        40_000_000_000,
+        4,
+    )(info, block_types, aggregate_map, blocks, row_first, row_second, row_sums)
+    col_first, col_second = swap(first, "col", 0), swap(second, "col", 1)
+
+    big = pltpu.VMEM(((many + 1) * sizings, nodes), F32)
+    coarse_shape = (n_col + 2, sizings, count)
+    inverses, cross, solved = call(
+        functools.partial(coarse_kernel, dims, mesh_dims),
+        [VMEM] * 3,
+        [
+            shape((count, n_col * count), F32),
+            shape((n_col, count, count), F32),
+            shape(coarse_shape, F32),
+        ],
+        [],
+        10_000_000_000,
+        8 if count <= 64 else 48,
+    )(gathered, row_sums, strap_conductance)
     maps = ring_maps(rows, cols, count)
     longest = int(max(maps[1].sum(), maps[2].sum())) + (TILE - 1) * kinds + GROUP * TILE
     longest = -(-longest // 128) * 128
     edge_meta = pl.BlockSpec((8, 128), lambda i: (sizings * 2 * cols // 8, 0))
     side_meta = pl.BlockSpec((8, 128), lambda i: (side_rows // 8, 0))
     plan, keys = call(
-        functools.partial(order_kernel, dims, kinds, longest),
-        [VMEM] * 3 + [edge_meta, edge_meta, side_meta, side_meta],
+        functools.partial(order_kernel, dims, kinds),
+        [SMEM] + [VMEM] * 3 + [edge_meta, edge_meta, side_meta, side_meta, VMEM],
         [shape((8, longest), jnp.int32), shape((1, maps.shape[1]), jnp.int32)],
         [],
         1_000_000,
-        16,
+        8,
         grid=(1,),
-    )(jnp.asarray(maps), block_types, aggregate_map, above, below, west, east)
-    info = jnp.stack(
-        [
-            col,
-            (row > 0).astype(jnp.int32),
-            (row < n_row - 1).astype(jnp.int32),
-            (col > 0).astype(jnp.int32),
-            (col < n_col - 1).astype(jnp.int32),
-        ]
+    )(
+        info, jnp.asarray(maps), block_types, aggregate_map,
+        row_first, row_second, col_first, col_second, solved,
     )
-    big = pltpu.VMEM(((many + 1) * sizings, nodes), F32)
-    coarse = pltpu.VMEM((n_col + 2, sizings, count), F32)
-    z, q, u, au, inverses, cross, pay = call(
-        functools.partial(middle_kernel, dims, mesh_dims),
+    z, q, u, au, pay = call(
+        functools.partial(middle_kernel, dims),
         [SMEM] * 3 + [VMEM] * 11,
-        [own] * 4
-        + [
-            shape((count, n_col * count), F32),
-            shape((n_col, count, count), F32),
-            shape((n_dev, 2 * height + 1, 128), F32),
-        ],
-        [big] * 7 + [coarse],
+        [own] * 4 + [shape((n_dev, 2 * height + 1, 1, 128), F32)],
+        [big] * 7,
         1_000_000_000,
-        32 if count <= 64 else 56,
+        20 if count <= 64 else 48,
     )(
         plan, info, aggregate_map,
-        gathered, keys, blocks, above, below, west, east, stacked, low, row_sums,
-        strap_conductance,
+        solved, keys, blocks, row_first, row_second, col_first, col_second,
+        stacked, low, row_sums, strap_conductance,
     )
     gathered = lax.all_to_all(pay, ("row", "col"), 0, 0)
     out = shape((sizings * rows * cols, nodes), F32)
@@ -769,9 +850,9 @@
         functools.partial(last_kernel, dims, mesh_dims),
         [SMEM] * 2 + [VMEM] * 11,
         [out, out],
-        [big, coarse],
+        [big, pltpu.VMEM(coarse_shape, F32)],
         1_000_000_000,
-        16 if count <= 64 else 32,
+        8 if count <= 64 else 32,
     )(
         block_types, info,
         gathered, keys, inverses, cross, z, q, u, au, blocks, row_sums, strap_conductance,

time: 76.4 us -> 67.1 us (0.88)
  starting transfers between devices: 16.4 us -> 11.9 us
  blocking collectives: 21.8 us -> 17.8 us
  waiting for transfers between devices: 3.36 us -> 4.54 us
  local copies, waits for them, and re-layouts: 4.53 us -> 3.53 us
  Pallas kernels: 29 us -> 28.1 us
    all_to_all x1, blocking collectives: 21.8 us -> 17.8 us  [on_device(): gathered = lax.all_to_all(pay, ('row', 'col'), 0, 0)]
    ppermute x4, starting transfers between devices: 10.2 us -> 7.2 us  [swap(): return lax.ppermute(payload, axis, pairs + [(j, i) for i, j in pairs])]
    all_to_all x1, starting transfers between devices: 6.22 us -> 4.72 us  [on_device(): gathered = lax.all_to_all(pay, ('row', 'col'), 0, 0)]
    all_to_all x1, waiting for transfers between devices: 0.01 us -> 1.22 us  [on_device(): gathered = lax.all_to_all(pay, ('row', 'col'), 0, 0)]
    unnamed x22 -> x18, local copies, waits for them, and re-layouts: 4.44 us -> 3.44 us
    pallas_call x5 -> x7, Pallas kernels: 22.2 us -> 21.3 us  [the longest x1 10.3 us: on_device(): call(functools.partial(middle_kernel, dims), [SMEM] * 3 + [VMEM] * 11, [o...]
  transfers between devices with their start and end apart: 5 -> 5, of which waited for: 2 -> 2; matrix products, arithmetic and copies ran while one was open for 0% -> 0% of each run, Pallas kernels for 8% -> 15%
where the time goes in v4:
time: 67.1 us; the launch traced here: 66.7 us
  Pallas kernels  28.1 us (42%)
  blocking collectives  17.8 us (27%)
  starting transfers between devices  11.9 us (18%)
  waiting for transfers between devices  4.54 us (7%)
  local copies, waits for them, and re-layouts  3.53 us (5%)
  between operations  0.82 us (1%)
    all_to_all x1, blocking collectives, on_device(): gathered = lax.all_to_all(pay, ('row', 'col'), 0, 0)  17.8 us
    pallas_call x1, Pallas kernels, on_device(): call(functools.partial(middle_kernel, dims), [SMEM] * 3 + [VMEM] * 11, [o...  10.3 us
    ppermute x4, starting transfers between devices, swap(): return lax.ppermute(payload, axis, pairs + [(j, i) for i, j in pairs])  7.2 us
    pallas_call x1, Pallas kernels, on_device(): call(functools.partial(last_kernel, dims, mesh_dims), [SMEM] * 2 + [VMEM]...  5.33 us
    pallas_call x1, Pallas kernels, on_device(): call(functools.partial(coarse_kernel, dims, mesh_dims), [VMEM] * 3, [shap...  5.19 us
    all_to_all x1, starting transfers between devices, on_device(): gathered = lax.all_to_all(pay, ('row', 'col'), 0, 0)  4.72 us
    unnamed x18, local copies, waits for them, and re-layouts  3.44 us
    ppermute x4, waiting for transfers between devices, swap(): return lax.ppermute(payload, axis, pairs + [(j, i) for i, j in pairs])  3.32 us
  transfers between devices with their start and end apart: 5, of which 2 were waited for; matrix products, arithmetic and copies ran while one was open for 0% of the time, Pallas kernels for 15%

profile of v4, /device:TPU:0, one launch (start us, length us, event | category | flops | bytes accessed | tf_op | source)
XLA Modules:
  0.0 66.7 jit_solution(3816944298770305567)
XLA Ops:
  0.7 0.0 copy-start.4
  0.7 0.0 copy-start.3
  0.7 0.1 stack.47.info
  0.8 0.6 copy-done.4
  1.3 0.0 copy-done.3
  1.4 0.0 copy-start
  1.4 1.2 %copy-done = f32[16,8,16,128]{3,2,1,0:T(8,128)S(1)} copy-done((f32[16,8,16,128]{3,2,1,0:T(8,128)S(1)}, f32[16,8,16,128]{3,2,1,0:T(8,128)}, u32[]{:S(2)}) %copy-start) | copy-done | bytes 1048600
  2.6 0.0 copy-start.1
  2.6 0.8 %shard_map.77 = (f32[17,2,16,128]{3,2,1,0:T(8,128)S(1)}, f32[17,2,16,128]{3,2,1,0:T(8,128)S(1)}) custom-call(s32[7]{0:T(128)S(1)} %stack.47.info, f32[16,8,16,128]{3,2,1,0:T(8,128)S(1)} %copy-done, s32[8,16]{1,0:T(8,128)S(1)} %copy-done.3, s32[8,16]{1,0:T(8,128)S(1)} %copy-done.4), custom_call_target="tpu_custom_call" | custom-call | flops 1000000 | bytes 4000000 | tf_op jit(solution)/shard_map/pallas_call | solution.py:754
  3.4 0.7 %collective-permute-start.1 = (f32[544,128]{1,0:T(8,128)S(1)}, f32[544,128]{1,0:T(8,128)S(1)}, u32[]{:S(2)}, u32[]{:S(2)}) collective-permute-start(f32[544,128]{1,0:T(8,128)S(1)} %bitcast.15), channel_id=1, source_target_pairs={{4,8},{12,16},{20,24},{8,4},{16,12},{24,20},{5,9},{13,17},{21,25},... | collective-permute-start | bytes 835592 | tf_op jit(solution)/shard_map/ppermute | solution.py:725
  4.1 5.8 %collective-permute-start = (f32[544,128]{1,0:T(8,128)S(1)}, f32[544,128]{1,0:T(8,128)S(1)}, u32[]{:S(2)}, u32[]{:S(2)}) collective-permute-start(f32[544,128]{1,0:T(8,128)S(1)} %bitcast.14), channel_id=1, source_target_pairs={{0,4},{8,12},{16,20},{24,28},{4,0},{12,8},{20,16},{28,24},{1,5},{9... | collective-permute-start | bytes 835592 | tf_op jit(solution)/shard_map/ppermute | solution.py:725
  9.9 0.0 copy-done.1
  9.9 2.0 %shard_map.81 = f32[32,10,1,128]{3,2,1,0:T(1,128)} custom-call(s32[8,16]{1,0:T(8,128)S(1)} %copy-done.4, s32[8,16]{1,0:T(8,128)S(1)} %copy-done.3, s32[8,16]{1,0:T(8,128)S(1)} %copy-done.4, f32[2048,128]{1,0:T(8,128)S(1)} %bitcast.12), custom_call_target="tpu_custom_call" | custom-call | flops 20000000000 | bytes 4000000 | tf_op jit(solution)/shard_map/pallas_call | solution.py:768
  11.9 4.7 %all-to-all-start = ((f32[32,10,1,128]{3,2,1,0:T(1,128)}), f32[32,10,1,128]{3,2,1,0:T(1,128)S(1)}, u32[]{:S(2)}, u32[]{:S(2)}) async-start(f32[32,10,1,128]{3,2,1,0:T(1,128)} %shard_map.81), calls=%async_computation | async-start | bytes 327680 | tf_op jit(solution)/shard_map/all_to_all | solution.py:776
  16.6 0.0 copy-start.2
  16.6 0.0 copy-start.6
  16.6 0.7 shard_map.78.blocks
  17.3 0.4 copy-done.2
  17.6 0.0 copy-done.6
  17.6 1.4 %shard_map.79 = (bf16[8,256,256]{2,1,0:T(8,128)(2,1)S(1)}, bf16[8,128,256]{2,1,0:T(8,128)(2,1)S(1)}, f32[8,128]{1,0:T(8,128)S(1)}) custom-call(f32[8,128,128]{2,1,0:T(8,128)S(1)} %copy-done.2, f32[2,128]{1,0:T(2,128)S(1)} %copy-done.6), custom_call_target="tpu_custom_call" | custom-call | flops 1000000 | bytes 4000000 | tf_op jit(solution)/shard_map/pallas_call | solution.py:777
  19.0 0.0 copy-start.7
  19.1 0.0 collective-permute-done.1.row_second
  19.1 3.3 %collective-permute-done.row_first = f32[544,128]{1,0:T(8,128)S(1)} collective-permute-done((f32[544,128]{1,0:T(8,128)S(1)}, f32[544,128]{1,0:T(8,128)S(1)}, u32[]{:S(2)}, u32[]{:S(2)}) %collective-permute-start) | collective-permute-done | bytes 278560 | tf_op jit(solution)/shard_map/ppermute | solution.py:725
  22.4 0.8 %shard_map.80 = (f32[328,128]{1,0:T(8,128)S(1)}, f32[328,128]{1,0:T(8,128)S(1)}) custom-call(s32[7]{0:T(128)S(1)} %stack.47.info, s32[8,16]{1,0:T(8,128)S(1)} %copy-done.3, s32[8,16]{1,0:T(8,128)S(1)} %copy-done.4, f32[2048,128]{1,0:T(8,128)S(1)} %shard_map.78.blocks, f32[544,128]{1,0:T(8,128)S(1)} %collective-permute-done.row_first, ...), custom_call_target="tpu_custom_call" | custom-call | flops 40000000000 | bytes 4000000 | tf_op jit(solution)/shard_map/pallas_call | solution.py:794
  23.2 0.0 copy-done.7
  23.2 0.1 collective-permute-start.2
  23.2 0.0 copy-start.5
  23.3 0.7 %collective-permute-start.3 = (f32[328,128]{1,0:T(8,128)S(1)}, f32[328,128]{1,0:T(8,128)S(1)}, u32[]{:S(2)}, u32[]{:S(2)}) collective-permute-start(f32[328,128]{1,0:T(8,128)S(1)} %get-tuple-element.25), channel_id=1, source_target_pairs={{1,2},{2,1},{5,6},{6,5},{9,10},{10,9},{13,14},{14,13},{17,18},{18,... | collective-permute-start | bytes 503816 | tf_op jit(solution)/shard_map/ppermute | solution.py:725
  23.9 1.2 %all-to-all-done.gathered = f32[32,10,1,128]{3,2,1,0:T(1,128)S(1)} async-done(((f32[32,10,1,128]{3,2,1,0:T(1,128)}), f32[32,10,1,128]{3,2,1,0:T(1,128)S(1)}, u32[]{:S(2)}, u32[]{:S(2)}) %all-to-all-start) | async-done | bytes 163872 | tf_op jit(solution)/shard_map/all_to_all | solution.py:776
  25.2 5.2 %shard_map.82 = (f32[64,256]{1,0:T(8,128)S(1)}, f32[4,64,64]{2,1,0:T(8,128)S(1)}, f32[6,16,64]{2,1,0:T(8,128)S(1)}) custom-call(f32[32,10,1,128]{3,2,1,0:T(1,128)S(1)} %all-to-all-done.gathered, f32[8,128]{1,0:T(8,128)S(1)} %get-tuple-element.23.row_sums, f32[2,128]{1,0:T(2,128)S(1)} %copy-done.6), custom_call_target="tpu_custom_call" | custom-call | flops 10000000000 | bytes 4000000 | tf_op jit(solution)/shard_map/pallas_call | solution.py:806
  30.4 0.0 collective-permute-done.2.col_first
  30.4 0.0 collective-permute-done.3.col_second
  30.4 0.0 copy-done.5
  30.4 1.6 %shard_map.83 = (s32[8,384]{1,0:T(8,128)S(1)}, s32[1,256]{1,0:T(1,128)S(1)}) custom-call(s32[7]{0:T(128)S(1)} %stack.47.info, s32[8,256]{1,0:T(8,128)S(1)} %copy-done.5, s32[8,16]{1,0:T(8,128)S(1)} %copy-done.3, s32[8,16]{1,0:T(8,128)S(1)} %copy-done.4, f32[544,128]{1,0:T(8,128)S(1)} %collective-permute-done.row_first, ...), custom_call_target="tpu_custom_call" | custom-call | flops 1000000 | bytes 4000000 | tf_op jit(solution)/shard_map/pallas_call | solution.py:823
  32.0 0.0 copy-start.8
  32.0 1.2 %copy-done.8 = bf16[8,256,256]{2,1,0:T(8,128)(2,1)S(1)} copy-done((bf16[8,256,256]{2,1,0:T(8,128)(2,1)S(1)}, bf16[8,256,256]{2,1,0:T(8,128)(2,1)}, u32[]{:S(2)}) %copy-start.8) | copy-done | bytes 1048600
  33.2 10.3 %shard_map.84 = (f32[2048,128]{1,0:T(8,128)S(1)}, f32[2048,128]{1,0:T(8,128)S(1)}, f32[2048,128]{1,0:T(8,128)S(1)}, f32[2048,128]{1,0:T(8,128)S(1)}, f32[32,17,1,128]{3,2,1,0:T(1,128)S(1)}) custom-call(s32[8,384]{1,0:T(8,128)S(1)} %get-tuple-element.27.plan, s32[7]{0:T(128)S(1)} %stack.47.info, s32[8,16]{1,0:T(8,128)S(1)} %copy-done.4, ...), custom_call_target="tpu_custom_call" | custom-call | flops 1000000000 | bytes 4000000 | tf_op jit(solution)/shard_map/pallas_call | solution.py:835
  43.6 17.8 %all_to_all.10.gathered = f32[32,17,1,128]{3,2,1,0:T(1,128)S(1)} all-to-all(f32[32,17,1,128]{3,2,1,0:T(1,128)S(1)} %get-tuple-element.31), channel_id=1, replica_groups=mesh['row'=8,'col'=4] {'row','col'}, dimensions={0} | all-to-all | bytes 557056 | tf_op jit(solution)/shard_map/all_to_all | solution.py:847
  61.4 5.3 %shard_map.85 = (f32[2048,128]{1,0:T(8,128)}, f32[2048,128]{1,0:T(8,128)}) custom-call(s32[8,16]{1,0:T(8,128)S(1)} %copy-done.3, s32[7]{0:T(128)S(1)} %stack.47.info, f32[32,17,1,128]{3,2,1,0:T(1,128)S(1)} %all_to_all.10.gathered, s32[1,256]{1,0:T(1,128)S(1)} %get-tuple-element.28.keys, f32[64,256]{1,0:T(8,128)S(1)} %get-tuple-element.32.inverses, ...), custom_call_target="tpu_custom_call" | custom-call | flops 1000000000 | bytes 4000000 | tf_op jit(solution)/shard_map/pallas_call | solution.py:849
Async XLA Ops:
  0.7 0.7 %copy-start.4 = (s32[8,16]{1,0:T(8,128)S(1)}, s32[8,16]{1,0:T(8,128)}, u32[]{:S(2)}) copy-start(s32[8,16]{1,0:T(8,128)} %ids.7) | copy-start | bytes 1540
  0.7 0.7 %copy-start.3 = (s32[8,16]{1,0:T(8,128)S(1)}, s32[8,16]{1,0:T(8,128)}, u32[]{:S(2)}) copy-start(s32[8,16]{1,0:T(8,128)} %types.7) | copy-start | bytes 1540
  1.4 1.2 %copy-start = (f32[16,8,16,128]{3,2,1,0:T(8,128)S(1)}, f32[16,8,16,128]{3,2,1,0:T(8,128)}, u32[]{:S(2)}) copy-start(f32[16,8,16,128]{3,2,1,0:T(8,128)} %load.1) | copy-start | bytes 3145732
  2.6 7.3 %copy-start.1 = (f32[16,8,16,128]{3,2,1,0:T(8,128)S(1)}, f32[16,8,16,128]{3,2,1,0:T(8,128)}, u32[]{:S(2)}) copy-start(f32[16,8,16,128]{3,2,1,0:T(8,128)} %load.1) | copy-start | bytes 3145732
  3.4 15.6 %collective-permute-start.1 = (f32[544,128]{1,0:T(8,128)S(1)}, f32[544,128]{1,0:T(8,128)S(1)}, u32[]{:S(2)}, u32[]{:S(2)}) collective-permute-start(f32[544,128]{1,0:T(8,128)S(1)} %bitcast.15), channel_id=1, source_target_pairs={{4,8},{12,16},{20,24},{8,4},{16,12},{24,20},{5,9},{13,17},{21,25},... | collective-permute-start | bytes 835592 | tf_op jit(solution)/shard_map/ppermute | solution.py:725
  4.1 18.3 %collective-permute-start = (f32[544,128]{1,0:T(8,128)S(1)}, f32[544,128]{1,0:T(8,128)S(1)}, u32[]{:S(2)}, u32[]{:S(2)}) collective-permute-start(f32[544,128]{1,0:T(8,128)S(1)} %bitcast.14), channel_id=1, source_target_pairs={{0,4},{8,12},{16,20},{24,28},{4,0},{12,8},{20,16},{28,24},{1,5},{9... | collective-permute-start | bytes 835592 | tf_op jit(solution)/shard_map/ppermute | solution.py:725
  11.9 13.3 %all-to-all-start = ((f32[32,10,1,128]{3,2,1,0:T(1,128)}), f32[32,10,1,128]{3,2,1,0:T(1,128)S(1)}, u32[]{:S(2)}, u32[]{:S(2)}) async-start(f32[32,10,1,128]{3,2,1,0:T(1,128)} %shard_map.81), calls=%async_computation | async-start | bytes 327680 | tf_op jit(solution)/shard_map/all_to_all | solution.py:776
  16.6 1.0 %copy-start.2 = (f32[8,128,128]{2,1,0:T(8,128)S(1)}, f32[8,128,128]{2,1,0:T(8,128)}, u32[]{:S(2)}) copy-start(f32[8,128,128]{2,1,0:T(8,128)} %library.1) | copy-start | bytes 1572868
  16.6 1.0 %copy-start.6 = (f32[2,128]{1,0:T(2,128)S(1)}, f32[2,128]{1,0:T(2,128)}, u32[]{:S(2)}) copy-start(f32[2,128]{1,0:T(2,128)} %strap.7) | copy-start | bytes 3076
  19.0 4.1 %copy-start.7 = (bf16[8,256,256]{2,1,0:T(8,128)(2,1)}, bf16[8,256,256]{2,1,0:T(8,128)(2,1)S(1)}, u32[]{:S(2)}) copy-start(bf16[8,256,256]{2,1,0:T(8,128)(2,1)S(1)} %get-tuple-element.29.stacked) | copy-start | bytes 3145732
  23.2 7.2 %collective-permute-start.2 = (f32[328,128]{1,0:T(8,128)S(1)}, f32[328,128]{1,0:T(8,128)S(1)}, u32[]{:S(2)}, u32[]{:S(2)}) collective-permute-start(f32[328,128]{1,0:T(8,128)S(1)} %get-tuple-element.24), channel_id=1, source_target_pairs={{0,1},{2,3},{1,0},{3,2},{4,5},{6,7},{5,4},{7,6},{8,9},{10,11},{9,8... | collective-permute-start | bytes 503816 | tf_op jit(solution)/shard_map/ppermute | solution.py:725
  23.2 7.1 %copy-start.5 = (s32[8,256]{1,0:T(8,128)S(1)}, s32[8,256]{1,0:T(8,128)}, u32[]{:S(2)}) copy-start(s32[8,256]{1,0:T(8,128)} %constant.33.clone.maps) | copy-start | bytes 24580
  23.3 7.1 %collective-permute-start.3 = (f32[328,128]{1,0:T(8,128)S(1)}, f32[328,128]{1,0:T(8,128)S(1)}, u32[]{:S(2)}, u32[]{:S(2)}) collective-permute-start(f32[328,128]{1,0:T(8,128)S(1)} %get-tuple-element.25), channel_id=1, source_target_pairs={{1,2},{2,1},{5,6},{6,5},{9,10},{10,9},{13,14},{14,13},{17,18},{18,... | collective-permute-start | bytes 503816 | tf_op jit(solution)/shard_map/ppermute | solution.py:725
  32.0 1.2 %copy-start.8 = (bf16[8,256,256]{2,1,0:T(8,128)(2,1)S(1)}, bf16[8,256,256]{2,1,0:T(8,128)(2,1)}, u32[]{:S(2)}) copy-start(bf16[8,256,256]{2,1,0:T(8,128)(2,1)} %copy-done.7) | copy-start | bytes 3145732

commit v5 on v4

--- a/solution.py
+++ b/solution.py
@@ -18,7 +18,6 @@
 HIGHEST = lax.Precision.HIGHEST
 VMEM = pl.BlockSpec(memory_space=pltpu.VMEM)
 SMEM = pl.BlockSpec(memory_space=pltpu.SMEM)
-HBM = pl.BlockSpec(memory_space=pltpu.HBM)
 
 
 def iota(shape, dim):
@@ -69,41 +68,6 @@
 
 def either(odd, if_even, if_odd):
     return jnp.where(odd == 1, if_odd, if_even)
-
-
-def edges_kernel(
-    dims, info, load, types_hbm, ids_hbm, first, second, types, ids, sems
-):
-    sizings, rows, cols, nodes, count = dims
-    many = rows * cols
-    odd = info[5]
-    copies = [
-        pltpu.make_async_copy(types_hbm, types, sems.at[0]),
-        pltpu.make_async_copy(ids_hbm, ids, sems.at[1]),
-        pltpu.make_async_copy(
-            load.at[:, pl.ds(either(odd, rows - 2, 0), 2)],
-            first.at[pl.ds(0, sizings)],
-            sems.at[2],
-        ),
-        pltpu.make_async_copy(
-            load.at[:, pl.ds(either(odd, 0, rows - 2), 2)],
-            second.at[pl.ds(0, sizings)],
-            sems.at[3],
-        ),
-    ]
-    for copy in copies:
-        copy.start()
-    copies[0].wait()
-    copies[1].wait()
-    meta = meta_rows(types, ids, many, cols)
-    blank = jnp.zeros((cols, nodes), F32)
-    top, bottom = meta, pltpu.roll(meta, 2 * cols, 1)
-    first[sizings, 0] = either(odd, bottom, top)
-    first[sizings, 1] = blank
-    second[sizings, 0] = either(odd, top, bottom)
-    second[sizings, 1] = blank
-    copies[2].wait()
-    copies[3].wait()
 
 
 def sums_kernel(dims, ids_smem, types, ids, load, pay):
@@ -178,18 +142,9 @@
     lax.fori_loop(0, kinds, step, 0, unroll=True)
 
 
-def sides_kernel(
-    dims, info, types, ids, blocks, row_first, row_second, row_sums, first, second
-):
+def sides_kernel(dims, info, blocks, row_first, row_second, row_sums, first, second):
     sizings, rows, cols, nodes, count = dims
-    last = sizings * 2 * cols
     row_odd, odd = info[5], info[6]
-    own = meta_rows(types, ids, rows * cols, 8)
-    one, two = row_first[last : last + 8, :], row_second[last : last + 8, :]
-    metas = [own, either(row_odd, two, one), either(row_odd, one, two)]
-    metas = jnp.concatenate(metas, axis=1).astype(BF16)
-    shape = (metas.shape[1], 128)
-    slot, lane = iota(shape, 0), iota(shape, 1)
     for out, begin in ((first, either(odd, cols - 2, 0)), (second, either(odd, 0, cols - 2))):
         for side in range(2):
             c = begin + side
@@ -203,24 +158,20 @@
                 at = pl.multiple_of((r * cols + c) * sizings, sizings)
                 to = ((r + 1) * 2 + side) * sizings
                 out[to : to + sizings, :] = blocks[pl.ds(at, sizings), :]
-        k = lane // 2
-        place = (k - 1) * cols
-        place = jnp.where(k == 0, rows * cols + cols, place)
-        place = jnp.where(k == rows + 1, 2 * rows * cols, place) + begin + lane % 2
-        pick = (slot == place) & (k < rows + 2)
-        picked = jnp.dot(metas, pick.astype(F32).astype(BF16), preferred_element_type=F32)
-        out[(rows + 2) * 2 * sizings :, :] = picked
-
-
-def order_kernel(
-    dims, kinds, info, maps, types, ids, row_first, row_second, col_first, col_second, solved, plan, keys
-):
+
+
+def order_blocks(dims, mesh_dims, kinds, info, maps, gathered, plan, keys):
     sizings, rows, cols, nodes, count = dims
-    many = rows * cols
-    own = meta_rows(types, ids, many, 8)
-    metas = [own]
-    for odd, one, two in ((info[5], row_first, row_second), (info[6], col_first, col_second)):
-        metas += [either(odd, two[...], one[...]), either(odd, one[...], two[...])]
+    n_row, n_col = mesh_dims
+    height = sizings * count // 128
+    metas = []
+    for down in (-1, 0, 1):
+        for right in (-1, 0, 1):
+            r, c = info[7] + down, info[0] + right
+            inside = (r >= 0) & (r < n_row) & (c >= 0) & (c < n_col)
+            device = jnp.clip(r, 0, n_row - 1) * n_col + jnp.clip(c, 0, n_col - 1)
+            meta = gathered[device, height : height + 2].reshape(2, 128)
+            metas.append(meta * inside.astype(F32))
     metas = jnp.concatenate(metas, axis=1)
     shape = (metas.shape[1], maps.shape[1])
     pick = (iota(shape, 0) == maps[0:1, :]).astype(F32).astype(BF16)
@@ -446,10 +397,14 @@
         )
 
 
-def coarse_kernel(dims, mesh_dims, gathered, row_sums, strap, inverses, cross, solved):
+def coarse_kernel(
+    dims, mesh_dims, kinds, info, maps, gathered, row_sums, strap,
+    inverses, cross, solved, plan, keys,
+):
     sizings, rows, cols, nodes, count = dims
     n_col = mesh_dims[1]
     height = sizings * count // 128
+    order_blocks(dims, mesh_dims, kinds, info, maps, gathered, plan, keys)
     coarse_matrices(dims, mesh_dims, gathered, row_sums, strap, inverses, cross)
     if count <= 64:
         invert_unrolled(inverses, count)
@@ -684,7 +639,6 @@
 
 def ring_maps(rows, cols, count):
     tall, wide = rows + 4, cols + 4
-    many = rows * cols
     length = -(-tall * wide // 128) * 128
     maps = np.zeros((8, length), np.int32)
     maps[0] = -1
@@ -696,14 +650,8 @@
             maps[1, e] = down + over <= 2
             maps[2, e] = down + over <= 1
             maps[3, e] = count * ((ec >= 2) + (ec >= cols + 2))
-            if not down and not over:
-                maps[0, e] = (er - 2) * cols + ec - 2
-            elif not over:
-                south = er > 1
-                maps[0, e] = (1 + south) * many + (er - (rows + 2 if south else 0)) * cols + ec - 2
-            elif down <= 1:
-                right = ec > 1
-                maps[0, e] = (3 + right) * many + (er - 1) * 2 + ec - (cols + 2 if right else 0)
+            device = 3 * ((er >= 2) + (er >= rows + 2)) + (ec >= 2) + (ec >= cols + 2)
+            maps[0, e] = (device * rows + (er - 2) % rows) * cols + (ec - 2) % cols
     return maps
 
 
@@ -748,20 +696,14 @@
             (col < n_col - 1).astype(jnp.int32),
             row % 2,
             col % 2,
+            row,
         ]
     )
-    edge = shape((sizings + 1, 2, cols, nodes), F32)
-    first, second = call(
-        functools.partial(edges_kernel, dims),
-        [SMEM] + [HBM] * 3,
-        [edge, edge],
-        [pltpu.VMEM((rows, cols), jnp.int32)] * 2 + [pltpu.SemaphoreType.DMA((4,))],
-        1_000_000,
-        4,
-    )(info, load_currents, block_types, aggregate_map)
-    edge_rows = (sizings + 1) * 2 * cols
-    row_first = swap(first.reshape(edge_rows, nodes), "row", 0)
-    row_second = swap(second.reshape(edge_rows, nodes), "row", 1)
+    begin = (rows - 2) * (1 - row % 2)
+    first = lax.dynamic_slice_in_dim(load_currents, begin, 2, axis=1)
+    second = lax.dynamic_slice_in_dim(load_currents, rows - 2 - begin, 2, axis=1)
+    row_first = swap(first.reshape(-1, nodes), "row", 0)
+    row_second = swap(second.reshape(-1, nodes), "row", 1)
 
     pay_rows = height + 2
     flat_load = load_currents.reshape(-1, nodes)
@@ -790,48 +732,36 @@
         functools.partial(blocks_kernel, dims), [VMEM], [own], [], 1_000_000, 4
     )(flat_load)
     side_rows = (rows + 2) * 2 * sizings
-    side = shape((side_rows + 8, nodes), F32)
+    side = shape((side_rows, nodes), F32)
     first, second = call(
         functools.partial(sides_kernel, dims),
-        [SMEM] + [VMEM] * 6,
+        [SMEM] + [VMEM] * 4,
         [side, side],
         [],
         40_000_000_000,
         4,
-    )(info, block_types, aggregate_map, blocks, row_first, row_second, row_sums)
+    )(info, blocks, row_first, row_second, row_sums)
     col_first, col_second = swap(first, "col", 0), swap(second, "col", 1)
 
     big = pltpu.VMEM(((many + 1) * sizings, nodes), F32)
     coarse_shape = (n_col + 2, sizings, count)
-    inverses, cross, solved = call(
-        functools.partial(coarse_kernel, dims, mesh_dims),
-        [VMEM] * 3,
+    maps = ring_maps(rows, cols, count)
+    longest = int(max(maps[1].sum(), maps[2].sum())) + (TILE - 1) * kinds + GROUP * TILE
+    longest = -(-longest // 128) * 128
+    inverses, cross, solved, plan, keys = call(
+        functools.partial(coarse_kernel, dims, mesh_dims, kinds),
+        [SMEM] + [VMEM] * 4,
         [
             shape((count, n_col * count), F32),
             shape((n_col, count, count), F32),
             shape(coarse_shape, F32),
+            shape((8, longest), jnp.int32),
+            shape((1, maps.shape[1]), jnp.int32),
         ],
         [],
         10_000_000_000,
         8 if count <= 64 else 48,
-    )(gathered, row_sums, strap_conductance)
-    maps = ring_maps(rows, cols, count)
-    longest = int(max(maps[1].sum(), maps[2].sum())) + (TILE - 1) * kinds + GROUP * TILE
-    longest = -(-longest // 128) * 128
-    edge_meta = pl.BlockSpec((8, 128), lambda i: (sizings * 2 * cols // 8, 0))
-    side_meta = pl.BlockSpec((8, 128), lambda i: (side_rows // 8, 0))
-    plan, keys = call(
-        functools.partial(order_kernel, dims, kinds),
-        [SMEM] + [VMEM] * 3 + [edge_meta, edge_meta, side_meta, side_meta, VMEM],
-        [shape((8, longest), jnp.int32), shape((1, maps.shape[1]), jnp.int32)],
-        [],
-        1_000_000,
-        8,
-        grid=(1,),
-    )(
-        info, jnp.asarray(maps), block_types, aggregate_map,
-        row_first, row_second, col_first, col_second, solved,
-    )
+    )(info, jnp.asarray(maps), gathered, row_sums, strap_conductance)
     z, q, u, au, pay = call(
         functools.partial(middle_kernel, dims),
         [SMEM] * 3 + [VMEM] * 11,

time: 67.1 us -> 61.9 us (0.923)
  blocking collectives: 17.8 us -> 15.2 us
  waiting for transfers between devices: 4.54 us -> 3.21 us
  local copies, waits for them, and re-layouts: 3.53 us -> 2.43 us
    ppermute x4, waiting for transfers between devices: 3.32 us -> 0.01 us  [swap(): return lax.ppermute(payload, axis, pairs + [(j, i) for i, j in pairs])]
    unnamed x18 -> x12, local copies, waits for them, and re-layouts: 3.44 us -> 0.4 us
    all_to_all x1, blocking collectives: 17.8 us -> 15.2 us  [on_device(): gathered = lax.all_to_all(pay, ('row', 'col'), 0, 0)]
    all_to_all x1, starting transfers between devices: 4.72 us -> 6.94 us  [on_device(): gathered = lax.all_to_all(pay, ('row', 'col'), 0, 0)]
    ppermute x4, starting transfers between devices: 7.2 us -> 5.22 us  [swap(): return lax.ppermute(payload, axis, pairs + [(j, i) for i, j in pairs])]
    all_to_all x1, waiting for transfers between devices: 1.22 us -> 3.2 us  [on_device(): gathered = lax.all_to_all(pay, ('row', 'col'), 0, 0)]
    dynamic_slice x0 -> x1, local copies, waits for them, and re-layouts: none -> 1.94 us  [on_device(): lax.dynamic_slice_in_dim(load_currents, rows - 2 - begin, 2, axis=1)]
    pallas_call x4 -> x2, Pallas kernels: 8.4 us -> 8.18 us  [the longest x1 6.33 us: on_device(): call(functools.partial(coarse_kernel, dims, mesh_dims, kinds), [SMEM] + [...]
  transfers between devices with their start and end apart: 5 -> 5, of which waited for: 2 -> 1; matrix products, arithmetic and copies ran while one was open for 0% -> 0% of each run, Pallas kernels for 15% -> 20%
where the time goes in v5:
time: 61.9 us; the launch traced here: 61.5 us
  Pallas kernels  27.7 us (45%)
  blocking collectives  15.2 us (25%)
  starting transfers between devices  12.2 us (20%)
  waiting for transfers between devices  3.21 us (5%)
  local copies, waits for them, and re-layouts  2.43 us (4%)
  between operations  0.76 us (1%)
    all_to_all x1, blocking collectives, on_device(): gathered = lax.all_to_all(pay, ('row', 'col'), 0, 0)  15.2 us
    pallas_call x1, Pallas kernels, on_device(): call(functools.partial(middle_kernel, dims), [SMEM] * 3 + [VMEM] * 11, [o...  10.3 us
    all_to_all x1, starting transfers between devices, on_device(): gathered = lax.all_to_all(pay, ('row', 'col'), 0, 0)  6.94 us
    pallas_call x1, Pallas kernels, on_device(): call(functools.partial(coarse_kernel, dims, mesh_dims, kinds), [SMEM] + [...  6.33 us
    ppermute x4, starting transfers between devices, swap(): return lax.ppermute(payload, axis, pairs + [(j, i) for i, j in pairs])  5.22 us
    pallas_call x1, Pallas kernels, on_device(): call(functools.partial(last_kernel, dims, mesh_dims), [SMEM] * 2 + [VMEM]...  5.22 us
    all_to_all x1, waiting for transfers between devices, on_device(): gathered = lax.all_to_all(pay, ('row', 'col'), 0, 0)  3.2 us
    pallas_call x1, Pallas kernels, on_device(): call(functools.partial(sums_kernel, dims), [SMEM] + [VMEM] * 3, [shape((n...  1.95 us
  transfers between devices with their start and end apart: 5, of which 1 were waited for; matrix products, arithmetic and copies ran while one was open for 0% of the time, Pallas kernels for 20%

profile of v5, /device:TPU:0, one launch (start us, length us, event | category | flops | bytes accessed | tf_op | source)
XLA Modules:
  0.0 61.5 jit_solution(16440839402585283139)
XLA Ops:
  0.6 0.0 copy-start
  0.7 1.9 %constant_dynamic-slice_fusion = (f32[16,2,16,128]{3,2,1,0:T(8,128)}, f32[16,2,16,128]{3,2,1,0:T(8,128)}) fusion(f32[16,8,16,128]{3,2,1,0:T(8,128)} %param.6, s32[]{:T(128)S(6)} %select_n.22, s32[]{:T(128)S(6)} %select_n.21), kind=kLoop, calls=%fused_computation | loop fusion | bytes 1048584 | tf_op jit(solution)/shard_map/dynamic_slice | solution.py:704
  2.6 0.0 copy-start.4
  2.6 0.0 copy-start.2
  2.6 3.0 %collective-permute-start = (f32[512,128]{1,0:T(8,128)}, f32[512,128]{1,0:T(8,128)}, u32[]{:S(2)}, u32[]{:S(2)}) collective-permute-start(f32[512,128]{1,0:T(8,128)} %bitcast.9), channel_id=1, source_target_pairs={{0,4},{8,12},{16,20},{24,28},{4,0},{12,8},{20,16},{28,24},{1,5},{9... | collective-permute-start | bytes 786440 | tf_op jit(solution)/shard_map/ppermute | solution.py:673
  5.6 1.3 %collective-permute-start.1 = (f32[512,128]{1,0:T(8,128)}, f32[512,128]{1,0:T(8,128)}, u32[]{:S(2)}, u32[]{:S(2)}) collective-permute-start(f32[512,128]{1,0:T(8,128)} %bitcast.10), channel_id=1, source_target_pairs={{4,8},{12,16},{20,24},{8,4},{16,12},{24,20},{5,9},{13,17},{21,25},... | collective-permute-start | bytes 786440 | tf_op jit(solution)/shard_map/ppermute | solution.py:673
  6.9 0.0 copy-done
  6.9 0.0 copy-done.4
  6.9 0.0 copy-done.2
  6.9 2.0 %shard_map.77 = f32[32,10,1,128]{3,2,1,0:T(1,128)} custom-call(s32[8,16]{1,0:T(8,128)S(1)} %copy-done.4, s32[8,16]{1,0:T(8,128)S(1)} %copy-done.2, s32[8,16]{1,0:T(8,128)S(1)} %copy-done.4, f32[2048,128]{1,0:T(8,128)S(1)} %bitcast.13), custom_call_target="tpu_custom_call" | custom-call | flops 20000000000 | bytes 4000000 | tf_op jit(solution)/shard_map/pallas_call | solution.py:710
  8.9 6.9 %all-to-all-start = ((f32[32,10,1,128]{3,2,1,0:T(1,128)}), f32[32,10,1,128]{3,2,1,0:T(1,128)S(1)}, u32[]{:S(2)}, u32[]{:S(2)}) async-start(f32[32,10,1,128]{3,2,1,0:T(1,128)} %shard_map.77), calls=%async_computation | async-start | bytes 327680 | tf_op jit(solution)/shard_map/all_to_all | solution.py:718
  15.9 0.1 stack.51.info
  15.9 0.0 copy-start.1
  15.9 0.0 copy-start.3
  16.0 0.7 %shard_map.80.blocks = f32[2048,128]{1,0:T(8,128)S(1)} custom-call(f32[2048,128]{1,0:T(8,128)S(1)} %bitcast.14), custom_call_target="tpu_custom_call" | custom-call | flops 1000000 | bytes 4000000 | tf_op jit(solution)/shard_map/pallas_call | solution.py:731
  16.6 0.4 copy-done.1
  17.0 0.0 copy-done.3
  17.0 1.4 %shard_map.78 = (bf16[8,256,256]{2,1,0:T(8,128)(2,1)S(1)}, bf16[8,128,256]{2,1,0:T(8,128)(2,1)S(1)}, f32[8,128]{1,0:T(8,128)S(1)}) custom-call(f32[8,128,128]{2,1,0:T(8,128)S(1)} %copy-done.1, f32[2,128]{1,0:T(2,128)S(1)} %copy-done.3), custom_call_target="tpu_custom_call" | custom-call | flops 1000000 | bytes 4000000 | tf_op jit(solution)/shard_map/pallas_call | solution.py:719
  18.4 0.0 collective-permute-done.row_first
  18.4 0.0 collective-permute-done.1.row_second
  18.4 0.0 copy-start.5
  18.4 1.9 %shard_map.81 = (f32[320,128]{1,0:T(8,128)}, f32[320,128]{1,0:T(8,128)}) custom-call(s32[8]{0:T(128)S(1)} %stack.51.info, f32[2048,128]{1,0:T(8,128)S(1)} %shard_map.80.blocks, f32[512,128]{1,0:T(8,128)} %collective-permute-done.row_first, f32[512,128]{1,0:T(8,128)} %collective-permute-done.1.row_second, f32[8,128]{1,0:T(8,128)S(1)} %get-tuple-element.19.row_sums), custom_call_target="tpu_custom_call" | custom-call | flops 40000000000 | bytes 4000000 | tf_op jit(solution)/shard_map/pallas_call | solution.py:736
  20.3 0.3 collective-permute-start.2
  20.5 0.7 %collective-permute-start.3 = (f32[320,128]{1,0:T(8,128)}, f32[320,128]{1,0:T(8,128)S(1)}, u32[]{:S(2)}, u32[]{:S(2)}) collective-permute-start(f32[320,128]{1,0:T(8,128)} %get-tuple-element.24), channel_id=1, source_target_pairs={{1,2},{2,1},{5,6},{6,5},{9,10},{10,9},{13,14},{14,13},{17,18},{18,... | collective-permute-start | bytes 491528 | tf_op jit(solution)/shard_map/ppermute | solution.py:673
  21.2 3.2 %all-to-all-done.gathered = f32[32,10,1,128]{3,2,1,0:T(1,128)S(1)} async-done(((f32[32,10,1,128]{3,2,1,0:T(1,128)}), f32[32,10,1,128]{3,2,1,0:T(1,128)S(1)}, u32[]{:S(2)}, u32[]{:S(2)}) %all-to-all-start) | async-done | bytes 163872 | tf_op jit(solution)/shard_map/all_to_all | solution.py:718
  24.4 0.0 copy-done.5
  24.4 6.3 %shard_map.79 = (f32[64,256]{1,0:T(8,128)S(1)}, f32[4,64,64]{2,1,0:T(8,128)S(1)}, f32[6,16,64]{2,1,0:T(8,128)S(1)}, s32[8,384]{1,0:T(8,128)S(1)}, s32[1,256]{1,0:T(1,128)S(1)}) custom-call(s32[8]{0:T(128)S(1)} %stack.51.info, s32[8,256]{1,0:T(8,128)S(1)} %copy-done.5, f32[32,10,1,128]{3,2,1,0:T(1,128)S(1)} %all-to-all-done.gathered, ...), custom_call_target="tpu_custom_call" | custom-call | flops 10000000000 | bytes 4000000 | tf_op jit(solution)/shard_map/pallas_call | solution.py:751
  30.7 0.0 collective-permute-done.2.col_first
  30.7 0.0 collective-permute-done.3.col_second
  30.8 10.3 %shard_map.82 = (f32[2048,128]{1,0:T(8,128)S(1)}, f32[2048,128]{1,0:T(8,128)S(1)}, f32[2048,128]{1,0:T(8,128)S(1)}, f32[2048,128]{1,0:T(8,128)S(1)}, f32[32,17,1,128]{3,2,1,0:T(1,128)S(1)}) custom-call(s32[8,384]{1,0:T(8,128)S(1)} %get-tuple-element.20.plan, s32[8]{0:T(128)S(1)} %stack.51.info, s32[8,16]{1,0:T(8,128)S(1)} %copy-done.4, ...), custom_call_target="tpu_custom_call" | custom-call | flops 1000000000 | bytes 4000000 | tf_op jit(solution)/shard_map/pallas_call | solution.py:765
  41.0 15.2 %all_to_all.10.gathered = f32[32,17,1,128]{3,2,1,0:T(1,128)S(1)} all-to-all(f32[32,17,1,128]{3,2,1,0:T(1,128)S(1)} %get-tuple-element.27), channel_id=1, replica_groups=mesh['row'=8,'col'=4] {'row','col'}, dimensions={0} | all-to-all | bytes 557056 | tf_op jit(solution)/shard_map/all_to_all | solution.py:777
  56.2 5.2 %shard_map.83 = (f32[2048,128]{1,0:T(8,128)}, f32[2048,128]{1,0:T(8,128)}) custom-call(s32[8,16]{1,0:T(8,128)S(1)} %copy-done.2, s32[8]{0:T(128)S(1)} %stack.51.info, f32[32,17,1,128]{3,2,1,0:T(1,128)S(1)} %all_to_all.10.gathered, s32[1,256]{1,0:T(1,128)S(1)} %get-tuple-element.22.keys, f32[64,256]{1,0:T(8,128)S(1)} %get-tuple-element.28.inverses, ...), custom_call_target="tpu_custom_call" | custom-call | flops 1000000000 | bytes 4000000 | tf_op jit(solution)/shard_map/pallas_call | solution.py:779
Async XLA Ops:
  0.6 6.3 %copy-start = (f32[16,8,16,128]{3,2,1,0:T(8,128)S(1)}, f32[16,8,16,128]{3,2,1,0:T(8,128)}, u32[]{:S(2)}) copy-start(f32[16,8,16,128]{3,2,1,0:T(8,128)} %param.6) | copy-start | bytes 3145732
  2.6 4.3 %copy-start.4 = (s32[8,16]{1,0:T(8,128)S(1)}, s32[8,16]{1,0:T(8,128)}, u32[]{:S(2)}) copy-start(s32[8,16]{1,0:T(8,128)} %ids.3) | copy-start | bytes 1540
  2.6 4.3 %copy-start.2 = (s32[8,16]{1,0:T(8,128)S(1)}, s32[8,16]{1,0:T(8,128)}, u32[]{:S(2)}) copy-start(s32[8,16]{1,0:T(8,128)} %types.3) | copy-start | bytes 1540
  2.6 15.8 %collective-permute-start = (f32[512,128]{1,0:T(8,128)}, f32[512,128]{1,0:T(8,128)}, u32[]{:S(2)}, u32[]{:S(2)}) collective-permute-start(f32[512,128]{1,0:T(8,128)} %bitcast.9), channel_id=1, source_target_pairs={{0,4},{8,12},{16,20},{24,28},{4,0},{12,8},{20,16},{28,24},{1,5},{9... | collective-permute-start | bytes 786440 | tf_op jit(solution)/shard_map/ppermute | solution.py:673
  5.6 12.8 %collective-permute-start.1 = (f32[512,128]{1,0:T(8,128)}, f32[512,128]{1,0:T(8,128)}, u32[]{:S(2)}, u32[]{:S(2)}) collective-permute-start(f32[512,128]{1,0:T(8,128)} %bitcast.10), channel_id=1, source_target_pairs={{4,8},{12,16},{20,24},{8,4},{16,12},{24,20},{5,9},{13,17},{21,25},... | collective-permute-start | bytes 786440 | tf_op jit(solution)/shard_map/ppermute | solution.py:673
  8.9 15.5 %all-to-all-start = ((f32[32,10,1,128]{3,2,1,0:T(1,128)}), f32[32,10,1,128]{3,2,1,0:T(1,128)S(1)}, u32[]{:S(2)}, u32[]{:S(2)}) async-start(f32[32,10,1,128]{3,2,1,0:T(1,128)} %shard_map.77), calls=%async_computation | async-start | bytes 327680 | tf_op jit(solution)/shard_map/all_to_all | solution.py:718
  15.9 1.0 %copy-start.1 = (f32[8,128,128]{2,1,0:T(8,128)S(1)}, f32[8,128,128]{2,1,0:T(8,128)}, u32[]{:S(2)}) copy-start(f32[8,128,128]{2,1,0:T(8,128)} %library.1) | copy-start | bytes 1572868
  15.9 1.0 %copy-start.3 = (f32[2,128]{1,0:T(2,128)S(1)}, f32[2,128]{1,0:T(2,128)}, u32[]{:S(2)}) copy-start(f32[2,128]{1,0:T(2,128)} %strap.7) | copy-start | bytes 3076
  18.4 6.0 %copy-start.5 = (s32[8,256]{1,0:T(8,128)S(1)}, s32[8,256]{1,0:T(8,128)}, u32[]{:S(2)}) copy-start(s32[8,256]{1,0:T(8,128)} %constant.42.clone.maps) | copy-start | bytes 24580
  20.3 10.5 %collective-permute-start.2 = (f32[320,128]{1,0:T(8,128)}, f32[320,128]{1,0:T(8,128)S(1)}, u32[]{:S(2)}, u32[]{:S(2)}) collective-permute-start(f32[320,128]{1,0:T(8,128)} %get-tuple-element.23), channel_id=1, source_target_pairs={{0,1},{2,3},{1,0},{3,2},{4,5},{6,7},{5,4},{7,6},{8,9},{10,11},{9,8... | collective-permute-start | bytes 491528 | tf_op jit(solution)/shard_map/ppermute | solution.py:673
  20.5 10.2 %collective-permute-start.3 = (f32[320,128]{1,0:T(8,128)}, f32[320,128]{1,0:T(8,128)S(1)}, u32[]{:S(2)}, u32[]{:S(2)}) collective-permute-start(f32[320,128]{1,0:T(8,128)} %get-tuple-element.24), channel_id=1, source_target_pairs={{1,2},{2,1},{5,6},{6,5},{9,10},{10,9},{13,14},{14,13},{17,18},{18,... | collective-permute-start | bytes 491528 | tf_op jit(solution)/shard_map/ppermute | solution.py:673

commit v6 on v5

--- a/solution.py
+++ b/solution.py
@@ -11,7 +11,7 @@
 AGR = 4
 AGC = 4
 TILE = 8
-GROUP = 4
+GROUP = 8
 PANEL = 8
 F32 = jnp.float32
 BF16 = jnp.bfloat16
@@ -95,11 +95,13 @@
 
 
 def send_all(pay, whole):
+    rows = whole.reshape(pay.shape[1:])
+
     def copy(d, carry):
-        pay[d] = whole.reshape(pay.shape[1:])
+        pay[d] = rows
         return carry
 
-    lax.fori_loop(0, pay.shape[0], copy, 0)
+    lax.fori_loop(0, pay.shape[0], copy, 0, unroll=4)
 
 
 def blocks_kernel(dims, load, blocks):
@@ -275,7 +277,10 @@
             k = first + j
             at, within = k // 8, k % 8
             here = columns[j]
-            inverse = 1.0 / here[at][within : within + 1, :]
+            pivots = here[at][within : within + 1, :]
+            inverse = pl.reciprocal(pivots, approx=True)
+            inverse = inverse * (2.0 - pivots * inverse)
+            inverse = inverse * (2.0 - pivots * inverse)
             scaled = jnp.where(
                 lane[:1] == k, inverse, tiles[at][within : within + 1, :] * inverse
             )
@@ -561,7 +566,7 @@
     types, info,
     gathered, keys, inverses, cross, z, q, u, au, blocks, row_sums, strap,
     voltage, residual,
-    level, solved,
+    level, solved, voltage_rows, residual_rows, sems,
 ):
     sizings, rows, cols, nodes, count = dims
     n_row, n_col = mesh_dims
@@ -611,30 +616,44 @@
     north, east_strap = strap[0:1, :], strap[1:2, :]
     couple = 2.0 * north + 2.0 * east_strap
 
+    span = sizings * cols
+    flat_voltage = voltage_rows.reshape(rows * span, nodes)
+    flat_residual = residual_rows.reshape(rows * span, nodes)
+
+    def value(er, ec):
+        at = (er * wide + ec) * sizings
+        return level[pl.ds(pl.multiple_of(at, sizings), sizings), :]
+
+    def copies(r):
+        return [
+            pltpu.make_async_copy(buffer.at[r], out.at[:, r], sems.at[i, r])
+            for i, (buffer, out) in enumerate(((voltage_rows, voltage), (residual_rows, residual)))
+        ]
+
     def step(r, carry):
+        line = [value(r + 2, 1), value(r + 2, 2)]
         for c in range(cols):
-            b = r * cols + c
-            own = pl.ds(pl.multiple_of(b * sizings, sizings), sizings)
-
-            def value(dr, dc):
-                e = (r + 2 + dr) * wide + c + 2 + dc
-                return level[pl.ds(pl.multiple_of(e * sizings, sizings), sizings), :]
-
-            here = value(0, 0)
+            line.append(value(r + 2, c + 3))
+            here = line[c + 1]
+            own = pl.ds(pl.multiple_of((r * cols + c) * sizings, sizings), sizings)
             lift = (
                 (row_sums[pl.ds(types[r, c], 1), :] + couple) * here
-                - north * (value(-1, 0) + value(1, 0))
-                - east_strap * (value(0, -1) + value(0, 1))
+                - north * (value(r + 1, c + 2) + value(r + 3, c + 2))
+                - east_strap * (line[c] + line[c + 2])
             )
-            voltage[pl.ds(b, sizings, stride=rows * cols), :] = alpha * z[own, :] + gamma * (
-                u[own, :] + here
-            )
-            residual[pl.ds(b, sizings, stride=rows * cols), :] = (
+            to = pl.ds(r * span + c, sizings, stride=cols)
+            flat_voltage[to, :] = alpha * z[own, :] + gamma * (u[own, :] + here)
+            flat_residual[to, :] = (
                 blocks[own, :] - alpha * q[own, :] - gamma * (au[own, :] + lift)
             )
+        for copy in copies(r):
+            copy.start()
         return carry
 
     lax.fori_loop(0, rows, step, 0)
+    for r in range(rows):
+        for copy in copies(r):
+            copy.wait()
 
 
 def ring_maps(rows, cols, count):
@@ -659,7 +678,7 @@
     return pl.pallas_call(
         kernel,
         in_specs=in_specs,
-        out_specs=jax.tree.map(lambda _: VMEM, out_shape),
+        out_specs=more.pop("out_specs", [VMEM] * len(out_shape)),
         out_shape=out_shape,
         scratch_shapes=scratch,
         compiler_params=pltpu.CompilerParams(vmem_limit_bytes=megabytes * 1024 * 1024),
@@ -775,19 +794,21 @@
         stacked, low, row_sums, strap_conductance,
     )
     gathered = lax.all_to_all(pay, ("row", "col"), 0, 0)
-    out = shape((sizings * rows * cols, nodes), F32)
-    voltage, residual = call(
+    out = shape(load_currents.shape, F32)
+    row_buffer = pltpu.VMEM((rows, sizings, cols, nodes), F32)
+    return call(
         functools.partial(last_kernel, dims, mesh_dims),
         [SMEM] * 2 + [VMEM] * 11,
         [out, out],
-        [big, pltpu.VMEM(coarse_shape, F32)],
+        [big, pltpu.VMEM(coarse_shape, F32), row_buffer, row_buffer]
+        + [pltpu.SemaphoreType.DMA((2, rows))],
         1_000_000_000,
         8 if count <= 64 else 32,
+        out_specs=[pl.BlockSpec(memory_space=pl.ANY)] * 2,
     )(
         block_types, info,
         gathered, keys, inverses, cross, z, q, u, au, blocks, row_sums, strap_conductance,
     )
-    return voltage.reshape(load_currents.shape), residual.reshape(load_currents.shape)
 
 
 def solution(mesh):

time: 61.9 us -> 58.8 us (0.950)
  Pallas kernels: 27.7 us -> 24.8 us
    pallas_call x1, Pallas kernels: 5.22 us -> 3.84 us  [on_device(): call(functools.partial(last_kernel, dims, mesh_dims), [SMEM] * 2 + [VMEM]...]
    pallas_call x1, Pallas kernels: 10.3 us -> 9.07 us  [on_device(): call(functools.partial(middle_kernel, dims), [SMEM] * 3 + [VMEM] * 11, [o...]
where the time goes in v6:
time: 58.8 us; the launch traced here: 58.5 us
  Pallas kernels  24.8 us (42%)
  blocking collectives  15.2 us (26%)
  starting transfers between devices  12.2 us (21%)
  waiting for transfers between devices  3.21 us (5%)
  local copies, waits for them, and re-layouts  2.43 us (4%)
  between operations  0.76 us (1%)
    all_to_all x1, blocking collectives, on_device(): gathered = lax.all_to_all(pay, ('row', 'col'), 0, 0)  15.2 us
    pallas_call x1, Pallas kernels, on_device(): call(functools.partial(middle_kernel, dims), [SMEM] * 3 + [VMEM] * 11, [o...  9.07 us
    all_to_all x1, starting transfers between devices, on_device(): gathered = lax.all_to_all(pay, ('row', 'col'), 0, 0)  6.93 us
    pallas_call x1, Pallas kernels, on_device(): call(functools.partial(coarse_kernel, dims, mesh_dims, kinds), [SMEM] + [...  6.12 us
    ppermute x4, starting transfers between devices, swap(): return lax.ppermute(payload, axis, pairs + [(j, i) for i, j in pairs])  5.23 us
    pallas_call x1, Pallas kernels, on_device(): call(functools.partial(last_kernel, dims, mesh_dims), [SMEM] * 2 + [VMEM]...  3.84 us
    all_to_all x1, waiting for transfers between devices, on_device(): gathered = lax.all_to_all(pay, ('row', 'col'), 0, 0)  3.2 us
    dynamic_slice x1, local copies, waits for them, and re-layouts, on_device(): lax.dynamic_slice_in_dim(load_currents, rows - 2 - begin, 2, axis=1)  1.94 us
  transfers between devices with their start and end apart: 5, of which 1 were waited for; matrix products, arithmetic and copies ran while one was open for 0% of the time, Pallas kernels for 20%

profile of v6, /device:TPU:0, one launch (start us, length us, event | category | flops | bytes accessed | tf_op | source)
XLA Modules:
  0.0 58.5 jit_solution(13900454834736127092)
XLA Ops:
  0.6 0.0 copy-start
  0.7 1.9 %constant_dynamic-slice_fusion = (f32[16,2,16,128]{3,2,1,0:T(8,128)}, f32[16,2,16,128]{3,2,1,0:T(8,128)}) fusion(f32[16,8,16,128]{3,2,1,0:T(8,128)} %param.6, s32[]{:T(128)S(6)} %select_n.22, s32[]{:T(128)S(6)} %select_n.21), kind=kLoop, calls=%fused_computation | loop fusion | bytes 1048584 | tf_op jit(solution)/shard_map/dynamic_slice | solution.py:723
  2.6 0.0 copy-start.4
  2.6 0.0 copy-start.2
  2.6 3.0 %collective-permute-start = (f32[512,128]{1,0:T(8,128)}, f32[512,128]{1,0:T(8,128)}, u32[]{:S(2)}, u32[]{:S(2)}) collective-permute-start(f32[512,128]{1,0:T(8,128)} %bitcast.9), channel_id=1, source_target_pairs={{0,4},{8,12},{16,20},{24,28},{4,0},{12,8},{20,16},{28,24},{1,5},{9... | collective-permute-start | bytes 786440 | tf_op jit(solution)/shard_map/ppermute | solution.py:692
  5.6 1.4 %collective-permute-start.1 = (f32[512,128]{1,0:T(8,128)}, f32[512,128]{1,0:T(8,128)}, u32[]{:S(2)}, u32[]{:S(2)}) collective-permute-start(f32[512,128]{1,0:T(8,128)} %bitcast.10), channel_id=1, source_target_pairs={{4,8},{12,16},{20,24},{8,4},{16,12},{24,20},{5,9},{13,17},{21,25},... | collective-permute-start | bytes 786440 | tf_op jit(solution)/shard_map/ppermute | solution.py:692
  6.9 0.0 copy-done
  6.9 0.0 copy-done.4
  6.9 0.0 copy-done.2
  6.9 1.8 %shard_map.77 = f32[32,10,1,128]{3,2,1,0:T(1,128)} custom-call(s32[8,16]{1,0:T(8,128)S(1)} %copy-done.4, s32[8,16]{1,0:T(8,128)S(1)} %copy-done.2, s32[8,16]{1,0:T(8,128)S(1)} %copy-done.4, f32[2048,128]{1,0:T(8,128)S(1)} %bitcast.11), custom_call_target="tpu_custom_call" | custom-call | flops 20000000000 | bytes 4000000 | tf_op jit(solution)/shard_map/pallas_call | solution.py:729
  8.8 6.9 %all-to-all-start = ((f32[32,10,1,128]{3,2,1,0:T(1,128)}), f32[32,10,1,128]{3,2,1,0:T(1,128)S(1)}, u32[]{:S(2)}, u32[]{:S(2)}) async-start(f32[32,10,1,128]{3,2,1,0:T(1,128)} %shard_map.77), calls=%async_computation | async-start | bytes 327680 | tf_op jit(solution)/shard_map/all_to_all | solution.py:737
  15.7 0.1 stack.51.info
  15.8 0.0 copy-start.1
  15.8 0.0 copy-start.3
  15.8 0.7 %shard_map.80.blocks = f32[2048,128]{1,0:T(8,128)S(1)} custom-call(f32[2048,128]{1,0:T(8,128)S(1)} %bitcast.12), custom_call_target="tpu_custom_call" | custom-call | flops 1000000 | bytes 4000000 | tf_op jit(solution)/shard_map/pallas_call | solution.py:750
  16.5 0.4 copy-done.1
  16.9 0.0 copy-done.3
  16.9 1.4 %shard_map.78 = (bf16[8,256,256]{2,1,0:T(8,128)(2,1)S(1)}, bf16[8,128,256]{2,1,0:T(8,128)(2,1)S(1)}, f32[8,128]{1,0:T(8,128)S(1)}) custom-call(f32[8,128,128]{2,1,0:T(8,128)S(1)} %copy-done.1, f32[2,128]{1,0:T(2,128)S(1)} %copy-done.3), custom_call_target="tpu_custom_call" | custom-call | flops 1000000 | bytes 4000000 | tf_op jit(solution)/shard_map/pallas_call | solution.py:738
  18.3 0.0 collective-permute-done.row_first
  18.3 0.0 collective-permute-done.1.row_second
  18.3 0.0 copy-start.5
  18.3 1.9 %shard_map.81 = (f32[320,128]{1,0:T(8,128)}, f32[320,128]{1,0:T(8,128)}) custom-call(s32[8]{0:T(128)S(1)} %stack.51.info, f32[2048,128]{1,0:T(8,128)S(1)} %shard_map.80.blocks, f32[512,128]{1,0:T(8,128)} %collective-permute-done.row_first, f32[512,128]{1,0:T(8,128)} %collective-permute-done.1.row_second, f32[8,128]{1,0:T(8,128)S(1)} %get-tuple-element.17.row_sums), custom_call_target="tpu_custom_call" | custom-call | flops 40000000000 | bytes 4000000 | tf_op jit(solution)/shard_map/pallas_call | solution.py:755
  20.2 0.3 collective-permute-start.2
  20.4 0.7 %collective-permute-start.3 = (f32[320,128]{1,0:T(8,128)}, f32[320,128]{1,0:T(8,128)S(1)}, u32[]{:S(2)}, u32[]{:S(2)}) collective-permute-start(f32[320,128]{1,0:T(8,128)} %get-tuple-element.22), channel_id=1, source_target_pairs={{1,2},{2,1},{5,6},{6,5},{9,10},{10,9},{13,14},{14,13},{17,18},{18,... | collective-permute-start | bytes 491528 | tf_op jit(solution)/shard_map/ppermute | solution.py:692
  21.1 3.2 %all-to-all-done.gathered = f32[32,10,1,128]{3,2,1,0:T(1,128)S(1)} async-done(((f32[32,10,1,128]{3,2,1,0:T(1,128)}), f32[32,10,1,128]{3,2,1,0:T(1,128)S(1)}, u32[]{:S(2)}, u32[]{:S(2)}) %all-to-all-start) | async-done | bytes 163872 | tf_op jit(solution)/shard_map/all_to_all | solution.py:737
  24.3 0.0 copy-done.5
  24.3 6.1 %shard_map.79 = (f32[64,256]{1,0:T(8,128)S(1)}, f32[4,64,64]{2,1,0:T(8,128)S(1)}, f32[6,16,64]{2,1,0:T(8,128)S(1)}, s32[8,384]{1,0:T(8,128)S(1)}, s32[1,256]{1,0:T(1,128)S(1)}) custom-call(s32[8]{0:T(128)S(1)} %stack.51.info, s32[8,256]{1,0:T(8,128)S(1)} %copy-done.5, f32[32,10,1,128]{3,2,1,0:T(1,128)S(1)} %all-to-all-done.gathered, ...), custom_call_target="tpu_custom_call" | custom-call | flops 10000000000 | bytes 4000000 | tf_op jit(solution)/shard_map/pallas_call | solution.py:770
  30.4 0.0 collective-permute-done.2.col_first
  30.4 0.0 collective-permute-done.3.col_second
  30.4 9.1 %shard_map.82 = (f32[2048,128]{1,0:T(8,128)S(1)}, f32[2048,128]{1,0:T(8,128)S(1)}, f32[2048,128]{1,0:T(8,128)S(1)}, f32[2048,128]{1,0:T(8,128)S(1)}, f32[32,17,1,128]{3,2,1,0:T(1,128)S(1)}) custom-call(s32[8,384]{1,0:T(8,128)S(1)} %get-tuple-element.18.plan, s32[8]{0:T(128)S(1)} %stack.51.info, s32[8,16]{1,0:T(8,128)S(1)} %copy-done.4, ...), custom_call_target="tpu_custom_call" | custom-call | flops 1000000000 | bytes 4000000 | tf_op jit(solution)/shard_map/pallas_call | solution.py:784
  39.5 15.2 %all_to_all.10.gathered = f32[32,17,1,128]{3,2,1,0:T(1,128)S(1)} all-to-all(f32[32,17,1,128]{3,2,1,0:T(1,128)S(1)} %get-tuple-element.25), channel_id=1, replica_groups=mesh['row'=8,'col'=4] {'row','col'}, dimensions={0} | all-to-all | bytes 557056 | tf_op jit(solution)/shard_map/all_to_all | solution.py:796
  54.7 3.8 %shard_map.83 = (f32[16,8,16,128]{3,2,1,0:T(8,128)}, f32[16,8,16,128]{3,2,1,0:T(8,128)}) custom-call(s32[8,16]{1,0:T(8,128)S(1)} %copy-done.2, s32[8]{0:T(128)S(1)} %stack.51.info, f32[32,17,1,128]{3,2,1,0:T(1,128)S(1)} %all_to_all.10.gathered, s32[1,256]{1,0:T(1,128)S(1)} %get-tuple-element.20.keys, f32[64,256]{1,0:T(8,128)S(1)} %get-tuple-element.26.inverses, ...), custom_call_target="tpu_custom_call" | custom-call | flops 1000000000 | bytes 4000000 | tf_op jit(solution)/shard_map/pallas_call | solution.py:799
Async XLA Ops:
  0.6 6.3 %copy-start = (f32[16,8,16,128]{3,2,1,0:T(8,128)S(1)}, f32[16,8,16,128]{3,2,1,0:T(8,128)}, u32[]{:S(2)}) copy-start(f32[16,8,16,128]{3,2,1,0:T(8,128)} %param.6) | copy-start | bytes 3145732
  2.6 4.3 %copy-start.4 = (s32[8,16]{1,0:T(8,128)S(1)}, s32[8,16]{1,0:T(8,128)}, u32[]{:S(2)}) copy-start(s32[8,16]{1,0:T(8,128)} %ids.3) | copy-start | bytes 1540
  2.6 4.3 %copy-start.2 = (s32[8,16]{1,0:T(8,128)S(1)}, s32[8,16]{1,0:T(8,128)}, u32[]{:S(2)}) copy-start(s32[8,16]{1,0:T(8,128)} %types.3) | copy-start | bytes 1540
  2.6 15.7 %collective-permute-start = (f32[512,128]{1,0:T(8,128)}, f32[512,128]{1,0:T(8,128)}, u32[]{:S(2)}, u32[]{:S(2)}) collective-permute-start(f32[512,128]{1,0:T(8,128)} %bitcast.9), channel_id=1, source_target_pairs={{0,4},{8,12},{16,20},{24,28},{4,0},{12,8},{20,16},{28,24},{1,5},{9... | collective-permute-start | bytes 786440 | tf_op jit(solution)/shard_map/ppermute | solution.py:692
  5.6 12.7 %collective-permute-start.1 = (f32[512,128]{1,0:T(8,128)}, f32[512,128]{1,0:T(8,128)}, u32[]{:S(2)}, u32[]{:S(2)}) collective-permute-start(f32[512,128]{1,0:T(8,128)} %bitcast.10), channel_id=1, source_target_pairs={{4,8},{12,16},{20,24},{8,4},{16,12},{24,20},{5,9},{13,17},{21,25},... | collective-permute-start | bytes 786440 | tf_op jit(solution)/shard_map/ppermute | solution.py:692
  8.8 15.5 %all-to-all-start = ((f32[32,10,1,128]{3,2,1,0:T(1,128)}), f32[32,10,1,128]{3,2,1,0:T(1,128)S(1)}, u32[]{:S(2)}, u32[]{:S(2)}) async-start(f32[32,10,1,128]{3,2,1,0:T(1,128)} %shard_map.77), calls=%async_computation | async-start | bytes 327680 | tf_op jit(solution)/shard_map/all_to_all | solution.py:737
  15.8 1.0 %copy-start.1 = (f32[8,128,128]{2,1,0:T(8,128)S(1)}, f32[8,128,128]{2,1,0:T(8,128)}, u32[]{:S(2)}) copy-start(f32[8,128,128]{2,1,0:T(8,128)} %library.1) | copy-start | bytes 1572868
  15.8 1.0 %copy-start.3 = (f32[2,128]{1,0:T(2,128)S(1)}, f32[2,128]{1,0:T(2,128)}, u32[]{:S(2)}) copy-start(f32[2,128]{1,0:T(2,128)} %strap.7) | copy-start | bytes 3076
  18.3 6.0 %copy-start.5 = (s32[8,256]{1,0:T(8,128)S(1)}, s32[8,256]{1,0:T(8,128)}, u32[]{:S(2)}) copy-start(s32[8,256]{1,0:T(8,128)} %constant.42.clone.maps) | copy-start | bytes 24580
  20.2 10.2 %collective-permute-start.2 = (f32[320,128]{1,0:T(8,128)}, f32[320,128]{1,0:T(8,128)S(1)}, u32[]{:S(2)}, u32[]{:S(2)}) collective-permute-start(f32[320,128]{1,0:T(8,128)} %get-tuple-element.21), channel_id=1, source_target_pairs={{0,1},{2,3},{1,0},{3,2},{4,5},{6,7},{5,4},{7,6},{8,9},{10,11},{9,8... | collective-permute-start | bytes 491528 | tf_op jit(solution)/shard_map/ppermute | solution.py:692
  20.4 10.0 %collective-permute-start.3 = (f32[320,128]{1,0:T(8,128)}, f32[320,128]{1,0:T(8,128)S(1)}, u32[]{:S(2)}, u32[]{:S(2)}) collective-permute-start(f32[320,128]{1,0:T(8,128)} %get-tuple-element.22), channel_id=1, source_target_pairs={{1,2},{2,1},{5,6},{6,5},{9,10},{10,9},{13,14},{14,13},{17,18},{18,... | collective-permute-start | bytes 491528 | tf_op jit(solution)/shard_map/ppermute | solution.py:692

commit v7 on v6

--- a/solution.py
+++ b/solution.py
@@ -262,38 +262,51 @@
     tiles = [ref[i * 8 : (i + 1) * 8, :] for i in range(many)]
 
     def column(tile, k):
-        parts = []
-        for base in range(0, width, 128):
-            part = jnp.broadcast_to(tile[:, base + k : base + k + 1], (8, 128))
-            for j in range(1, fold):
-                at = base + j * count + k
-                part = jnp.where(tile_lane >= j * count, tile[:, at : at + 1], part)
-            parts.append(part)
-        return jnp.concatenate(parts, axis=1)
+        place = tile_lane // count * count + k
+        return jnp.concatenate(
+            [
+                jnp.take_along_axis(tile[:, base : base + 128], place, axis=1)
+                for base in range(0, width, 128)
+            ],
+            axis=1,
+        )
 
     for first in range(0, count, PANEL):
         columns = [[column(t, first + j) for t in tiles] for j in range(PANEL)]
-        for j in range(PANEL):
+        for j in range(0, PANEL, 2):
             k = first + j
-            at, within = k // 8, k % 8
-            here = columns[j]
-            pivots = here[at][within : within + 1, :]
-            inverse = pl.reciprocal(pivots, approx=True)
-            inverse = inverse * (2.0 - pivots * inverse)
-            inverse = inverse * (2.0 - pivots * inverse)
-            scaled = jnp.where(
-                lane[:1] == k, inverse, tiles[at][within : within + 1, :] * inverse
+            at, one, two = k // 8, slice(k % 8, k % 8 + 1), slice(k % 8 + 1, k % 8 + 2)
+            left, right = columns[j], columns[j + 1]
+            a, b, c, d = left[at][one], right[at][one], left[at][two], right[at][two]
+            det = a * d - b * c
+            scale = pl.reciprocal(det, approx=True)
+            scale = scale * (2.0 - det * scale)
+            scale = scale * (2.0 - det * scale)
+            a, b, c, d = a * scale, b * scale, c * scale, d * scale
+
+            def pivoted(upper, lower):
+                return d * upper - b * lower, a * lower - c * upper
+
+            def update(old, i, upper, lower):
+                new = old - left[i] * upper - right[i] * lower
+                if i == at:
+                    new = jnp.where(row == k % 8, upper, new)
+                    new = jnp.where(row == k % 8 + 1, lower, new)
+                return new
+
+            upper, lower = tiles[at][one], tiles[at][two]
+            on, after = lane[:1] == k, lane[:1] == k + 1
+            upper, lower = pivoted(
+                jnp.where(on, 1.0, jnp.where(after, 0.0, upper)),
+                jnp.where(on, 0.0, jnp.where(after, 1.0, lower)),
             )
-            pivot = row == within
+            cleared = (lane == k) | (lane == k + 1)
             for i in range(many):
-                new = jnp.where(lane == k, 0.0, tiles[i]) - here[i] * scaled
-                tiles[i] = jnp.where(pivot, scaled, new) if i == at else new
-            for later in range(j + 1, PANEL):
-                other = columns[later]
-                factor = other[at][within : within + 1, :] * inverse
+                tiles[i] = update(jnp.where(cleared, 0.0, tiles[i]), i, upper, lower)
+            for other in columns[j + 2 :]:
+                upper, lower = pivoted(other[at][one], other[at][two])
                 for i in range(many):
-                    new = other[i] - here[i] * factor
-                    other[i] = jnp.where(pivot, factor, new) if i == at else new
+                    other[i] = update(other[i], i, upper, lower)
     for i in range(many):
         ref[i * 8 : (i + 1) * 8, :] = tiles[i]
 
@@ -388,18 +401,42 @@
     return sums, solved
 
 
-def spread(solved, col, keys, out, count, sizings, nodes, many):
-    three = jnp.concatenate([solved[col], solved[col + 1], solved[col + 2]], axis=1)
+def spread(solved, info, keys, ids, out, table, dims, reach):
+    sizings, rows, cols, nodes, count = dims
+    wide = cols + 4
+    col = info[0]
+    own = solved[col + 1]
+    for a in range(count):
+        table[a * sizings : (a + 1) * sizings, :] = jnp.broadcast_to(
+            own[:, a : a + 1], (sizings, nodes)
+        )
+    table[count * sizings :, :] = jnp.zeros((sizings, nodes), F32)
+
+    def row(er, carry):
+        for ec in range(2, cols + 2):
+            e = er * wide + ec
+            key = ids[0, e]
+            place = jnp.where(key < 0, count, key - count) * sizings
+            to = pl.ds(pl.multiple_of(e * sizings, sizings), sizings)
+            out[to, :] = table[pl.ds(pl.multiple_of(place, sizings), sizings), :]
+        return carry
+
+    lax.fori_loop(2 - reach, rows + 2 + reach, row, 0)
+
+    three = jnp.concatenate([solved[col], own, solved[col + 2]], axis=1)
     hot = (iota((3 * count, keys.shape[1]), 0) == keys[...]).astype(F32).astype(BF16)
     parts = jnp.concatenate(split3(three), axis=0)
     values = jnp.dot(parts, hot, preferred_element_type=F32)
     values = (
         values[2 * sizings : 3 * sizings] + values[sizings : 2 * sizings] + values[:sizings]
     )
-    for e in range(many):
-        out[e * sizings : (e + 1) * sizings, :] = jnp.broadcast_to(
-            values[:, e : e + 1], (sizings, nodes)
-        )
+    for over in range(1, reach + 1):
+        for ec in (2 - over, cols + 1 + over):
+            for er in range(2 - reach + over, rows + 2 + reach - over):
+                e = er * wide + ec
+                out[e * sizings : (e + 1) * sizings, :] = jnp.broadcast_to(
+                    values[:, e : e + 1], (sizings, nodes)
+                )
 
 
 def coarse_kernel(
@@ -425,11 +462,11 @@
 
 def middle_kernel(
     dims,
-    plan, info, ids,
+    plan, info, ids, near_ids,
     solved, keys, blocks, row_first, row_second, col_first, col_second,
     stacked, low, row_sums, strap,
     z_out, q_out, u_out, au_out, pay,
-    field, level, z, bz, q, u, bu,
+    field, level, z, bz, q, u, bu, table,
 ):
     sizings, rows, cols, nodes, count = dims
     wide = cols + 4
@@ -461,7 +498,7 @@
     field[many * sizings :, :] = jnp.zeros((sizings, nodes), F32)
     level[many * sizings :, :] = jnp.zeros((sizings, nodes), F32)
     q[many * sizings :, :] = jnp.zeros((sizings, nodes), F32)
-    spread(solved, info[0], keys, level, count, sizings, nodes, many)
+    spread(solved, info, keys, near_ids, level, table, dims, 2)
 
     def store_z(kind, places, out):
         sums = row_sums[pl.ds(kind, 1), :]
@@ -563,10 +600,10 @@
 
 def last_kernel(
     dims, mesh_dims,
-    types, info,
+    types, info, near_ids,
     gathered, keys, inverses, cross, z, q, u, au, blocks, row_sums, strap,
     voltage, residual,
-    level, solved, voltage_rows, residual_rows, sems,
+    level, solved, table, voltage_rows, residual_rows, sems,
 ):
     sizings, rows, cols, nodes, count = dims
     n_row, n_col = mesh_dims
@@ -592,7 +629,7 @@
                 before, cross[g - 1], precision=HIGHEST, preferred_element_type=F32
             )
         before = one
-    spread(solved, info[0], keys, level, count, sizings, nodes, many)
+    spread(solved, info, keys, near_ids, level, table, dims, 1)
 
     dots = gathered[0, 2 * height]
     for d in range(1, n_row * n_col):
@@ -764,6 +801,7 @@
 
     big = pltpu.VMEM(((many + 1) * sizings, nodes), F32)
     coarse_shape = (n_col + 2, sizings, count)
+    table = pltpu.VMEM(((count + 1) * sizings, nodes), F32)
     maps = ring_maps(rows, cols, count)
     longest = int(max(maps[1].sum(), maps[2].sum())) + (TILE - 1) * kinds + GROUP * TILE
     longest = -(-longest // 128) * 128
@@ -783,13 +821,13 @@
     )(info, jnp.asarray(maps), gathered, row_sums, strap_conductance)
     z, q, u, au, pay = call(
         functools.partial(middle_kernel, dims),
-        [SMEM] * 3 + [VMEM] * 11,
+        [SMEM] * 4 + [VMEM] * 11,
         [own] * 4 + [shape((n_dev, 2 * height + 1, 1, 128), F32)],
-        [big] * 7,
+        [big] * 7 + [table],
         1_000_000_000,
         20 if count <= 64 else 48,
     )(
-        plan, info, aggregate_map,
+        plan, info, aggregate_map, keys,
         solved, keys, blocks, row_first, row_second, col_first, col_second,
         stacked, low, row_sums, strap_conductance,
     )
@@ -798,15 +836,15 @@
     row_buffer = pltpu.VMEM((rows, sizings, cols, nodes), F32)
     return call(
         functools.partial(last_kernel, dims, mesh_dims),
-        [SMEM] * 2 + [VMEM] * 11,
+        [SMEM] * 3 + [VMEM] * 11,
         [out, out],
-        [big, pltpu.VMEM(coarse_shape, F32), row_buffer, row_buffer]
+        [big, pltpu.VMEM(coarse_shape, F32), table, row_buffer, row_buffer]
         + [pltpu.SemaphoreType.DMA((2, rows))],
         1_000_000_000,
         8 if count <= 64 else 32,
         out_specs=[pl.BlockSpec(memory_space=pl.ANY)] * 2,
     )(
-        block_types, info,
+        block_types, info, keys,
         gathered, keys, inverses, cross, z, q, u, au, blocks, row_sums, strap_conductance,
     )
 

time: 58.8 us -> 57.4 us (0.976)
  Pallas kernels: 24.8 us -> 23.7 us
    pallas_call x1, Pallas kernels: 6.12 us -> 4.81 us  [on_device(): call(functools.partial(coarse_kernel, dims, mesh_dims, kinds), [SMEM] + [...]
  transfers between devices with their start and end apart: 5 -> 5, of which waited for: 1 -> 1; matrix products, arithmetic and copies ran while one was open for 0% -> 0% of each run, Pallas kernels for 20% -> 18%
where the time goes in v7:
time: 57.4 us; the launch traced here: 57.2 us
  Pallas kernels  23.7 us (41%)
  blocking collectives  15 us (26%)
  starting transfers between devices  12.2 us (21%)
  waiting for transfers between devices  3.21 us (6%)
  local copies, waits for them, and re-layouts  2.43 us (4%)
  between operations  0.76 us (1%)
    all_to_all x1, blocking collectives, on_device(): gathered = lax.all_to_all(pay, ('row', 'col'), 0, 0)  15 us
    pallas_call x1, Pallas kernels, on_device(): call(functools.partial(middle_kernel, dims), [SMEM] * 4 + [VMEM] * 11, [o...  9.46 us
    all_to_all x1, starting transfers between devices, on_device(): gathered = lax.all_to_all(pay, ('row', 'col'), 0, 0)  6.93 us
    ppermute x4, starting transfers between devices, swap(): return lax.ppermute(payload, axis, pairs + [(j, i) for i, j in pairs])  5.23 us
    pallas_call x1, Pallas kernels, on_device(): call(functools.partial(coarse_kernel, dims, mesh_dims, kinds), [SMEM] + [...  4.81 us
    pallas_call x1, Pallas kernels, on_device(): call(functools.partial(last_kernel, dims, mesh_dims), [SMEM] * 3 + [VMEM]...  3.65 us
    all_to_all x1, waiting for transfers between devices, on_device(): gathered = lax.all_to_all(pay, ('row', 'col'), 0, 0)  3.2 us
    dynamic_slice x1, local copies, waits for them, and re-layouts, on_device(): lax.dynamic_slice_in_dim(load_currents, rows - 2 - begin, 2, axis=1)  1.94 us
  transfers between devices with their start and end apart: 5, of which 1 were waited for; matrix products, arithmetic and copies ran while one was open for 0% of the time, Pallas kernels for 18%

profile of v7, /device:TPU:0, one launch (start us, length us, event | category | flops | bytes accessed | tf_op | source)
XLA Modules:
  0.0 57.2 jit_solution(16490677534496987021)
XLA Ops:
  0.6 0.0 copy-start
  0.7 1.9 %constant_dynamic-slice_fusion = (f32[16,2,16,128]{3,2,1,0:T(8,128)}, f32[16,2,16,128]{3,2,1,0:T(8,128)}) fusion(f32[16,8,16,128]{3,2,1,0:T(8,128)} %param.6, s32[]{:T(128)S(6)} %select_n.22, s32[]{:T(128)S(6)} %select_n.21), kind=kLoop, calls=%fused_computation | loop fusion | bytes 1048584 | tf_op jit(solution)/shard_map/dynamic_slice | solution.py:760
  2.6 0.0 copy-start.4
  2.6 0.0 copy-start.2
  2.6 3.0 %collective-permute-start = (f32[512,128]{1,0:T(8,128)}, f32[512,128]{1,0:T(8,128)}, u32[]{:S(2)}, u32[]{:S(2)}) collective-permute-start(f32[512,128]{1,0:T(8,128)} %bitcast.9), channel_id=1, source_target_pairs={{0,4},{8,12},{16,20},{24,28},{4,0},{12,8},{20,16},{28,24},{1,5},{9... | collective-permute-start | bytes 786440 | tf_op jit(solution)/shard_map/ppermute | solution.py:729
  5.6 1.4 %collective-permute-start.1 = (f32[512,128]{1,0:T(8,128)}, f32[512,128]{1,0:T(8,128)}, u32[]{:S(2)}, u32[]{:S(2)}) collective-permute-start(f32[512,128]{1,0:T(8,128)} %bitcast.10), channel_id=1, source_target_pairs={{4,8},{12,16},{20,24},{8,4},{16,12},{24,20},{5,9},{13,17},{21,25},... | collective-permute-start | bytes 786440 | tf_op jit(solution)/shard_map/ppermute | solution.py:729
  6.9 0.0 copy-done
  6.9 0.0 copy-done.4
  6.9 0.0 copy-done.2
  6.9 1.8 %shard_map.77 = f32[32,10,1,128]{3,2,1,0:T(1,128)} custom-call(s32[8,16]{1,0:T(8,128)S(1)} %copy-done.4, s32[8,16]{1,0:T(8,128)S(1)} %copy-done.2, s32[8,16]{1,0:T(8,128)S(1)} %copy-done.4, f32[2048,128]{1,0:T(8,128)S(1)} %bitcast.11), custom_call_target="tpu_custom_call" | custom-call | flops 20000000000 | bytes 4000000 | tf_op jit(solution)/shard_map/pallas_call | solution.py:766
  8.8 6.9 %all-to-all-start = ((f32[32,10,1,128]{3,2,1,0:T(1,128)}), f32[32,10,1,128]{3,2,1,0:T(1,128)S(1)}, u32[]{:S(2)}, u32[]{:S(2)}) async-start(f32[32,10,1,128]{3,2,1,0:T(1,128)} %shard_map.77), calls=%async_computation | async-start | bytes 327680 | tf_op jit(solution)/shard_map/all_to_all | solution.py:774
  15.7 0.1 stack.51.info
  15.8 0.0 copy-start.1
  15.8 0.0 copy-start.3
  15.8 0.7 %shard_map.80.blocks = f32[2048,128]{1,0:T(8,128)S(1)} custom-call(f32[2048,128]{1,0:T(8,128)S(1)} %bitcast.12), custom_call_target="tpu_custom_call" | custom-call | flops 1000000 | bytes 4000000 | tf_op jit(solution)/shard_map/pallas_call | solution.py:787
  16.5 0.4 copy-done.1
  16.9 0.0 copy-done.3
  16.9 1.4 %shard_map.78 = (bf16[8,256,256]{2,1,0:T(8,128)(2,1)S(1)}, bf16[8,128,256]{2,1,0:T(8,128)(2,1)S(1)}, f32[8,128]{1,0:T(8,128)S(1)}) custom-call(f32[8,128,128]{2,1,0:T(8,128)S(1)} %copy-done.1, f32[2,128]{1,0:T(2,128)S(1)} %copy-done.3), custom_call_target="tpu_custom_call" | custom-call | flops 1000000 | bytes 4000000 | tf_op jit(solution)/shard_map/pallas_call | solution.py:775
  18.3 0.0 collective-permute-done.row_first
  18.3 0.0 collective-permute-done.1.row_second
  18.3 0.0 copy-start.5
  18.3 1.9 %shard_map.81 = (f32[320,128]{1,0:T(8,128)}, f32[320,128]{1,0:T(8,128)}) custom-call(s32[8]{0:T(128)S(1)} %stack.51.info, f32[2048,128]{1,0:T(8,128)S(1)} %shard_map.80.blocks, f32[512,128]{1,0:T(8,128)} %collective-permute-done.row_first, f32[512,128]{1,0:T(8,128)} %collective-permute-done.1.row_second, f32[8,128]{1,0:T(8,128)S(1)} %get-tuple-element.17.row_sums), custom_call_target="tpu_custom_call" | custom-call | flops 40000000000 | bytes 4000000 | tf_op jit(solution)/shard_map/pallas_call | solution.py:792
  20.2 0.3 collective-permute-start.2
  20.4 0.7 %collective-permute-start.3 = (f32[320,128]{1,0:T(8,128)}, f32[320,128]{1,0:T(8,128)S(1)}, u32[]{:S(2)}, u32[]{:S(2)}) collective-permute-start(f32[320,128]{1,0:T(8,128)} %get-tuple-element.22), channel_id=1, source_target_pairs={{1,2},{2,1},{5,6},{6,5},{9,10},{10,9},{13,14},{14,13},{17,18},{18,... | collective-permute-start | bytes 491528 | tf_op jit(solution)/shard_map/ppermute | solution.py:729
  21.1 3.2 %all-to-all-done.gathered = f32[32,10,1,128]{3,2,1,0:T(1,128)S(1)} async-done(((f32[32,10,1,128]{3,2,1,0:T(1,128)}), f32[32,10,1,128]{3,2,1,0:T(1,128)S(1)}, u32[]{:S(2)}, u32[]{:S(2)}) %all-to-all-start) | async-done | bytes 163872 | tf_op jit(solution)/shard_map/all_to_all | solution.py:774
  24.3 0.0 copy-done.5
  24.3 4.8 %shard_map.79 = (f32[64,256]{1,0:T(8,128)S(1)}, f32[4,64,64]{2,1,0:T(8,128)S(1)}, f32[6,16,64]{2,1,0:T(8,128)S(1)}, s32[8,384]{1,0:T(8,128)S(1)}, s32[1,256]{1,0:T(1,128)S(1)}) custom-call(s32[8]{0:T(128)S(1)} %stack.51.info, s32[8,256]{1,0:T(8,128)S(1)} %copy-done.5, f32[32,10,1,128]{3,2,1,0:T(1,128)S(1)} %all-to-all-done.gathered, ...), custom_call_target="tpu_custom_call" | custom-call | flops 10000000000 | bytes 4000000 | tf_op jit(solution)/shard_map/pallas_call | solution.py:808
  29.1 0.0 collective-permute-done.2.col_first
  29.1 0.0 collective-permute-done.3.col_second
  29.1 9.5 %shard_map.82 = (f32[2048,128]{1,0:T(8,128)S(1)}, f32[2048,128]{1,0:T(8,128)S(1)}, f32[2048,128]{1,0:T(8,128)S(1)}, f32[2048,128]{1,0:T(8,128)S(1)}, f32[32,17,1,128]{3,2,1,0:T(1,128)S(1)}) custom-call(s32[8,384]{1,0:T(8,128)S(1)} %get-tuple-element.19.plan, s32[8]{0:T(128)S(1)} %stack.51.info, s32[8,16]{1,0:T(8,128)S(1)} %copy-done.4, ...), custom_call_target="tpu_custom_call" | custom-call | flops 1000000000 | bytes 4000000 | tf_op jit(solution)/shard_map/pallas_call | solution.py:822
  38.6 15.0 %all_to_all.10.gathered = f32[32,17,1,128]{3,2,1,0:T(1,128)S(1)} all-to-all(f32[32,17,1,128]{3,2,1,0:T(1,128)S(1)} %get-tuple-element.25), channel_id=1, replica_groups=mesh['row'=8,'col'=4] {'row','col'}, dimensions={0} | all-to-all | bytes 557056 | tf_op jit(solution)/shard_map/all_to_all | solution.py:834
  53.6 3.6 %shard_map.83 = (f32[16,8,16,128]{3,2,1,0:T(8,128)}, f32[16,8,16,128]{3,2,1,0:T(8,128)}) custom-call(s32[8,16]{1,0:T(8,128)S(1)} %copy-done.2, s32[8]{0:T(128)S(1)} %stack.51.info, s32[1,256]{1,0:T(1,128)S(1)} %get-tuple-element.18.near_ids.keys, f32[32,17,1,128]{3,2,1,0:T(1,128)S(1)} %all_to_all.10.gathered, s32[1,256]{1,0:T(1,128)S(1)} %get-tuple-element.18.near_ids.keys, ...), custom_call_target="tpu_custom_call" | custom-call | flops 1000000000 | bytes 4000000 | tf_op jit(solution)/shard_map/pallas_call | solution.py:837
Async XLA Ops:
  0.6 6.3 %copy-start = (f32[16,8,16,128]{3,2,1,0:T(8,128)S(1)}, f32[16,8,16,128]{3,2,1,0:T(8,128)}, u32[]{:S(2)}) copy-start(f32[16,8,16,128]{3,2,1,0:T(8,128)} %param.6) | copy-start | bytes 3145732
  2.6 4.3 %copy-start.4 = (s32[8,16]{1,0:T(8,128)S(1)}, s32[8,16]{1,0:T(8,128)}, u32[]{:S(2)}) copy-start(s32[8,16]{1,0:T(8,128)} %ids.3) | copy-start | bytes 1540
  2.6 4.3 %copy-start.2 = (s32[8,16]{1,0:T(8,128)S(1)}, s32[8,16]{1,0:T(8,128)}, u32[]{:S(2)}) copy-start(s32[8,16]{1,0:T(8,128)} %types.3) | copy-start | bytes 1540
  2.6 15.7 %collective-permute-start = (f32[512,128]{1,0:T(8,128)}, f32[512,128]{1,0:T(8,128)}, u32[]{:S(2)}, u32[]{:S(2)}) collective-permute-start(f32[512,128]{1,0:T(8,128)} %bitcast.9), channel_id=1, source_target_pairs={{0,4},{8,12},{16,20},{24,28},{4,0},{12,8},{20,16},{28,24},{1,5},{9... | collective-permute-start | bytes 786440 | tf_op jit(solution)/shard_map/ppermute | solution.py:729
  5.6 12.7 %collective-permute-start.1 = (f32[512,128]{1,0:T(8,128)}, f32[512,128]{1,0:T(8,128)}, u32[]{:S(2)}, u32[]{:S(2)}) collective-permute-start(f32[512,128]{1,0:T(8,128)} %bitcast.10), channel_id=1, source_target_pairs={{4,8},{12,16},{20,24},{8,4},{16,12},{24,20},{5,9},{13,17},{21,25},... | collective-permute-start | bytes 786440 | tf_op jit(solution)/shard_map/ppermute | solution.py:729
  8.8 15.5 %all-to-all-start = ((f32[32,10,1,128]{3,2,1,0:T(1,128)}), f32[32,10,1,128]{3,2,1,0:T(1,128)S(1)}, u32[]{:S(2)}, u32[]{:S(2)}) async-start(f32[32,10,1,128]{3,2,1,0:T(1,128)} %shard_map.77), calls=%async_computation | async-start | bytes 327680 | tf_op jit(solution)/shard_map/all_to_all | solution.py:774
  15.8 1.0 %copy-start.1 = (f32[8,128,128]{2,1,0:T(8,128)S(1)}, f32[8,128,128]{2,1,0:T(8,128)}, u32[]{:S(2)}) copy-start(f32[8,128,128]{2,1,0:T(8,128)} %library.1) | copy-start | bytes 1572868
  15.8 1.0 %copy-start.3 = (f32[2,128]{1,0:T(2,128)S(1)}, f32[2,128]{1,0:T(2,128)}, u32[]{:S(2)}) copy-start(f32[2,128]{1,0:T(2,128)} %strap.7) | copy-start | bytes 3076
  18.3 6.0 %copy-start.5 = (s32[8,256]{1,0:T(8,128)S(1)}, s32[8,256]{1,0:T(8,128)}, u32[]{:S(2)}) copy-start(s32[8,256]{1,0:T(8,128)} %constant.42.clone.maps) | copy-start | bytes 24580
  20.2 8.9 %collective-permute-start.2 = (f32[320,128]{1,0:T(8,128)}, f32[320,128]{1,0:T(8,128)S(1)}, u32[]{:S(2)}, u32[]{:S(2)}) collective-permute-start(f32[320,128]{1,0:T(8,128)} %get-tuple-element.21), channel_id=1, source_target_pairs={{0,1},{2,3},{1,0},{3,2},{4,5},{6,7},{5,4},{7,6},{8,9},{10,11},{9,8... | collective-permute-start | bytes 491528 | tf_op jit(solution)/shard_map/ppermute | solution.py:729
  20.4 8.7 %collective-permute-start.3 = (f32[320,128]{1,0:T(8,128)}, f32[320,128]{1,0:T(8,128)S(1)}, u32[]{:S(2)}, u32[]{:S(2)}) collective-permute-start(f32[320,128]{1,0:T(8,128)} %get-tuple-element.22), channel_id=1, source_target_pairs={{1,2},{2,1},{5,6},{6,5},{9,10},{10,9},{13,14},{14,13},{17,18},{18,... | collective-permute-start | bytes 491528 | tf_op jit(solution)/shard_map/ppermute | solution.py:729

commit v8 on v7

--- a/solution.py
+++ b/solution.py
@@ -118,7 +118,7 @@
     lax.fori_loop(0, rows, step, 0)
 
 
-def weights_kernel(library, strap, stacked, low, row_sums):
+def weights_kernel(library, strap, after, stacked, low, row_sums):
     kinds, nodes, _ = library.shape
     eye = iota((nodes, nodes), 0) == iota((nodes, nodes), 1)
     couple_row = 2.0 * strap[0:1, :] + 2.0 * strap[1:2, :]
@@ -144,7 +144,7 @@
     lax.fori_loop(0, kinds, step, 0, unroll=True)
 
 
-def sides_kernel(dims, info, blocks, row_first, row_second, row_sums, first, second):
+def sides_kernel(dims, info, blocks, row_first, row_second, first, second):
     sizings, rows, cols, nodes, count = dims
     row_odd, odd = info[5], info[6]
     for out, begin in ((first, either(odd, cols - 2, 0)), (second, either(odd, 0, cols - 2))):
@@ -772,9 +772,23 @@
         4 if count <= 64 else 16,
     )(aggregate_map, block_types, aggregate_map, flat_load)
     gathered = lax.all_to_all(pay, ("row", "col"), 0, 0)
+    (blocks,) = call(
+        functools.partial(blocks_kernel, dims), [VMEM], [own], [], 1_000_000, 4
+    )(flat_load)
+    side_rows = (rows + 2) * 2 * sizings
+    side = shape((side_rows, nodes), F32)
+    first, second = call(
+        functools.partial(sides_kernel, dims),
+        [SMEM] + [VMEM] * 3,
+        [side, side],
+        [],
+        40_000_000_000,
+        4,
+    )(info, blocks, row_first, row_second)
+    col_first, col_second = swap(first, "col", 0), swap(second, "col", 1)
     stacked, low, row_sums = call(
         weights_kernel,
-        [VMEM, VMEM],
+        [VMEM, VMEM, pl.BlockSpec(memory_space=pl.ANY)],
         [
             shape((kinds, 2 * nodes, 2 * nodes), BF16),
             shape((kinds, nodes, 2 * nodes), BF16),
@@ -783,21 +797,7 @@
         [],
         1_000_000,
         8,
-    )(block_library, strap_conductance)
-    (blocks,) = call(
-        functools.partial(blocks_kernel, dims), [VMEM], [own], [], 1_000_000, 4
-    )(flat_load)
-    side_rows = (rows + 2) * 2 * sizings
-    side = shape((side_rows, nodes), F32)
-    first, second = call(
-        functools.partial(sides_kernel, dims),
-        [SMEM] + [VMEM] * 4,
-        [side, side],
-        [],
-        40_000_000_000,
-        4,
-    )(info, blocks, row_first, row_second, row_sums)
-    col_first, col_second = swap(first, "col", 0), swap(second, "col", 1)
+    )(block_library, strap_conductance, first)
 
     big = pltpu.VMEM(((many + 1) * sizings, nodes), F32)
     coarse_shape = (n_col + 2, sizings, count)

time: 57.4 us -> 56.8 us (0.990)
  starting transfers between devices: 12.2 us -> 15 us
  waiting for transfers between devices: 3.21 us -> 1.3 us
  local copies, waits for them, and re-layouts: 2.43 us -> 1.31 us
  Pallas kernels: 23.7 us -> 22.6 us
  blocking collectives: 15 us -> 15.6 us
    all_to_all x1, waiting for transfers between devices: 3.2 us -> 0.9 us  [on_device(): gathered = lax.all_to_all(pay, ('row', 'col'), 0, 0)]
    ppermute x4, starting transfers between devices: 5.23 us -> 7.44 us  [swap(): return lax.ppermute(payload, axis, pairs + [(j, i) for i, j in pairs])]
    dynamic_slice x1, local copies, waits for them, and re-layouts: 1.94 us -> 1.16 us  [on_device(): lax.dynamic_slice_in_dim(load_currents, rows - 2 - begin, 2, axis=1)]
    all_to_all x1, starting transfers between devices: 6.93 us -> 7.59 us  [on_device(): gathered = lax.all_to_all(pay, ('row', 'col'), 0, 0)]
    all_to_all x1, blocking collectives: 15 us -> 15.6 us  [on_device(): gathered = lax.all_to_all(pay, ('row', 'col'), 0, 0)]
  transfers between devices with their start and end apart: 5 -> 5, of which waited for: 1 -> 2; matrix products, arithmetic and copies ran while one was open for 0% -> 0% of each run, Pallas kernels for 18% -> 18%
where the time goes in v8:
time: 56.8 us; the launch traced here: 56.6 us
  Pallas kernels  22.6 us (40%)
  blocking collectives  15.6 us (27%)
  starting transfers between devices  15 us (26%)
  local copies, waits for them, and re-layouts  1.31 us (2%)
  waiting for transfers between devices  1.3 us (2%)
  between operations  0.82 us (1%)
    all_to_all x1, blocking collectives, on_device(): gathered = lax.all_to_all(pay, ('row', 'col'), 0, 0)  15.6 us
    pallas_call x1, Pallas kernels, on_device(): call(functools.partial(middle_kernel, dims), [SMEM] * 4 + [VMEM] * 11, [o...  8.89 us
    all_to_all x1, starting transfers between devices, on_device(): gathered = lax.all_to_all(pay, ('row', 'col'), 0, 0)  7.59 us
    ppermute x4, starting transfers between devices, swap(): return lax.ppermute(payload, axis, pairs + [(j, i) for i, j in pairs])  7.44 us
    pallas_call x1, Pallas kernels, on_device(): call(functools.partial(coarse_kernel, dims, mesh_dims, kinds), [SMEM] + [...  4.81 us
    pallas_call x1, Pallas kernels, on_device(): call(functools.partial(last_kernel, dims, mesh_dims), [SMEM] * 3 + [VMEM]...  3.69 us
    pallas_call x1, Pallas kernels, on_device(): call(functools.partial(sums_kernel, dims), [SMEM] + [VMEM] * 3, [shape((n...  1.83 us
    pallas_call x1, Pallas kernels, on_device(): call(weights_kernel, [VMEM, VMEM, pl.BlockSpec(memory_space=pl.ANY)], [sh...  1.41 us
  transfers between devices with their start and end apart: 5, of which 2 were waited for; matrix products, arithmetic and copies ran while one was open for 0% of the time, Pallas kernels for 18%

profile of v8, /device:TPU:0, one launch (start us, length us, event | category | flops | bytes accessed | tf_op | source)
XLA Modules:
  0.0 56.6 jit_solution(2899973296977561600)
XLA Ops:
  0.6 0.0 copy-start
  0.7 1.2 %constant_dynamic-slice_fusion = (f32[16,2,16,128]{3,2,1,0:T(8,128)S(1)}, f32[16,2,16,128]{3,2,1,0:T(8,128)S(1)}) fusion(f32[16,8,16,128]{3,2,1,0:T(8,128)} %param.6, s32[]{:T(128)S(6)} %select_n.22, s32[]{:T(128)S(6)} %select_n.21), kind=kLoop, calls=%fused_computation | loop fusion | bytes 1048584 | tf_op jit(solution)/shard_map/dynamic_slice | solution.py:760
  1.8 0.0 copy-start.8
  1.8 0.0 copy-start.2
  1.8 3.0 %collective-permute-start = (f32[512,128]{1,0:T(8,128)S(1)}, f32[512,128]{1,0:T(8,128)S(1)}, u32[]{:S(2)}, u32[]{:S(2)}) collective-permute-start(f32[512,128]{1,0:T(8,128)S(1)} %bitcast.14), channel_id=1, source_target_pairs={{0,4},{8,12},{16,20},{24,28},{4,0},{12,8},{20,16},{28,24},{1,5},{9... | collective-permute-start | bytes 786440 | tf_op jit(solution)/shard_map/ppermute | solution.py:729
  4.9 0.7 %collective-permute-start.1 = (f32[512,128]{1,0:T(8,128)S(1)}, f32[512,128]{1,0:T(8,128)S(1)}, u32[]{:S(2)}, u32[]{:S(2)}) collective-permute-start(f32[512,128]{1,0:T(8,128)S(1)} %bitcast.13), channel_id=1, source_target_pairs={{4,8},{12,16},{20,24},{8,4},{16,12},{24,20},{5,9},{13,17},{21,25},... | collective-permute-start | bytes 786440 | tf_op jit(solution)/shard_map/ppermute | solution.py:729
  5.6 0.0 copy-done
  5.6 0.0 copy-done.8
  5.6 0.0 copy-done.2
  5.6 1.8 %shard_map.77 = f32[32,10,1,128]{3,2,1,0:T(1,128)} custom-call(s32[8,16]{1,0:T(8,128)S(1)} %copy-done.8, s32[8,16]{1,0:T(8,128)S(1)} %copy-done.2, s32[8,16]{1,0:T(8,128)S(1)} %copy-done.8, f32[2048,128]{1,0:T(8,128)S(1)} %bitcast.11), custom_call_target="tpu_custom_call" | custom-call | flops 20000000000 | bytes 4000000 | tf_op jit(solution)/shard_map/pallas_call | solution.py:766
  7.4 7.6 %all-to-all-start = ((f32[32,10,1,128]{3,2,1,0:T(1,128)}), f32[32,10,1,128]{3,2,1,0:T(1,128)S(1)}, u32[]{:S(2)}, u32[]{:S(2)}) async-start(f32[32,10,1,128]{3,2,1,0:T(1,128)} %shard_map.77), calls=%async_computation | async-start | bytes 327680 | tf_op jit(solution)/shard_map/all_to_all | solution.py:774
  15.0 0.1 stack.51.info
  15.1 0.6 %shard_map.78.blocks = f32[2048,128]{1,0:T(8,128)S(1)} custom-call(f32[2048,128]{1,0:T(8,128)S(1)} %bitcast.12), custom_call_target="tpu_custom_call" | custom-call | flops 1000000 | bytes 4000000 | tf_op jit(solution)/shard_map/pallas_call | solution.py:775
  15.8 0.0 copy-start.1
  15.8 0.4 collective-permute-done.row_first
  16.2 0.0 copy-start.4
  16.2 0.0 collective-permute-done.1.row_second
  16.2 0.0 copy-start.6
  16.2 1.3 %shard_map.79 = (f32[320,128]{1,0:T(8,128)S(1)}, f32[320,128]{1,0:T(8,128)}) custom-call(s32[8]{0:T(128)S(1)} %stack.51.info, f32[2048,128]{1,0:T(8,128)S(1)} %shard_map.78.blocks, f32[512,128]{1,0:T(8,128)S(1)} %collective-permute-done.row_first, f32[512,128]{1,0:T(8,128)S(1)} %collective-permute-done.1.row_second), custom_call_target="tpu_custom_call" | custom-call | flops 40000000000 | bytes 4000000 | tf_op jit(solution)/shard_map/pallas_call | solution.py:780
  17.5 0.0 copy-done.4
  17.5 0.0 copy-done.6
  17.5 0.0 copy-start.3
  17.5 0.8 %collective-permute-start.3 = (f32[320,128]{1,0:T(8,128)}, f32[320,128]{1,0:T(8,128)S(1)}, u32[]{:S(2)}, u32[]{:S(2)}) collective-permute-start(f32[320,128]{1,0:T(8,128)} %get-tuple-element.22), channel_id=1, source_target_pairs={{1,2},{2,1},{5,6},{6,5},{9,10},{10,9},{13,14},{14,13},{17,18},{18,... | collective-permute-start | bytes 491528 | tf_op jit(solution)/shard_map/ppermute | solution.py:729
  18.3 0.0 copy-start.9
  18.3 2.9 %collective-permute-start.2 = (f32[320,128]{1,0:T(8,128)S(1)}, f32[320,128]{1,0:T(8,128)}, u32[]{:S(2)}, u32[]{:S(2)}) collective-permute-start(f32[320,128]{1,0:T(8,128)S(1)} %get-tuple-element.17.after), channel_id=1, source_target_pairs={{0,1},{2,3},{1,0},{3,2},{4,5},{6,7},{5,4},{7,6},{8,9},{10,11},{9,8... | collective-permute-start | bytes 491528 | tf_op jit(solution)/shard_map/ppermute | solution.py:729
  21.3 0.0 copy-done.1
  21.3 0.0 copy-done.3
  21.3 1.4 %shard_map.80 = (bf16[8,256,256]{2,1,0:T(8,128)(2,1)S(1)}, bf16[8,128,256]{2,1,0:T(8,128)(2,1)S(1)}, f32[8,128]{1,0:T(8,128)S(1)}) custom-call(f32[8,128,128]{2,1,0:T(8,128)S(1)} %copy-done.1, f32[2,128]{1,0:T(2,128)S(1)} %copy-done.3, f32[320,128]{1,0:T(8,128)S(1)} %get-tuple-element.17.after), custom_call_target="tpu_custom_call" | custom-call | flops 1000000 | bytes 4000000 | tf_op jit(solution)/shard_map/pallas_call | solution.py:789
  22.7 0.9 %all-to-all-done.gathered = f32[32,10,1,128]{3,2,1,0:T(1,128)S(1)} async-done(((f32[32,10,1,128]{3,2,1,0:T(1,128)}), f32[32,10,1,128]{3,2,1,0:T(1,128)S(1)}, u32[]{:S(2)}, u32[]{:S(2)}) %all-to-all-start) | async-done | bytes 163872 | tf_op jit(solution)/shard_map/all_to_all | solution.py:774
  23.6 0.0 copy-done.9
  23.6 0.0 copy-start.5
  23.6 0.0 copy-start.7
  23.6 4.8 %shard_map.81 = (f32[64,256]{1,0:T(8,128)S(1)}, f32[4,64,64]{2,1,0:T(8,128)S(1)}, f32[6,16,64]{2,1,0:T(8,128)S(1)}, s32[8,384]{1,0:T(8,128)S(1)}, s32[1,256]{1,0:T(1,128)S(1)}) custom-call(s32[8]{0:T(128)S(1)} %stack.51.info, s32[8,256]{1,0:T(8,128)S(1)} %copy-done.9, f32[32,10,1,128]{3,2,1,0:T(1,128)S(1)} %all-to-all-done.gathered, ...), custom_call_target="tpu_custom_call" | custom-call | flops 10000000000 | bytes 4000000 | tf_op jit(solution)/shard_map/pallas_call | solution.py:808
  28.4 0.0 collective-permute-done.3.col_second
  28.4 0.0 collective-permute-done.2.col_first
  28.4 0.0 copy-done.5
  28.4 0.0 copy-done.7
  28.4 8.9 %shard_map.82 = (f32[2048,128]{1,0:T(8,128)S(1)}, f32[2048,128]{1,0:T(8,128)S(1)}, f32[2048,128]{1,0:T(8,128)S(1)}, f32[2048,128]{1,0:T(8,128)S(1)}, f32[32,17,1,128]{3,2,1,0:T(1,128)S(1)}) custom-call(s32[8,384]{1,0:T(8,128)S(1)} %get-tuple-element.20.plan, s32[8]{0:T(128)S(1)} %stack.51.info, s32[8,16]{1,0:T(8,128)S(1)} %copy-done.8, ...), custom_call_target="tpu_custom_call" | custom-call | flops 1000000000 | bytes 4000000 | tf_op jit(solution)/shard_map/pallas_call | solution.py:822
  37.3 15.6 %all_to_all.10.gathered = f32[32,17,1,128]{3,2,1,0:T(1,128)S(1)} all-to-all(f32[32,17,1,128]{3,2,1,0:T(1,128)S(1)} %get-tuple-element.25), channel_id=1, replica_groups=mesh['row'=8,'col'=4] {'row','col'}, dimensions={0} | all-to-all | bytes 557056 | tf_op jit(solution)/shard_map/all_to_all | solution.py:834
  52.9 3.7 %shard_map.83 = (f32[16,8,16,128]{3,2,1,0:T(8,128)}, f32[16,8,16,128]{3,2,1,0:T(8,128)}) custom-call(s32[8,16]{1,0:T(8,128)S(1)} %copy-done.2, s32[8]{0:T(128)S(1)} %stack.51.info, s32[1,256]{1,0:T(1,128)S(1)} %get-tuple-element.19.near_ids.keys, f32[32,17,1,128]{3,2,1,0:T(1,128)S(1)} %all_to_all.10.gathered, s32[1,256]{1,0:T(1,128)S(1)} %get-tuple-element.19.near_ids.keys, ...), custom_call_target="tpu_custom_call" | custom-call | flops 1000000000 | bytes 4000000 | tf_op jit(solution)/shard_map/pallas_call | solution.py:837
Async XLA Ops:
  0.6 4.9 %copy-start = (f32[16,8,16,128]{3,2,1,0:T(8,128)S(1)}, f32[16,8,16,128]{3,2,1,0:T(8,128)}, u32[]{:S(2)}) copy-start(f32[16,8,16,128]{3,2,1,0:T(8,128)} %param.6) | copy-start | bytes 3145732
  1.8 3.7 %copy-start.8 = (s32[8,16]{1,0:T(8,128)S(1)}, s32[8,16]{1,0:T(8,128)}, u32[]{:S(2)}) copy-start(s32[8,16]{1,0:T(8,128)} %ids.3) | copy-start | bytes 1540
  1.8 3.7 %copy-start.2 = (s32[8,16]{1,0:T(8,128)S(1)}, s32[8,16]{1,0:T(8,128)}, u32[]{:S(2)}) copy-start(s32[8,16]{1,0:T(8,128)} %types.3) | copy-start | bytes 1540
  1.8 14.3 %collective-permute-start = (f32[512,128]{1,0:T(8,128)S(1)}, f32[512,128]{1,0:T(8,128)S(1)}, u32[]{:S(2)}, u32[]{:S(2)}) collective-permute-start(f32[512,128]{1,0:T(8,128)S(1)} %bitcast.14), channel_id=1, source_target_pairs={{0,4},{8,12},{16,20},{24,28},{4,0},{12,8},{20,16},{28,24},{1,5},{9... | collective-permute-start | bytes 786440 | tf_op jit(solution)/shard_map/ppermute | solution.py:729
  4.9 11.3 %collective-permute-start.1 = (f32[512,128]{1,0:T(8,128)S(1)}, f32[512,128]{1,0:T(8,128)S(1)}, u32[]{:S(2)}, u32[]{:S(2)}) collective-permute-start(f32[512,128]{1,0:T(8,128)S(1)} %bitcast.13), channel_id=1, source_target_pairs={{4,8},{12,16},{20,24},{8,4},{16,12},{24,20},{5,9},{13,17},{21,25},... | collective-permute-start | bytes 786440 | tf_op jit(solution)/shard_map/ppermute | solution.py:729
  7.4 16.2 %all-to-all-start = ((f32[32,10,1,128]{3,2,1,0:T(1,128)}), f32[32,10,1,128]{3,2,1,0:T(1,128)S(1)}, u32[]{:S(2)}, u32[]{:S(2)}) async-start(f32[32,10,1,128]{3,2,1,0:T(1,128)} %shard_map.77), calls=%async_computation | async-start | bytes 327680 | tf_op jit(solution)/shard_map/all_to_all | solution.py:774
  15.8 5.5 %copy-start.1 = (f32[8,128,128]{2,1,0:T(8,128)S(1)}, f32[8,128,128]{2,1,0:T(8,128)}, u32[]{:S(2)}) copy-start(f32[8,128,128]{2,1,0:T(8,128)} %library.1) | copy-start | bytes 1572868
  16.2 1.3 %copy-start.4 = (f32[512,128]{1,0:T(8,128)}, f32[512,128]{1,0:T(8,128)S(1)}, u32[]{:S(2)}) copy-start(f32[512,128]{1,0:T(8,128)S(1)} %collective-permute-done.row_first) | copy-start | bytes 786436
  16.2 1.3 %copy-start.6 = (f32[512,128]{1,0:T(8,128)}, f32[512,128]{1,0:T(8,128)S(1)}, u32[]{:S(2)}) copy-start(f32[512,128]{1,0:T(8,128)S(1)} %collective-permute-done.1.row_second) | copy-start | bytes 786436
  17.5 3.8 %copy-start.3 = (f32[2,128]{1,0:T(2,128)S(1)}, f32[2,128]{1,0:T(2,128)}, u32[]{:S(2)}) copy-start(f32[2,128]{1,0:T(2,128)} %strap.7) | copy-start | bytes 3076
  17.5 10.9 %collective-permute-start.3 = (f32[320,128]{1,0:T(8,128)}, f32[320,128]{1,0:T(8,128)S(1)}, u32[]{:S(2)}, u32[]{:S(2)}) collective-permute-start(f32[320,128]{1,0:T(8,128)} %get-tuple-element.22), channel_id=1, source_target_pairs={{1,2},{2,1},{5,6},{6,5},{9,10},{10,9},{13,14},{14,13},{17,18},{18,... | collective-permute-start | bytes 491528 | tf_op jit(solution)/shard_map/ppermute | solution.py:729
  18.3 5.3 %copy-start.9 = (s32[8,256]{1,0:T(8,128)S(1)}, s32[8,256]{1,0:T(8,128)}, u32[]{:S(2)}) copy-start(s32[8,256]{1,0:T(8,128)} %constant.42.clone.maps) | copy-start | bytes 24580
  18.3 10.1 %collective-permute-start.2 = (f32[320,128]{1,0:T(8,128)S(1)}, f32[320,128]{1,0:T(8,128)}, u32[]{:S(2)}, u32[]{:S(2)}) collective-permute-start(f32[320,128]{1,0:T(8,128)S(1)} %get-tuple-element.17.after), channel_id=1, source_target_pairs={{0,1},{2,3},{1,0},{3,2},{4,5},{6,7},{5,4},{7,6},{8,9},{10,11},{9,8... | collective-permute-start | bytes 491528 | tf_op jit(solution)/shard_map/ppermute | solution.py:729
  23.6 4.8 %copy-start.5 = (f32[512,128]{1,0:T(8,128)S(1)}, f32[512,128]{1,0:T(8,128)}, u32[]{:S(2)}) copy-start(f32[512,128]{1,0:T(8,128)} %copy-done.4) | copy-start | bytes 786436
  23.6 4.8 %copy-start.7 = (f32[512,128]{1,0:T(8,128)S(1)}, f32[512,128]{1,0:T(8,128)}, u32[]{:S(2)}) copy-start(f32[512,128]{1,0:T(8,128)} %copy-done.6) | copy-start | bytes 786436

commit v9 on v8

--- a/solution.py
+++ b/solution.py
@@ -11,7 +11,7 @@
 AGR = 4
 AGC = 4
 TILE = 8
-GROUP = 8
+GROUP = 4
 PANEL = 8
 F32 = jnp.float32
 BF16 = jnp.bfloat16
@@ -218,9 +218,9 @@
 
 
 def sorted_products(plan, which, source, stacked, low, sizings, store):
-    def step(it, carry):
-        for one in range(GROUP):
-            tile = it * GROUP + one
+    def step(begin, size):
+        for one in range(size):
+            tile = begin + one
             kind = plan[2 + which, tile]
             places = [
                 pl.ds(pl.multiple_of(plan[which, tile * TILE + j] * sizings, sizings), sizings)
@@ -233,9 +233,19 @@
                 jnp.concatenate([high, rest], axis=1), stacked[kind], preferred_element_type=F32
             ) + jnp.dot(high, low[kind], preferred_element_type=F32)
             store(kind, places, out)
+
+    groups = plan[4 + which, 0]
+
+    def double(it, carry):
+        step(it * (2 * GROUP), 2 * GROUP)
         return carry
 
-    lax.fori_loop(0, plan[4 + which, 0], step, 0)
+    def single(it, carry):
+        step((groups - 1) * GROUP, GROUP)
+        return carry
+
+    lax.fori_loop(0, groups // 2, double, 0)
+    lax.fori_loop(0, groups % 2, single, 0)
 
 
 def neighbour_ids(ids, cols):

time: 56.8 us -> 56.8 us (level)
  no operation moved by 1% of the time
where the time goes in v9:
time: 56.8 us; the launch traced here: 56.7 us
  Pallas kernels  22.4 us (39%)
  blocking collectives  15.8 us (28%)
  starting transfers between devices  15 us (26%)
  local copies, waits for them, and re-layouts  1.31 us (2%)
  waiting for transfers between devices  1.3 us (2%)
  between operations  0.82 us (1%)
    all_to_all x1, blocking collectives, on_device(): gathered = lax.all_to_all(pay, ('row', 'col'), 0, 0)  15.8 us
    pallas_call x1, Pallas kernels, on_device(): call(functools.partial(middle_kernel, dims), [SMEM] * 4 + [VMEM] * 11, [o...  8.74 us
    all_to_all x1, starting transfers between devices, on_device(): gathered = lax.all_to_all(pay, ('row', 'col'), 0, 0)  7.59 us
    ppermute x4, starting transfers between devices, swap(): return lax.ppermute(payload, axis, pairs + [(j, i) for i, j in pairs])  7.44 us
    pallas_call x1, Pallas kernels, on_device(): call(functools.partial(coarse_kernel, dims, mesh_dims, kinds), [SMEM] + [...  4.81 us
    pallas_call x1, Pallas kernels, on_device(): call(functools.partial(last_kernel, dims, mesh_dims), [SMEM] * 3 + [VMEM]...  3.69 us
    pallas_call x1, Pallas kernels, on_device(): call(functools.partial(sums_kernel, dims), [SMEM] + [VMEM] * 3, [shape((n...  1.83 us
    pallas_call x1, Pallas kernels, on_device(): call(weights_kernel, [VMEM, VMEM, pl.BlockSpec(memory_space=pl.ANY)], [sh...  1.41 us
  transfers between devices with their start and end apart: 5, of which 2 were waited for; matrix products, arithmetic and copies ran while one was open for 0% of the time, Pallas kernels for 18%

profile of v9, /device:TPU:0, one launch (start us, length us, event | category | flops | bytes accessed | tf_op | source)
XLA Modules:
  0.0 56.7 jit_solution(17967326393054564561)
XLA Ops:
  0.6 0.0 copy-start
  0.7 1.2 %constant_dynamic-slice_fusion = (f32[16,2,16,128]{3,2,1,0:T(8,128)S(1)}, f32[16,2,16,128]{3,2,1,0:T(8,128)S(1)}) fusion(f32[16,8,16,128]{3,2,1,0:T(8,128)} %param.6, s32[]{:T(128)S(6)} %select_n.22, s32[]{:T(128)S(6)} %select_n.21), kind=kLoop, calls=%fused_computation | loop fusion | bytes 1048584 | tf_op jit(solution)/shard_map/dynamic_slice | solution.py:770
  1.8 0.0 copy-start.8
  1.8 0.0 copy-start.2
  1.8 3.0 %collective-permute-start = (f32[512,128]{1,0:T(8,128)S(1)}, f32[512,128]{1,0:T(8,128)S(1)}, u32[]{:S(2)}, u32[]{:S(2)}) collective-permute-start(f32[512,128]{1,0:T(8,128)S(1)} %bitcast.14), channel_id=1, source_target_pairs={{0,4},{8,12},{16,20},{24,28},{4,0},{12,8},{20,16},{28,24},{1,5},{9... | collective-permute-start | bytes 786440 | tf_op jit(solution)/shard_map/ppermute | solution.py:739
  4.9 0.7 %collective-permute-start.1 = (f32[512,128]{1,0:T(8,128)S(1)}, f32[512,128]{1,0:T(8,128)S(1)}, u32[]{:S(2)}, u32[]{:S(2)}) collective-permute-start(f32[512,128]{1,0:T(8,128)S(1)} %bitcast.13), channel_id=1, source_target_pairs={{4,8},{12,16},{20,24},{8,4},{16,12},{24,20},{5,9},{13,17},{21,25},... | collective-permute-start | bytes 786440 | tf_op jit(solution)/shard_map/ppermute | solution.py:739
  5.6 0.0 copy-done
  5.6 0.0 copy-done.8
  5.6 0.0 copy-done.2
  5.6 1.8 %shard_map.77 = f32[32,10,1,128]{3,2,1,0:T(1,128)} custom-call(s32[8,16]{1,0:T(8,128)S(1)} %copy-done.8, s32[8,16]{1,0:T(8,128)S(1)} %copy-done.2, s32[8,16]{1,0:T(8,128)S(1)} %copy-done.8, f32[2048,128]{1,0:T(8,128)S(1)} %bitcast.11), custom_call_target="tpu_custom_call" | custom-call | flops 20000000000 | bytes 4000000 | tf_op jit(solution)/shard_map/pallas_call | solution.py:776
  7.4 7.6 %all-to-all-start = ((f32[32,10,1,128]{3,2,1,0:T(1,128)}), f32[32,10,1,128]{3,2,1,0:T(1,128)S(1)}, u32[]{:S(2)}, u32[]{:S(2)}) async-start(f32[32,10,1,128]{3,2,1,0:T(1,128)} %shard_map.77), calls=%async_computation | async-start | bytes 327680 | tf_op jit(solution)/shard_map/all_to_all | solution.py:784
  15.0 0.1 stack.51.info
  15.1 0.6 %shard_map.78.blocks = f32[2048,128]{1,0:T(8,128)S(1)} custom-call(f32[2048,128]{1,0:T(8,128)S(1)} %bitcast.12), custom_call_target="tpu_custom_call" | custom-call | flops 1000000 | bytes 4000000 | tf_op jit(solution)/shard_map/pallas_call | solution.py:785
  15.8 0.0 copy-start.1
  15.8 0.4 collective-permute-done.row_first
  16.2 0.0 copy-start.4
  16.2 0.0 collective-permute-done.1.row_second
  16.2 0.0 copy-start.6
  16.2 1.3 %shard_map.79 = (f32[320,128]{1,0:T(8,128)S(1)}, f32[320,128]{1,0:T(8,128)}) custom-call(s32[8]{0:T(128)S(1)} %stack.51.info, f32[2048,128]{1,0:T(8,128)S(1)} %shard_map.78.blocks, f32[512,128]{1,0:T(8,128)S(1)} %collective-permute-done.row_first, f32[512,128]{1,0:T(8,128)S(1)} %collective-permute-done.1.row_second), custom_call_target="tpu_custom_call" | custom-call | flops 40000000000 | bytes 4000000 | tf_op jit(solution)/shard_map/pallas_call | solution.py:790
  17.5 0.0 copy-done.4
  17.5 0.0 copy-done.6
  17.5 0.0 copy-start.3
  17.5 0.8 %collective-permute-start.3 = (f32[320,128]{1,0:T(8,128)}, f32[320,128]{1,0:T(8,128)S(1)}, u32[]{:S(2)}, u32[]{:S(2)}) collective-permute-start(f32[320,128]{1,0:T(8,128)} %get-tuple-element.22), channel_id=1, source_target_pairs={{1,2},{2,1},{5,6},{6,5},{9,10},{10,9},{13,14},{14,13},{17,18},{18,... | collective-permute-start | bytes 491528 | tf_op jit(solution)/shard_map/ppermute | solution.py:739
  18.3 0.0 copy-start.9
  18.3 2.9 %collective-permute-start.2 = (f32[320,128]{1,0:T(8,128)S(1)}, f32[320,128]{1,0:T(8,128)}, u32[]{:S(2)}, u32[]{:S(2)}) collective-permute-start(f32[320,128]{1,0:T(8,128)S(1)} %get-tuple-element.17.after), channel_id=1, source_target_pairs={{0,1},{2,3},{1,0},{3,2},{4,5},{6,7},{5,4},{7,6},{8,9},{10,11},{9,8... | collective-permute-start | bytes 491528 | tf_op jit(solution)/shard_map/ppermute | solution.py:739
  21.3 0.0 copy-done.1
  21.3 0.0 copy-done.3
  21.3 1.4 %shard_map.80 = (bf16[8,256,256]{2,1,0:T(8,128)(2,1)S(1)}, bf16[8,128,256]{2,1,0:T(8,128)(2,1)S(1)}, f32[8,128]{1,0:T(8,128)S(1)}) custom-call(f32[8,128,128]{2,1,0:T(8,128)S(1)} %copy-done.1, f32[2,128]{1,0:T(2,128)S(1)} %copy-done.3, f32[320,128]{1,0:T(8,128)S(1)} %get-tuple-element.17.after), custom_call_target="tpu_custom_call" | custom-call | flops 1000000 | bytes 4000000 | tf_op jit(solution)/shard_map/pallas_call | solution.py:799
  22.7 0.9 %all-to-all-done.gathered = f32[32,10,1,128]{3,2,1,0:T(1,128)S(1)} async-done(((f32[32,10,1,128]{3,2,1,0:T(1,128)}), f32[32,10,1,128]{3,2,1,0:T(1,128)S(1)}, u32[]{:S(2)}, u32[]{:S(2)}) %all-to-all-start) | async-done | bytes 163872 | tf_op jit(solution)/shard_map/all_to_all | solution.py:784
  23.6 0.0 copy-done.9
  23.6 0.0 copy-start.5
  23.6 0.0 copy-start.7
  23.6 4.8 %shard_map.81 = (f32[64,256]{1,0:T(8,128)S(1)}, f32[4,64,64]{2,1,0:T(8,128)S(1)}, f32[6,16,64]{2,1,0:T(8,128)S(1)}, s32[8,384]{1,0:T(8,128)S(1)}, s32[1,256]{1,0:T(1,128)S(1)}) custom-call(s32[8]{0:T(128)S(1)} %stack.51.info, s32[8,256]{1,0:T(8,128)S(1)} %copy-done.9, f32[32,10,1,128]{3,2,1,0:T(1,128)S(1)} %all-to-all-done.gathered, ...), custom_call_target="tpu_custom_call" | custom-call | flops 10000000000 | bytes 4000000 | tf_op jit(solution)/shard_map/pallas_call | solution.py:818
  28.4 0.0 collective-permute-done.3.col_second
  28.4 0.0 collective-permute-done.2.col_first
  28.4 0.0 copy-done.5
  28.4 0.0 copy-done.7
  28.4 8.7 %shard_map.82 = (f32[2048,128]{1,0:T(8,128)S(1)}, f32[2048,128]{1,0:T(8,128)S(1)}, f32[2048,128]{1,0:T(8,128)S(1)}, f32[2048,128]{1,0:T(8,128)S(1)}, f32[32,17,1,128]{3,2,1,0:T(1,128)S(1)}) custom-call(s32[8,384]{1,0:T(8,128)S(1)} %get-tuple-element.20.plan, s32[8]{0:T(128)S(1)} %stack.51.info, s32[8,16]{1,0:T(8,128)S(1)} %copy-done.8, ...), custom_call_target="tpu_custom_call" | custom-call | flops 1000000000 | bytes 4000000 | tf_op jit(solution)/shard_map/pallas_call | solution.py:832
  37.2 15.8 %all_to_all.10.gathered = f32[32,17,1,128]{3,2,1,0:T(1,128)S(1)} all-to-all(f32[32,17,1,128]{3,2,1,0:T(1,128)S(1)} %get-tuple-element.25), channel_id=1, replica_groups=mesh['row'=8,'col'=4] {'row','col'}, dimensions={0} | all-to-all | bytes 557056 | tf_op jit(solution)/shard_map/all_to_all | solution.py:844
  53.0 3.7 %shard_map.83 = (f32[16,8,16,128]{3,2,1,0:T(8,128)}, f32[16,8,16,128]{3,2,1,0:T(8,128)}) custom-call(s32[8,16]{1,0:T(8,128)S(1)} %copy-done.2, s32[8]{0:T(128)S(1)} %stack.51.info, s32[1,256]{1,0:T(1,128)S(1)} %get-tuple-element.19.near_ids.keys, f32[32,17,1,128]{3,2,1,0:T(1,128)S(1)} %all_to_all.10.gathered, s32[1,256]{1,0:T(1,128)S(1)} %get-tuple-element.19.near_ids.keys, ...), custom_call_target="tpu_custom_call" | custom-call | flops 1000000000 | bytes 4000000 | tf_op jit(solution)/shard_map/pallas_call | solution.py:847
Async XLA Ops:
  0.6 4.9 %copy-start = (f32[16,8,16,128]{3,2,1,0:T(8,128)S(1)}, f32[16,8,16,128]{3,2,1,0:T(8,128)}, u32[]{:S(2)}) copy-start(f32[16,8,16,128]{3,2,1,0:T(8,128)} %param.6) | copy-start | bytes 3145732
  1.8 3.7 %copy-start.8 = (s32[8,16]{1,0:T(8,128)S(1)}, s32[8,16]{1,0:T(8,128)}, u32[]{:S(2)}) copy-start(s32[8,16]{1,0:T(8,128)} %ids.3) | copy-start | bytes 1540
  1.8 3.7 %copy-start.2 = (s32[8,16]{1,0:T(8,128)S(1)}, s32[8,16]{1,0:T(8,128)}, u32[]{:S(2)}) copy-start(s32[8,16]{1,0:T(8,128)} %types.3) | copy-start | bytes 1540
  1.8 14.3 %collective-permute-start = (f32[512,128]{1,0:T(8,128)S(1)}, f32[512,128]{1,0:T(8,128)S(1)}, u32[]{:S(2)}, u32[]{:S(2)}) collective-permute-start(f32[512,128]{1,0:T(8,128)S(1)} %bitcast.14), channel_id=1, source_target_pairs={{0,4},{8,12},{16,20},{24,28},{4,0},{12,8},{20,16},{28,24},{1,5},{9... | collective-permute-start | bytes 786440 | tf_op jit(solution)/shard_map/ppermute | solution.py:739
  4.9 11.3 %collective-permute-start.1 = (f32[512,128]{1,0:T(8,128)S(1)}, f32[512,128]{1,0:T(8,128)S(1)}, u32[]{:S(2)}, u32[]{:S(2)}) collective-permute-start(f32[512,128]{1,0:T(8,128)S(1)} %bitcast.13), channel_id=1, source_target_pairs={{4,8},{12,16},{20,24},{8,4},{16,12},{24,20},{5,9},{13,17},{21,25},... | collective-permute-start | bytes 786440 | tf_op jit(solution)/shard_map/ppermute | solution.py:739
  7.4 16.2 %all-to-all-start = ((f32[32,10,1,128]{3,2,1,0:T(1,128)}), f32[32,10,1,128]{3,2,1,0:T(1,128)S(1)}, u32[]{:S(2)}, u32[]{:S(2)}) async-start(f32[32,10,1,128]{3,2,1,0:T(1,128)} %shard_map.77), calls=%async_computation | async-start | bytes 327680 | tf_op jit(solution)/shard_map/all_to_all | solution.py:784
  15.8 5.5 %copy-start.1 = (f32[8,128,128]{2,1,0:T(8,128)S(1)}, f32[8,128,128]{2,1,0:T(8,128)}, u32[]{:S(2)}) copy-start(f32[8,128,128]{2,1,0:T(8,128)} %library.1) | copy-start | bytes 1572868
  16.2 1.3 %copy-start.4 = (f32[512,128]{1,0:T(8,128)}, f32[512,128]{1,0:T(8,128)S(1)}, u32[]{:S(2)}) copy-start(f32[512,128]{1,0:T(8,128)S(1)} %collective-permute-done.row_first) | copy-start | bytes 786436
  16.2 1.3 %copy-start.6 = (f32[512,128]{1,0:T(8,128)}, f32[512,128]{1,0:T(8,128)S(1)}, u32[]{:S(2)}) copy-start(f32[512,128]{1,0:T(8,128)S(1)} %collective-permute-done.1.row_second) | copy-start | bytes 786436
  17.5 3.8 %copy-start.3 = (f32[2,128]{1,0:T(2,128)S(1)}, f32[2,128]{1,0:T(2,128)}, u32[]{:S(2)}) copy-start(f32[2,128]{1,0:T(2,128)} %strap.7) | copy-start | bytes 3076
  17.5 10.9 %collective-permute-start.3 = (f32[320,128]{1,0:T(8,128)}, f32[320,128]{1,0:T(8,128)S(1)}, u32[]{:S(2)}, u32[]{:S(2)}) collective-permute-start(f32[320,128]{1,0:T(8,128)} %get-tuple-element.22), channel_id=1, source_target_pairs={{1,2},{2,1},{5,6},{6,5},{9,10},{10,9},{13,14},{14,13},{17,18},{18,... | collective-permute-start | bytes 491528 | tf_op jit(solution)/shard_map/ppermute | solution.py:739
  18.3 5.3 %copy-start.9 = (s32[8,256]{1,0:T(8,128)S(1)}, s32[8,256]{1,0:T(8,128)}, u32[]{:S(2)}) copy-start(s32[8,256]{1,0:T(8,128)} %constant.42.clone.maps) | copy-start | bytes 24580
  18.3 10.1 %collective-permute-start.2 = (f32[320,128]{1,0:T(8,128)S(1)}, f32[320,128]{1,0:T(8,128)}, u32[]{:S(2)}, u32[]{:S(2)}) collective-permute-start(f32[320,128]{1,0:T(8,128)S(1)} %get-tuple-element.17.after), channel_id=1, source_target_pairs={{0,1},{2,3},{1,0},{3,2},{4,5},{6,7},{5,4},{7,6},{8,9},{10,11},{9,8... | collective-permute-start | bytes 491528 | tf_op jit(solution)/shard_map/ppermute | solution.py:739
  23.6 4.8 %copy-start.5 = (f32[512,128]{1,0:T(8,128)S(1)}, f32[512,128]{1,0:T(8,128)}, u32[]{:S(2)}) copy-start(f32[512,128]{1,0:T(8,128)} %copy-done.4) | copy-start | bytes 786436
  23.6 4.8 %copy-start.7 = (f32[512,128]{1,0:T(8,128)S(1)}, f32[512,128]{1,0:T(8,128)}, u32[]{:S(2)}) copy-start(f32[512,128]{1,0:T(8,128)} %copy-done.6) | copy-start | bytes 786436

commit v10 on v9

--- a/solution.py
+++ b/solution.py
@@ -101,7 +101,7 @@
         pay[d] = rows
         return carry
 
-    lax.fori_loop(0, pay.shape[0], copy, 0, unroll=4)
+    lax.fori_loop(0, pay.shape[0], copy, 0, unroll=8)
 
 
 def blocks_kernel(dims, load, blocks):

time: 56.8 us -> 56.8 us (level)
  no operation moved by 1% of the time
where the time goes in v10:
time: 56.8 us; the launch traced here: 56.3 us
  Pallas kernels  22.4 us (39%)
  blocking collectives  15.5 us (27%)
  starting transfers between devices  15 us (26%)
  local copies, waits for them, and re-layouts  1.31 us (2%)
  waiting for transfers between devices  1.29 us (2%)
  between operations  0.82 us (1%)
    all_to_all x1, blocking collectives, on_device(): gathered = lax.all_to_all(pay, ('row', 'col'), 0, 0)  15.5 us
    pallas_call x1, Pallas kernels, on_device(): call(functools.partial(middle_kernel, dims), [SMEM] * 4 + [VMEM] * 11, [o...  8.71 us
    all_to_all x1, starting transfers between devices, on_device(): gathered = lax.all_to_all(pay, ('row', 'col'), 0, 0)  7.59 us
    ppermute x4, starting transfers between devices, swap(): return lax.ppermute(payload, axis, pairs + [(j, i) for i, j in pairs])  7.45 us
    pallas_call x1, Pallas kernels, on_device(): call(functools.partial(coarse_kernel, dims, mesh_dims, kinds), [SMEM] + [...  4.81 us
    pallas_call x1, Pallas kernels, on_device(): call(functools.partial(last_kernel, dims, mesh_dims), [SMEM] * 3 + [VMEM]...  3.69 us
    pallas_call x1, Pallas kernels, on_device(): call(functools.partial(sums_kernel, dims), [SMEM] + [VMEM] * 3, [shape((n...  1.8 us
    pallas_call x1, Pallas kernels, on_device(): call(weights_kernel, [VMEM, VMEM, pl.BlockSpec(memory_space=pl.ANY)], [sh...  1.41 us
  transfers between devices with their start and end apart: 5, of which 2 were waited for; matrix products, arithmetic and copies ran while one was open for 0% of the time, Pallas kernels for 18%

profile of v10, /device:TPU:0, one launch (start us, length us, event | category | flops | bytes accessed | tf_op | source)
XLA Modules:
  0.0 56.3 jit_solution(138025038997640449)
XLA Ops:
  0.6 0.0 copy-start
  0.7 1.2 %constant_dynamic-slice_fusion = (f32[16,2,16,128]{3,2,1,0:T(8,128)S(1)}, f32[16,2,16,128]{3,2,1,0:T(8,128)S(1)}) fusion(f32[16,8,16,128]{3,2,1,0:T(8,128)} %param.6, s32[]{:T(128)S(6)} %select_n.22, s32[]{:T(128)S(6)} %select_n.21), kind=kLoop, calls=%fused_computation | loop fusion | bytes 1048584 | tf_op jit(solution)/shard_map/dynamic_slice | solution.py:770
  1.8 0.0 copy-start.8
  1.8 0.0 copy-start.2
  1.8 3.0 %collective-permute-start = (f32[512,128]{1,0:T(8,128)S(1)}, f32[512,128]{1,0:T(8,128)S(1)}, u32[]{:S(2)}, u32[]{:S(2)}) collective-permute-start(f32[512,128]{1,0:T(8,128)S(1)} %bitcast.14), channel_id=1, source_target_pairs={{0,4},{8,12},{16,20},{24,28},{4,0},{12,8},{20,16},{28,24},{1,5},{9... | collective-permute-start | bytes 786440 | tf_op jit(solution)/shard_map/ppermute | solution.py:739
  4.9 0.7 %collective-permute-start.1 = (f32[512,128]{1,0:T(8,128)S(1)}, f32[512,128]{1,0:T(8,128)S(1)}, u32[]{:S(2)}, u32[]{:S(2)}) collective-permute-start(f32[512,128]{1,0:T(8,128)S(1)} %bitcast.13), channel_id=1, source_target_pairs={{4,8},{12,16},{20,24},{8,4},{16,12},{24,20},{5,9},{13,17},{21,25},... | collective-permute-start | bytes 786440 | tf_op jit(solution)/shard_map/ppermute | solution.py:739
  5.6 0.0 copy-done
  5.6 0.0 copy-done.8
  5.6 0.0 copy-done.2
  5.6 1.8 %shard_map.77 = f32[32,10,1,128]{3,2,1,0:T(1,128)} custom-call(s32[8,16]{1,0:T(8,128)S(1)} %copy-done.8, s32[8,16]{1,0:T(8,128)S(1)} %copy-done.2, s32[8,16]{1,0:T(8,128)S(1)} %copy-done.8, f32[2048,128]{1,0:T(8,128)S(1)} %bitcast.11), custom_call_target="tpu_custom_call" | custom-call | flops 20000000000 | bytes 4000000 | tf_op jit(solution)/shard_map/pallas_call | solution.py:776
  7.4 7.6 %all-to-all-start = ((f32[32,10,1,128]{3,2,1,0:T(1,128)}), f32[32,10,1,128]{3,2,1,0:T(1,128)S(1)}, u32[]{:S(2)}, u32[]{:S(2)}) async-start(f32[32,10,1,128]{3,2,1,0:T(1,128)} %shard_map.77), calls=%async_computation | async-start | bytes 327680 | tf_op jit(solution)/shard_map/all_to_all | solution.py:784
  15.0 0.1 stack.51.info
  15.1 0.6 %shard_map.78.blocks = f32[2048,128]{1,0:T(8,128)S(1)} custom-call(f32[2048,128]{1,0:T(8,128)S(1)} %bitcast.12), custom_call_target="tpu_custom_call" | custom-call | flops 1000000 | bytes 4000000 | tf_op jit(solution)/shard_map/pallas_call | solution.py:785
  15.7 0.0 copy-start.1
  15.8 0.4 collective-permute-done.row_first
  16.2 0.0 copy-start.4
  16.2 0.0 collective-permute-done.1.row_second
  16.2 0.0 copy-start.6
  16.2 1.3 %shard_map.79 = (f32[320,128]{1,0:T(8,128)S(1)}, f32[320,128]{1,0:T(8,128)}) custom-call(s32[8]{0:T(128)S(1)} %stack.51.info, f32[2048,128]{1,0:T(8,128)S(1)} %shard_map.78.blocks, f32[512,128]{1,0:T(8,128)S(1)} %collective-permute-done.row_first, f32[512,128]{1,0:T(8,128)S(1)} %collective-permute-done.1.row_second), custom_call_target="tpu_custom_call" | custom-call | flops 40000000000 | bytes 4000000 | tf_op jit(solution)/shard_map/pallas_call | solution.py:790
  17.5 0.0 copy-done.4
  17.5 0.0 copy-done.6
  17.5 0.0 copy-start.3
  17.5 0.8 %collective-permute-start.3 = (f32[320,128]{1,0:T(8,128)}, f32[320,128]{1,0:T(8,128)S(1)}, u32[]{:S(2)}, u32[]{:S(2)}) collective-permute-start(f32[320,128]{1,0:T(8,128)} %get-tuple-element.22), channel_id=1, source_target_pairs={{1,2},{2,1},{5,6},{6,5},{9,10},{10,9},{13,14},{14,13},{17,18},{18,... | collective-permute-start | bytes 491528 | tf_op jit(solution)/shard_map/ppermute | solution.py:739
  18.3 0.0 copy-start.9
  18.3 3.0 %collective-permute-start.2 = (f32[320,128]{1,0:T(8,128)S(1)}, f32[320,128]{1,0:T(8,128)}, u32[]{:S(2)}, u32[]{:S(2)}) collective-permute-start(f32[320,128]{1,0:T(8,128)S(1)} %get-tuple-element.17.after), channel_id=1, source_target_pairs={{0,1},{2,3},{1,0},{3,2},{4,5},{6,7},{5,4},{7,6},{8,9},{10,11},{9,8... | collective-permute-start | bytes 491528 | tf_op jit(solution)/shard_map/ppermute | solution.py:739
  21.3 0.0 copy-done.1
  21.3 0.0 copy-done.3
  21.3 1.4 %shard_map.80 = (bf16[8,256,256]{2,1,0:T(8,128)(2,1)S(1)}, bf16[8,128,256]{2,1,0:T(8,128)(2,1)S(1)}, f32[8,128]{1,0:T(8,128)S(1)}) custom-call(f32[8,128,128]{2,1,0:T(8,128)S(1)} %copy-done.1, f32[2,128]{1,0:T(2,128)S(1)} %copy-done.3, f32[320,128]{1,0:T(8,128)S(1)} %get-tuple-element.17.after), custom_call_target="tpu_custom_call" | custom-call | flops 1000000 | bytes 4000000 | tf_op jit(solution)/shard_map/pallas_call | solution.py:799
  22.7 0.9 %all-to-all-done.gathered = f32[32,10,1,128]{3,2,1,0:T(1,128)S(1)} async-done(((f32[32,10,1,128]{3,2,1,0:T(1,128)}), f32[32,10,1,128]{3,2,1,0:T(1,128)S(1)}, u32[]{:S(2)}, u32[]{:S(2)}) %all-to-all-start) | async-done | bytes 163872 | tf_op jit(solution)/shard_map/all_to_all | solution.py:784
  23.6 0.0 copy-done.9
  23.6 0.0 copy-start.5
  23.6 0.0 copy-start.7
  23.6 4.8 %shard_map.81 = (f32[64,256]{1,0:T(8,128)S(1)}, f32[4,64,64]{2,1,0:T(8,128)S(1)}, f32[6,16,64]{2,1,0:T(8,128)S(1)}, s32[8,384]{1,0:T(8,128)S(1)}, s32[1,256]{1,0:T(1,128)S(1)}) custom-call(s32[8]{0:T(128)S(1)} %stack.51.info, s32[8,256]{1,0:T(8,128)S(1)} %copy-done.9, f32[32,10,1,128]{3,2,1,0:T(1,128)S(1)} %all-to-all-done.gathered, ...), custom_call_target="tpu_custom_call" | custom-call | flops 10000000000 | bytes 4000000 | tf_op jit(solution)/shard_map/pallas_call | solution.py:818
  28.4 0.0 collective-permute-done.3.col_second
  28.4 0.0 collective-permute-done.2.col_first
  28.4 0.0 copy-done.5
  28.4 0.0 copy-done.7
  28.4 8.7 %shard_map.82 = (f32[2048,128]{1,0:T(8,128)S(1)}, f32[2048,128]{1,0:T(8,128)S(1)}, f32[2048,128]{1,0:T(8,128)S(1)}, f32[2048,128]{1,0:T(8,128)S(1)}, f32[32,17,1,128]{3,2,1,0:T(1,128)S(1)}) custom-call(s32[8,384]{1,0:T(8,128)S(1)} %get-tuple-element.20.plan, s32[8]{0:T(128)S(1)} %stack.51.info, s32[8,16]{1,0:T(8,128)S(1)} %copy-done.8, ...), custom_call_target="tpu_custom_call" | custom-call | flops 1000000000 | bytes 4000000 | tf_op jit(solution)/shard_map/pallas_call | solution.py:832
  37.1 15.5 %all_to_all.10.gathered = f32[32,17,1,128]{3,2,1,0:T(1,128)S(1)} all-to-all(f32[32,17,1,128]{3,2,1,0:T(1,128)S(1)} %get-tuple-element.25), channel_id=1, replica_groups=mesh['row'=8,'col'=4] {'row','col'}, dimensions={0} | all-to-all | bytes 557056 | tf_op jit(solution)/shard_map/all_to_all | solution.py:844
  52.6 3.7 %shard_map.83 = (f32[16,8,16,128]{3,2,1,0:T(8,128)}, f32[16,8,16,128]{3,2,1,0:T(8,128)}) custom-call(s32[8,16]{1,0:T(8,128)S(1)} %copy-done.2, s32[8]{0:T(128)S(1)} %stack.51.info, s32[1,256]{1,0:T(1,128)S(1)} %get-tuple-element.19.near_ids.keys, f32[32,17,1,128]{3,2,1,0:T(1,128)S(1)} %all_to_all.10.gathered, s32[1,256]{1,0:T(1,128)S(1)} %get-tuple-element.19.near_ids.keys, ...), custom_call_target="tpu_custom_call" | custom-call | flops 1000000000 | bytes 4000000 | tf_op jit(solution)/shard_map/pallas_call | solution.py:847
Async XLA Ops:
  0.6 4.9 %copy-start = (f32[16,8,16,128]{3,2,1,0:T(8,128)S(1)}, f32[16,8,16,128]{3,2,1,0:T(8,128)}, u32[]{:S(2)}) copy-start(f32[16,8,16,128]{3,2,1,0:T(8,128)} %param.6) | copy-start | bytes 3145732
  1.8 3.7 %copy-start.8 = (s32[8,16]{1,0:T(8,128)S(1)}, s32[8,16]{1,0:T(8,128)}, u32[]{:S(2)}) copy-start(s32[8,16]{1,0:T(8,128)} %ids.3) | copy-start | bytes 1540
  1.8 3.7 %copy-start.2 = (s32[8,16]{1,0:T(8,128)S(1)}, s32[8,16]{1,0:T(8,128)}, u32[]{:S(2)}) copy-start(s32[8,16]{1,0:T(8,128)} %types.3) | copy-start | bytes 1540
  1.8 14.3 %collective-permute-start = (f32[512,128]{1,0:T(8,128)S(1)}, f32[512,128]{1,0:T(8,128)S(1)}, u32[]{:S(2)}, u32[]{:S(2)}) collective-permute-start(f32[512,128]{1,0:T(8,128)S(1)} %bitcast.14), channel_id=1, source_target_pairs={{0,4},{8,12},{16,20},{24,28},{4,0},{12,8},{20,16},{28,24},{1,5},{9... | collective-permute-start | bytes 786440 | tf_op jit(solution)/shard_map/ppermute | solution.py:739
  4.9 11.3 %collective-permute-start.1 = (f32[512,128]{1,0:T(8,128)S(1)}, f32[512,128]{1,0:T(8,128)S(1)}, u32[]{:S(2)}, u32[]{:S(2)}) collective-permute-start(f32[512,128]{1,0:T(8,128)S(1)} %bitcast.13), channel_id=1, source_target_pairs={{4,8},{12,16},{20,24},{8,4},{16,12},{24,20},{5,9},{13,17},{21,25},... | collective-permute-start | bytes 786440 | tf_op jit(solution)/shard_map/ppermute | solution.py:739
  7.4 16.2 %all-to-all-start = ((f32[32,10,1,128]{3,2,1,0:T(1,128)}), f32[32,10,1,128]{3,2,1,0:T(1,128)S(1)}, u32[]{:S(2)}, u32[]{:S(2)}) async-start(f32[32,10,1,128]{3,2,1,0:T(1,128)} %shard_map.77), calls=%async_computation | async-start | bytes 327680 | tf_op jit(solution)/shard_map/all_to_all | solution.py:784
  15.7 5.5 %copy-start.1 = (f32[8,128,128]{2,1,0:T(8,128)S(1)}, f32[8,128,128]{2,1,0:T(8,128)}, u32[]{:S(2)}) copy-start(f32[8,128,128]{2,1,0:T(8,128)} %library.1) | copy-start | bytes 1572868
  16.2 1.3 %copy-start.4 = (f32[512,128]{1,0:T(8,128)}, f32[512,128]{1,0:T(8,128)S(1)}, u32[]{:S(2)}) copy-start(f32[512,128]{1,0:T(8,128)S(1)} %collective-permute-done.row_first) | copy-start | bytes 786436
  16.2 1.3 %copy-start.6 = (f32[512,128]{1,0:T(8,128)}, f32[512,128]{1,0:T(8,128)S(1)}, u32[]{:S(2)}) copy-start(f32[512,128]{1,0:T(8,128)S(1)} %collective-permute-done.1.row_second) | copy-start | bytes 786436
  17.5 3.8 %copy-start.3 = (f32[2,128]{1,0:T(2,128)S(1)}, f32[2,128]{1,0:T(2,128)}, u32[]{:S(2)}) copy-start(f32[2,128]{1,0:T(2,128)} %strap.7) | copy-start | bytes 3076
  17.5 10.9 %collective-permute-start.3 = (f32[320,128]{1,0:T(8,128)}, f32[320,128]{1,0:T(8,128)S(1)}, u32[]{:S(2)}, u32[]{:S(2)}) collective-permute-start(f32[320,128]{1,0:T(8,128)} %get-tuple-element.22), channel_id=1, source_target_pairs={{1,2},{2,1},{5,6},{6,5},{9,10},{10,9},{13,14},{14,13},{17,18},{18,... | collective-permute-start | bytes 491528 | tf_op jit(solution)/shard_map/ppermute | solution.py:739
  18.3 5.3 %copy-start.9 = (s32[8,256]{1,0:T(8,128)S(1)}, s32[8,256]{1,0:T(8,128)}, u32[]{:S(2)}) copy-start(s32[8,256]{1,0:T(8,128)} %constant.42.clone.maps) | copy-start | bytes 24580
  18.3 10.1 %collective-permute-start.2 = (f32[320,128]{1,0:T(8,128)S(1)}, f32[320,128]{1,0:T(8,128)}, u32[]{:S(2)}, u32[]{:S(2)}) collective-permute-start(f32[320,128]{1,0:T(8,128)S(1)} %get-tuple-element.17.after), channel_id=1, source_target_pairs={{0,1},{2,3},{1,0},{3,2},{4,5},{6,7},{5,4},{7,6},{8,9},{10,11},{9,8... | collective-permute-start | bytes 491528 | tf_op jit(solution)/shard_map/ppermute | solution.py:739
  23.6 4.8 %copy-start.5 = (f32[512,128]{1,0:T(8,128)S(1)}, f32[512,128]{1,0:T(8,128)}, u32[]{:S(2)}) copy-start(f32[512,128]{1,0:T(8,128)} %copy-done.4) | copy-start | bytes 786436
  23.6 4.8 %copy-start.7 = (f32[512,128]{1,0:T(8,128)S(1)}, f32[512,128]{1,0:T(8,128)}, u32[]{:S(2)}) copy-start(f32[512,128]{1,0:T(8,128)} %copy-done.6) | copy-start | bytes 786436
